TPU v7x, 32 devices: a whole 2x2x4 slice. The times are simulated.
32 devices in a mesh: parts: 2 (over y), gx: 4 (over z), gy: 2 (over x), gz: 2 (over core).
Axes of the slice: x: 2, y: 2, z: 4, core: 2. Of those that a mesh axis runs over, the one named last changes fastest.
Arguments:
- forward_pops: bfloat16 [19, 256, 16, 256], P(None, ('parts', 'gx'), 'gy', 'gz'), parts along dimension 1, as said below
- adjoint_pops: bfloat16 [19, 256, 16, 256], P(None, ('parts', 'gx'), 'gy', 'gz'), parts along dimension 1, may hold values from -6 to 6
- coefficients: float32 [64, 4, 64], P(('parts', 'gx'), 'gy', 'gz'), parts along dimension 0, may hold values from -3 to 3
- node_kind: int32 [256, 16, 256], P(('parts', 'gx'), 'gy', 'gz'), parts along dimension 0, may hold values from 0 to 3, as said below
Outputs:
- prior_adjoint: bfloat16 [19, 256, 16, 256], P(None, ('parts', 'gx'), 'gy', 'gz'), parts along dimension 1
- coef_gradient: float32 [64, 4, 64], P(('parts', 'gx'), 'gy', 'gz'), parts along dimension 0
There are 2 independent parts, one for each index of `parts`. A program takes and returns all parts, laid end to end along the dimension named above; each array names one. Nothing has to cross between parts.
Inputs may be any that keep to these rules, and one draw needn't show every extreme that they name: `node_kind`: node kinds: 0 fluid, 1 solid, 2 inlet, 3 outlet. `forward_pops`: every population lies between 0.4 and 1.7 times the lattice weight of its velocity.
All inputs are finite; a program needn't handle non-finite values.
Results may differ from a plain program's by a relative error of at most 0.001.
Values may be sent and summed in bfloat16 or wider, within the bound.
No kernel may reach another device: no remote copies, remote signals or barrier semaphores. Data moves between devices by JAX's collectives and lax.ppermute only.
A program may use at most 64 MiB of HBM per device.

v0:
```python
import jax
import jax.numpy as jnp
from jax import lax
from jax.sharding import PartitionSpec as P

VELOCITY = (
    (0, 0, 0),
    (1, 0, 0),
    (-1, 0, 0),
    (0, 1, 0),
    (0, -1, 0),
    (0, 0, 1),
    (0, 0, -1),
    (1, 1, 0),
    (-1, -1, 0),
    (1, -1, 0),
    (-1, 1, 0),
    (1, 0, 1),
    (-1, 0, -1),
    (1, 0, -1),
    (-1, 0, 1),
    (0, 1, 1),
    (0, -1, -1),
    (0, 1, -1),
    (0, -1, 1),
)
OPPOSITE = (0, 2, 1, 4, 3, 6, 5, 8, 7, 10, 9, 12, 11, 14, 13, 16, 15, 18, 17)
WEIGHTS = (1.0 / 3.0,) + (1.0 / 18.0,) * 6 + (1.0 / 36.0,) * 12
relaxation = 1.6
inlet_speed = 0.05
highest = lax.Precision.HIGHEST


def padded(block, sides, width):
    for axis, dim in sides:
        count = lax.axis_size(axis)
        forward = [(i, i + 1) for i in range(count - 1)]
        backward = [(target, source) for source, target in forward]
        low = lax.ppermute(
            lax.slice_in_dim(block, block.shape[dim] - width, None, axis=dim), axis, forward
        )
        high = lax.ppermute(lax.slice_in_dim(block, 0, width, axis=dim), axis, backward)
        block = jnp.concatenate([low, block, high], axis=dim)
    return block


def equilibrium(density, flow_x, flow_y, flow_z):
    square = flow_x * flow_x + flow_y * flow_y + flow_z * flow_z
    layers = []
    for component in range(19):
        step_x, step_y, step_z = VELOCITY[component]
        projection = step_x * flow_x + step_y * flow_y + step_z * flow_z
        layers.append(
            WEIGHTS[component]
            * density
            * (1.0 + 3.0 * projection + 4.5 * projection * projection - 1.5 * square)
        )
    return jnp.stack(layers)


def moment(populations, dimension):
    total = jnp.zeros_like(populations[0])
    for component in range(19):
        factor = VELOCITY[component][dimension]
        if factor != 0:
            total = total + factor * populations[component]
    return total


def collide(populations, porosity, node_kind):
    density = jnp.sum(populations, axis=0)
    flow_x = moment(populations, 0) / density
    flow_y = moment(populations, 1) / density
    flow_z = moment(populations, 2) / density
    retained = 1.0 - porosity
    fluid_post = populations - relaxation * (
        populations - equilibrium(density, retained * flow_x, retained * flow_y, retained * flow_z)
    )
    solid_post = jnp.stack([populations[OPPOSITE[component]] for component in range(19)])
    unit_density = jnp.ones_like(density)
    inlet_post = equilibrium(
        unit_density, inlet_speed * unit_density, jnp.zeros_like(density), jnp.zeros_like(density)
    )
    outlet_post = equilibrium(unit_density, flow_x, flow_y, flow_z)
    kind_here = node_kind[None]
    return jnp.where(
        kind_here == 0,
        fluid_post,
        jnp.where(kind_here == 1, solid_post, jnp.where(kind_here == 2, inlet_post, outlet_post)),
    )


def basis_matrix(fine_count, coarse_count, fine_offset, coarse_offset):
    fine_pos = jnp.arange(fine_count, dtype=jnp.float32) + fine_offset
    coarse_pos = jnp.arange(coarse_count, dtype=jnp.float32) + coarse_offset
    distance = fine_pos[:, None] - 4.0 * coarse_pos[None, :] - 1.5
    radius = jnp.abs(distance) / 6.0
    return jnp.where(radius < 1.0, (1.0 - radius) ** 4 * (1.0 + 4.0 * radius), 0.0)


def moving(dimension):
    return [component for component in range(19) if VELOCITY[component][dimension] != 0]


def pull_along(lane_list, dimension, extended):
    length_here = lane_list[0].shape[dimension]
    result = list(lane_list)
    for position, component in enumerate(moving(dimension)):
        offset = 1 + VELOCITY[component][dimension]
        result[component] = lax.slice_in_dim(
            extended[position], offset, offset + length_here, axis=dimension
        )
    return result


def fold_rim(bordered, dimension):
    length_here = bordered.shape[dimension]
    middle = lax.slice_in_dim(bordered, 2, length_here - 2, axis=dimension)
    head_slice = lax.slice_in_dim(bordered, 0, 1, axis=dimension)
    tail_slice = lax.slice_in_dim(bordered, length_here - 1, length_here, axis=dimension)
    middle_count = length_here - 4
    head_pads = [(0, 0)] * 3
    tail_pads = [(0, 0)] * 3
    head_pads[dimension] = (0, middle_count - 1)
    tail_pads[dimension] = (middle_count - 1, 0)
    return middle + jnp.pad(head_slice, head_pads) + jnp.pad(tail_slice, tail_pads)


def per_device(forward_pops, adjoint_pops, coefficients, node_kind):
    cells_x, cells_y, cells_z = node_kind.shape
    coarse_x, coarse_y, coarse_z = coefficients.shape
    window = padded(coefficients, (("gx", 0), ("gy", 1), ("gz", 2)), 1)
    basis_x = basis_matrix(cells_x, coarse_x + 2, 0, -1)
    basis_y = basis_matrix(cells_y, coarse_y + 2, 0, -1)
    basis_z = basis_matrix(cells_z, coarse_z + 2, 0, -1)
    partway = jnp.einsum("ijk,zk->ijz", window, basis_z, precision=highest)
    partway = jnp.einsum("ijz,yj->iyz", partway, basis_y, precision=highest)
    level_set = jnp.einsum("iyz,xi->xyz", partway, basis_x, precision=highest)
    bent = jnp.tanh(4.0 * level_set)
    porosity = 0.45 * (1.0 - bent)
    slope_phi = -1.8 * (1.0 - bent * bent)
    lane_list = [adjoint_pops[component] for component in range(19)]
    extended = padded(jnp.stack([lane_list[component] for component in moving(0)]), (("gx", 1),), 1)
    lane_list = pull_along(lane_list, 0, extended)
    extended = padded(jnp.stack([lane_list[component] for component in moving(1)]), (("gy", 2),), 1)
    lane_list = pull_along(lane_list, 1, extended)
    extended = padded(jnp.stack([lane_list[component] for component in moving(2)]), (("gz", 3),), 1)
    lane_list = pull_along(lane_list, 2, extended)
    pulled = jnp.stack(lane_list).astype(jnp.float32)
    forward = forward_pops.astype(jnp.float32)

    def local_collide(populations, porosity_here):
        return collide(populations, porosity_here, node_kind)

    unused, pullback = jax.vjp(local_collide, forward, porosity)
    prior, porosity_bar = pullback(pulled)
    prior_adjoint = prior.astype(jnp.bfloat16)
    sensitivity = porosity_bar * slope_phi
    partial_value = jnp.einsum("xyz,xi->iyz", sensitivity, basis_x, precision=highest)
    partial_value = jnp.einsum("iyz,yj->ijz", partial_value, basis_y, precision=highest)
    partial_value = jnp.einsum("ijz,zk->ijk", partial_value, basis_z, precision=highest)
    bordered = padded(partial_value, (("gx", 0), ("gy", 1), ("gz", 2)), 1)
    gradient = fold_rim(fold_rim(fold_rim(bordered, 0), 1), 2)
    return (prior_adjoint, gradient)


def solution(mesh):
    in_specs = (
        P(None, ("parts", "gx"), "gy", "gz"),
        P(None, ("parts", "gx"), "gy", "gz"),
        P(("parts", "gx"), "gy", "gz"),
        P(("parts", "gx"), "gy", "gz"),
    )
    out_specs = (P(None, ("parts", "gx"), "gy", "gz"), P(("parts", "gx"), "gy", "gz"))
    return jax.shard_map(
        per_device, mesh=mesh, in_specs=in_specs, out_specs=out_specs, check_vma=False
    )
```

profile of v0, /device:TPU:0, one launch (start us, length us, event | category | flops | bytes accessed | tf_op | source)
XLA Modules:
  0.0 95.0 jit_solution(15775273977151735013)
XLA Ops:
  2.7 5.6 %collective-permute-start.6 = (f32[1,2,32]{2,1,0:T(2,128)S(1)}, f32[1,2,32]{2,1,0:T(2,128)S(1)}, u32[]{:S(2)}, u32[]{:S(2)}) collective-permute-start(f32[1,2,32]{2,1,0:T(2,128)S(1)} %get-tuple-element.148), channel_id=1, source_target_pairs={{0,4},{4,8},{8,12},{1,5},{5,9},{9,13},{2,6},{6,10},{10,14},{3,7},{... | collective-permute-start | bytes 776 | tf_op jit(solution)/shard_map/ppermute | solution.py:39
  10.7 3.9 %collective-permute-start.1 = (bf16[10,1,8,128]{3,1,2,0:T(2,128)(2,1)S(1)}, bf16[10,1,8,128]{3,1,2,0:T(2,128)(2,1)S(1)}, u32[]{:S(2)}, u32[]{:S(2)}) collective-permute-start(bf16[10,1,8,128]{3,1,2,0:T(2,128)(2,1)S(1)} %get-tuple-element.118), channel_id=1, source_target_pairs={{0,4},{4,8},{8,12},{1,5},{5,9},{9,13},{2,6},{6,10},{10,14},{3,7},{... | collective-permute-start | bytes 61448 | tf_op jit(solution)/shard_map/ppermute | solution.py:39
  14.6 1.3 %collective-permute-start = (bf16[10,1,8,128]{3,1,2,0:T(2,128)(2,1)S(1)}, bf16[10,1,8,128]{3,1,2,0:T(2,128)(2,1)S(1)}, u32[]{:S(2)}, u32[]{:S(2)}) collective-permute-start(bf16[10,1,8,128]{3,1,2,0:T(2,128)(2,1)S(1)} %get-tuple-element.119), channel_id=1, source_target_pairs={{4,0},{8,4},{12,8},{5,1},{9,5},{13,9},{6,2},{10,6},{14,10},{7,3},{... | collective-permute-start | bytes 61448 | tf_op jit(solution)/shard_map/ppermute | solution.py:42
  17.7 3.4 %collective-permute-start.8 = (f32[10,1,32]{2,1,0:T(1,128)S(1)}, f32[10,1,32]{2,1,0:T(1,128)S(1)}, u32[]{:S(2)}, u32[]{:S(2)}) collective-permute-start(f32[10,1,32]{2,1,0:T(1,128)S(1)} %get-tuple-element.145), channel_id=1, source_target_pairs={{0,2},{1,3},{4,6},{5,7},{8,10},{9,11},{12,14},{13,15},{16,18},{17,... | collective-permute-start | bytes 3848 | tf_op jit(solution)/shard_map/ppermute | solution.py:39
  22.5 4.1 %collective-permute-done.9 = f32[10,1,32]{2,1,0:T(1,128)S(1)} collective-permute-done((f32[10,1,32]{2,1,0:T(1,128)S(1)}, f32[10,1,32]{2,1,0:T(1,128)S(1)}, u32[]{:S(2)}, u32[]{:S(2)}) %collective-permute-start.9) | collective-permute-done | bytes 1312 | tf_op jit(solution)/shard_map/ppermute | solution.py:42
  29.4 1.7 %collective-permute-done.11 = f32[10,4,1]{2,1,0:T(4,128)S(1)} collective-permute-done((f32[10,4,1]{2,1,0:T(4,128)S(1)}, f32[10,4,1]{2,1,0:T(4,128)S(1)}, u32[]{:S(2)}, u32[]{:S(2)}) %collective-permute-start.11) | collective-permute-done | bytes 192 | tf_op jit(solution)/shard_map/ppermute | solution.py:42
  33.2 1.7 %collective-permute-start.2 = (bf16[10,32,1,128]{3,1,2,0:T(8,128)(2,1)S(1)}, bf16[10,32,1,128]{3,1,2,0:T(8,128)(2,1)S(1)}, u32[]{:S(2)}, u32[]{:S(2)}) collective-permute-start(bf16[10,32,1,128]{3,1,2,0:T(8,128)(2,1)S(1)} %get-tuple-element.116), channel_id=1, source_target_pairs={{0,2},{1,3},{4,6},{5,7},{8,10},{9,11},{12,14},{13,15},{16,18},{17,... | collective-permute-start | bytes 245768 | tf_op jit(solution)/shard_map/ppermute | solution.py:39
  36.9 4.2 %collective-permute-done.3 = bf16[10,32,1,128]{3,1,2,0:T(8,128)(2,1)S(1)} collective-permute-done((bf16[10,32,1,128]{3,1,2,0:T(8,128)(2,1)S(1)}, bf16[10,32,1,128]{3,1,2,0:T(8,128)(2,1)S(1)}, u32[]{:S(2)}, u32[]{:S(2)}) %collective-permute-start.3) | collective-permute-done | bytes 81952 | tf_op jit(solution)/shard_map/ppermute | solution.py:42
  42.1 1.3 %fusion.389 = (bf16[10,32,8,1]{3,1,2,0:T(8,128)(2,1)}, bf16[10,32,8,1]{3,1,2,0:T(8,128)(2,1)}) fusion(bf16[10,32,8,128]{3,1,2,0:T(8,128)(2,1)S(1)} %constant_dynamic-update-slice_fusion.4), kind=kLoop, calls=%fused_computation.692 | loop fusion | bytes 20480 | tf_op jit(solution)/shard_map/slice | solution.py:40
  43.4 2.2 %copy.26 = bf16[10,32,8,1]{1,2,3,0:T(8,128)(2,1)} copy(bf16[10,32,8,1]{3,1,2,0:T(8,128)(2,1)} %get-tuple-element.114) | data formatting | bytes 10240 | tf_op jit(solution)/shard_map/slice | solution.py:40
  45.7 2.2 %copy.27 = bf16[10,32,8,1]{1,2,3,0:T(8,128)(2,1)} copy(bf16[10,32,8,1]{3,1,2,0:T(8,128)(2,1)} %get-tuple-element.115) | data formatting | bytes 10240 | tf_op jit(solution)/shard_map/slice | solution.py:42
  49.2 4.2 %collective-permute-start.4 = (bf16[10,32,8,1]{1,2,3,0:T(8,128)(2,1)}, bf16[10,32,8,1]{1,2,3,0:T(8,128)(2,1)}, u32[]{:S(2)}, u32[]{:S(2)}) collective-permute-start(bf16[10,32,8,1]{1,2,3,0:T(8,128)(2,1)} %copy.26), channel_id=1, source_target_pairs={{0,1},{2,3},{4,5},{6,7},{8,9},{10,11},{12,13},{14,15},{16,17},{18,... | collective-permute-start | bytes 15368 | tf_op jit(solution)/shard_map/ppermute | solution.py:39
  53.4 1.5 %constant_dynamic-update-slice_fusion.27 = bf16[19,32,8,128]{3,1,2,0:T(8,128)(2,1)} fusion(bf16[19,32,8,128]{3,1,2,0:T(8,128)(2,1)} %get-tuple-element.106, bf16[32,10,128]{2,0,1:T(8,128)(2,1)} %get-tuple-element.103), kind=kLoop, calls=%fused_computation.548 | loop fusion | bytes 131072
  54.9 1.5 %constant_dynamic-update-slice_fusion.26 = bf16[19,32,8,128]{3,1,2,0:T(8,128)(2,1)} fusion(bf16[19,32,8,128]{3,1,2,0:T(8,128)(2,1)} %constant_dynamic-update-slice_fusion.27, bf16[32,10,128]{2,0,1:T(8,128)(2,1)} %get-tuple-element.102), kind=kLoop, calls=%fused_computation.547 | loop fusion | bytes 131072
  56.3 2.1 %copy.28 = bf16[10,32,8,1]{3,1,2,0:T(8,128)(2,1)} copy(bf16[10,32,8,1]{1,2,3,0:T(8,128)(2,1)} %collective-permute-done.4) | data formatting | bytes 10240 | tf_op jit(solution)/shard_map/ppermute | solution.py:39
  58.5 2.1 %copy.29 = bf16[10,32,8,1]{3,1,2,0:T(8,128)(2,1)} copy(bf16[10,32,8,1]{1,2,3,0:T(8,128)(2,1)} %collective-permute-done.5) | data formatting | bytes 10240 | tf_op jit(solution)/shard_map/ppermute | solution.py:42
  60.6 2.1 %pad_maximum_fusion = bf16[10,32,8,130]{3,1,2,0:T(8,128)(2,1)S(1)} fusion(bf16[10,32,8,1]{3,1,2,0:T(8,128)(2,1)} %copy.29, bf16[10,32,8,128]{3,1,2,0:T(8,128)(2,1)S(1)} %constant_dynamic-update-slice_fusion.4, bf16[10,32,8,1]{3,1,2,0:T(8,128)(2,1)} %copy.28), kind=kLoop, calls=%fused_computation.34 | loop fusion | flops 1996800 | bytes 1331200 | tf_op jit(solution)/shard_map/concatenate | solution.py:43
  67.5 2.8 %negate_add_fusion = (f32[32,8,128]{2,0,1:T(8,128)S(1)}, f32[32,8,128]{2,0,1:T(8,128)S(1)}, f32[32,8,128]{2,0,1:T(8,128)S(1)}, f32[32,8,128]{2,0,1:T(8,128)S(1)}...) fusion(f32[32,8,128]{2,0,1:T(8,128)S(1)} %get-tuple-element.15, ...), kind=kLoop, calls=%fused_computation.452 | loop fusion | flops 17006592 | bytes 12320768 | tf_op jit(solution)/shard_map/transpose(jvp())/add_any | solution.py:72
  71.1 4.5 %collective-permute-start.12 = (f32[1,4,34]{2,0,1:T(1,128)S(1)}, f32[1,4,34]{2,0,1:T(1,128)S(1)}, u32[]{:S(2)}, u32[]{:S(2)}) collective-permute-start(f32[1,4,34]{2,0,1:T(1,128)S(1)} %get-tuple-element.141), channel_id=1, source_target_pairs={{0,4},{4,8},{8,12},{1,5},{5,9},{9,13},{2,6},{6,10},{10,14},{3,7},{... | collective-permute-start | bytes 1640 | tf_op jit(solution)/shard_map/ppermute | solution.py:39
  75.7 1.3 %collective-permute-start.13 = (f32[1,4,34]{2,0,1:T(1,128)S(1)}, f32[1,4,34]{2,0,1:T(1,128)S(1)}, u32[]{:S(2)}, u32[]{:S(2)}) collective-permute-start(f32[1,4,34]{2,0,1:T(1,128)S(1)} %get-tuple-element.142), channel_id=1, source_target_pairs={{4,0},{8,4},{12,8},{5,1},{9,5},{13,9},{6,2},{10,6},{14,10},{7,3},{... | collective-permute-start | bytes 1640 | tf_op jit(solution)/shard_map/ppermute | solution.py:42
  77.3 3.9 %collective-permute-done.13 = f32[1,4,34]{2,0,1:T(1,128)S(1)} collective-permute-done((f32[1,4,34]{2,0,1:T(1,128)S(1)}, f32[1,4,34]{2,0,1:T(1,128)S(1)}, u32[]{:S(2)}, u32[]{:S(2)}) %collective-permute-start.13) | collective-permute-done | bytes 576 | tf_op jit(solution)/shard_map/ppermute | solution.py:42
  81.2 1.5 %collective-permute-start.14 = (f32[12,1,34]{2,0,1:T(8,128)S(1)}, f32[12,1,34]{2,0,1:T(8,128)S(1)}, u32[]{:S(2)}, u32[]{:S(2)}) collective-permute-start(f32[12,1,34]{2,0,1:T(8,128)S(1)} %get-tuple-element.139), channel_id=1, source_target_pairs={{0,2},{1,3},{4,6},{5,7},{8,10},{9,11},{12,14},{13,15},{16,18},{17,... | collective-permute-start | bytes 4904 | tf_op jit(solution)/shard_map/ppermute | solution.py:39
  84.1 4.2 %collective-permute-done.15 = f32[12,1,34]{2,0,1:T(8,128)S(1)} collective-permute-done((f32[12,1,34]{2,0,1:T(8,128)S(1)}, f32[12,1,34]{2,0,1:T(8,128)S(1)}, u32[]{:S(2)}, u32[]{:S(2)}) %collective-permute-start.15) | collective-permute-done | bytes 1664 | tf_op jit(solution)/shard_map/ppermute | solution.py:42
  92.3 1.6 %copy.32 = bf16[19,32,8,128]{3,2,1,0:T(8,128)(2,1)} copy(bf16[19,32,8,128]{3,1,2,0:T(8,128)(2,1)S(1)} %add_convert_fusion) | data formatting | bytes 2490368
  (124 shorter events, 28.6 us)
Async XLA Ops:
  0.6 15.3 %copy-start.1 = (bf16[19,32,8,128]{3,2,1,0:T(8,128)(2,1)S(1)}, bf16[19,32,8,128]{3,2,1,0:T(8,128)(2,1)}, u32[]{:S(2)}) copy-start(bf16[19,32,8,128]{3,2,1,0:T(8,128)(2,1)} %param.4) | copy-start | bytes 3735556
  1.4 16.2 %collective-permute-start.7 = (f32[1,2,32]{2,1,0:T(2,128)S(1)}, f32[1,2,32]{2,1,0:T(2,128)S(1)}, u32[]{:S(2)}, u32[]{:S(2)}) collective-permute-start(f32[1,2,32]{2,1,0:T(2,128)S(1)} %get-tuple-element.147), channel_id=1, source_target_pairs={{4,0},{8,4},{12,8},{5,1},{9,5},{13,9},{6,2},{10,6},{14,10},{7,3},{... | collective-permute-start | bytes 776 | tf_op jit(solution)/shard_map/ppermute | solution.py:42
  2.7 14.9 %collective-permute-start.6 = (f32[1,2,32]{2,1,0:T(2,128)S(1)}, f32[1,2,32]{2,1,0:T(2,128)S(1)}, u32[]{:S(2)}, u32[]{:S(2)}) collective-permute-start(f32[1,2,32]{2,1,0:T(2,128)S(1)} %get-tuple-element.148), channel_id=1, source_target_pairs={{0,4},{4,8},{8,12},{1,5},{5,9},{9,13},{2,6},{6,10},{10,14},{3,7},{... | collective-permute-start | bytes 776 | tf_op jit(solution)/shard_map/ppermute | solution.py:39
  10.7 20.9 %collective-permute-start.1 = (bf16[10,1,8,128]{3,1,2,0:T(2,128)(2,1)S(1)}, bf16[10,1,8,128]{3,1,2,0:T(2,128)(2,1)S(1)}, u32[]{:S(2)}, u32[]{:S(2)}) collective-permute-start(bf16[10,1,8,128]{3,1,2,0:T(2,128)(2,1)S(1)} %get-tuple-element.118), channel_id=1, source_target_pairs={{0,4},{4,8},{8,12},{1,5},{5,9},{9,13},{2,6},{6,10},{10,14},{3,7},{... | collective-permute-start | bytes 61448 | tf_op jit(solution)/shard_map/ppermute | solution.py:39
  14.6 16.8 %collective-permute-start = (bf16[10,1,8,128]{3,1,2,0:T(2,128)(2,1)S(1)}, bf16[10,1,8,128]{3,1,2,0:T(2,128)(2,1)S(1)}, u32[]{:S(2)}, u32[]{:S(2)}) collective-permute-start(bf16[10,1,8,128]{3,1,2,0:T(2,128)(2,1)S(1)} %get-tuple-element.119), channel_id=1, source_target_pairs={{4,0},{8,4},{12,8},{5,1},{9,5},{13,9},{6,2},{10,6},{14,10},{7,3},{... | collective-permute-start | bytes 61448 | tf_op jit(solution)/shard_map/ppermute | solution.py:42
  17.6 15.5 %slice-start.1 = ((bf16[19,32,8,128]{3,2,1,0:T(8,128)(2,1)}), bf16[4,32,8,128]{3,2,1,0:T(8,128)(2,1)S(1)}, s32[]{:S(2)}) async-start(bf16[19,32,8,128]{3,2,1,0:T(8,128)(2,1)} %param.5), calls=%async_computation.1 | async-start | bytes 524288 | tf_op jit(solution)/shard_map/slice | solution.py:142
  17.7 4.8 %collective-permute-start.8 = (f32[10,1,32]{2,1,0:T(1,128)S(1)}, f32[10,1,32]{2,1,0:T(1,128)S(1)}, u32[]{:S(2)}, u32[]{:S(2)}) collective-permute-start(f32[10,1,32]{2,1,0:T(1,128)S(1)} %get-tuple-element.145), channel_id=1, source_target_pairs={{0,2},{1,3},{4,6},{5,7},{8,10},{9,11},{12,14},{13,15},{16,18},{17,... | collective-permute-start | bytes 3848 | tf_op jit(solution)/shard_map/ppermute | solution.py:39
  21.1 5.5 %collective-permute-start.9 = (f32[10,1,32]{2,1,0:T(1,128)S(1)}, f32[10,1,32]{2,1,0:T(1,128)S(1)}, u32[]{:S(2)}, u32[]{:S(2)}) collective-permute-start(f32[10,1,32]{2,1,0:T(1,128)S(1)} %get-tuple-element.146), channel_id=1, source_target_pairs={{2,0},{3,1},{6,4},{7,5},{10,8},{11,9},{14,12},{15,13},{18,16},{19,... | collective-permute-start | bytes 3848 | tf_op jit(solution)/shard_map/ppermute | solution.py:42
  26.7 2.6 %collective-permute-start.10 = (f32[10,4,1]{2,1,0:T(4,128)S(1)}, f32[10,4,1]{2,1,0:T(4,128)S(1)}, u32[]{:S(2)}, u32[]{:S(2)}) collective-permute-start(f32[10,4,1]{2,1,0:T(4,128)S(1)} %get-tuple-element.143), channel_id=1, source_target_pairs={{0,1},{2,3},{4,5},{6,7},{8,9},{10,11},{12,13},{14,15},{16,17},{18,... | collective-permute-start | bytes 488 | tf_op jit(solution)/shard_map/ppermute | solution.py:39
  28.0 3.1 %collective-permute-start.11 = (f32[10,4,1]{2,1,0:T(4,128)S(1)}, f32[10,4,1]{2,1,0:T(4,128)S(1)}, u32[]{:S(2)}, u32[]{:S(2)}) collective-permute-start(f32[10,4,1]{2,1,0:T(4,128)S(1)} %get-tuple-element.144), channel_id=1, source_target_pairs={{1,0},{3,2},{5,4},{7,6},{9,8},{11,10},{13,12},{15,14},{17,16},{19,... | collective-permute-start | bytes 488 | tf_op jit(solution)/shard_map/ppermute | solution.py:42
  33.2 3.8 %collective-permute-start.2 = (bf16[10,32,1,128]{3,1,2,0:T(8,128)(2,1)S(1)}, bf16[10,32,1,128]{3,1,2,0:T(8,128)(2,1)S(1)}, u32[]{:S(2)}, u32[]{:S(2)}) collective-permute-start(bf16[10,32,1,128]{3,1,2,0:T(8,128)(2,1)S(1)} %get-tuple-element.116), channel_id=1, source_target_pairs={{0,2},{1,3},{4,6},{5,7},{8,10},{9,11},{12,14},{13,15},{16,18},{17,... | collective-permute-start | bytes 245768 | tf_op jit(solution)/shard_map/ppermute | solution.py:39
  34.8 6.3 %collective-permute-start.3 = (bf16[10,32,1,128]{3,1,2,0:T(8,128)(2,1)S(1)}, bf16[10,32,1,128]{3,1,2,0:T(8,128)(2,1)S(1)}, u32[]{:S(2)}, u32[]{:S(2)}) collective-permute-start(bf16[10,32,1,128]{3,1,2,0:T(8,128)(2,1)S(1)} %get-tuple-element.117), channel_id=1, source_target_pairs={{2,0},{3,1},{6,4},{7,5},{10,8},{11,9},{14,12},{15,13},{18,16},{19,... | collective-permute-start | bytes 245768 | tf_op jit(solution)/shard_map/ppermute | solution.py:42
  47.9 10.6 %collective-permute-start.5 = (bf16[10,32,8,1]{1,2,3,0:T(8,128)(2,1)}, bf16[10,32,8,1]{1,2,3,0:T(8,128)(2,1)}, u32[]{:S(2)}, u32[]{:S(2)}) collective-permute-start(bf16[10,32,8,1]{1,2,3,0:T(8,128)(2,1)} %copy.27), channel_id=1, source_target_pairs={{1,0},{3,2},{5,4},{7,6},{9,8},{11,10},{13,12},{15,14},{17,16},{19,... | collective-permute-start | bytes 15368 | tf_op jit(solution)/shard_map/ppermute | solution.py:42
  49.2 7.2 %collective-permute-start.4 = (bf16[10,32,8,1]{1,2,3,0:T(8,128)(2,1)}, bf16[10,32,8,1]{1,2,3,0:T(8,128)(2,1)}, u32[]{:S(2)}, u32[]{:S(2)}) collective-permute-start(bf16[10,32,8,1]{1,2,3,0:T(8,128)(2,1)} %copy.26), channel_id=1, source_target_pairs={{0,1},{2,3},{4,5},{6,7},{8,9},{10,11},{12,13},{14,15},{16,17},{18,... | collective-permute-start | bytes 15368 | tf_op jit(solution)/shard_map/ppermute | solution.py:39
  60.6 2.3 %copy-start = (bf16[19,32,8,128]{3,1,2,0:T(8,128)(2,1)S(1)}, bf16[19,32,8,128]{3,1,2,0:T(8,128)(2,1)}, u32[]{:S(2)}) copy-start(bf16[19,32,8,128]{3,1,2,0:T(8,128)(2,1)} %constant_dynamic-update-slice_fusion.26) | copy-start | bytes 3735556
  60.6 2.4 %copy-start.3 = (bf16[32,10,128]{2,0,1:T(8,128)(2,1)S(1)}, bf16[32,10,128]{2,0,1:T(8,128)(2,1)}, u32[]{:S(2)}) copy-start(bf16[32,10,128]{2,0,1:T(8,128)(2,1)} %get-tuple-element.97) | copy-start | bytes 245764
  60.6 2.4 %copy-start.2 = (bf16[32,10,128]{2,0,1:T(8,128)(2,1)S(1)}, bf16[32,10,128]{2,0,1:T(8,128)(2,1)}, u32[]{:S(2)}) copy-start(bf16[32,10,128]{2,0,1:T(8,128)(2,1)} %get-tuple-element.96) | copy-start | bytes 245764
  71.1 6.2 %collective-permute-start.12 = (f32[1,4,34]{2,0,1:T(1,128)S(1)}, f32[1,4,34]{2,0,1:T(1,128)S(1)}, u32[]{:S(2)}, u32[]{:S(2)}) collective-permute-start(f32[1,4,34]{2,0,1:T(1,128)S(1)} %get-tuple-element.141), channel_id=1, source_target_pairs={{0,4},{4,8},{8,12},{1,5},{5,9},{9,13},{2,6},{6,10},{10,14},{3,7},{... | collective-permute-start | bytes 1640 | tf_op jit(solution)/shard_map/ppermute | solution.py:39
  75.7 5.5 %collective-permute-start.13 = (f32[1,4,34]{2,0,1:T(1,128)S(1)}, f32[1,4,34]{2,0,1:T(1,128)S(1)}, u32[]{:S(2)}, u32[]{:S(2)}) collective-permute-start(f32[1,4,34]{2,0,1:T(1,128)S(1)} %get-tuple-element.142), channel_id=1, source_target_pairs={{4,0},{8,4},{12,8},{5,1},{9,5},{13,9},{6,2},{10,6},{14,10},{7,3},{... | collective-permute-start | bytes 1640 | tf_op jit(solution)/shard_map/ppermute | solution.py:42
  77.0 14.0 %copy-start.10 = (pred[19]{0:T(512)(128)(4,1)S(1)}, pred[19]{0:T(512)(128)(4,1)}, u32[]{:S(2)}) copy-start(pred[19]{0:T(512)(128)(4,1)} %constant.77.clone.1) | copy-start | bytes 61
  81.2 2.9 %collective-permute-start.14 = (f32[12,1,34]{2,0,1:T(8,128)S(1)}, f32[12,1,34]{2,0,1:T(8,128)S(1)}, u32[]{:S(2)}, u32[]{:S(2)}) collective-permute-start(f32[12,1,34]{2,0,1:T(8,128)S(1)} %get-tuple-element.139), channel_id=1, source_target_pairs={{0,2},{1,3},{4,6},{5,7},{8,10},{9,11},{12,14},{13,15},{16,18},{17,... | collective-permute-start | bytes 4904 | tf_op jit(solution)/shard_map/ppermute | solution.py:39
  82.7 5.5 %collective-permute-start.15 = (f32[12,1,34]{2,0,1:T(8,128)S(1)}, f32[12,1,34]{2,0,1:T(8,128)S(1)}, u32[]{:S(2)}, u32[]{:S(2)}) collective-permute-start(f32[12,1,34]{2,0,1:T(8,128)S(1)} %get-tuple-element.140), channel_id=1, source_target_pairs={{2,0},{3,1},{6,4},{7,5},{10,8},{11,9},{14,12},{15,13},{18,16},{19,... | collective-permute-start | bytes 4904 | tf_op jit(solution)/shard_map/ppermute | solution.py:42
  88.4 5.5 %collective-permute-start.16 = (f32[12,6,1]{2,0,1:T(8,128)S(1)}, f32[12,6,1]{2,0,1:T(8,128)S(1)}, u32[]{:S(2)}, u32[]{:S(2)}) collective-permute-start(f32[12,6,1]{2,0,1:T(8,128)S(1)} %get-tuple-element.137), channel_id=1, source_target_pairs={{0,1},{2,3},{4,5},{6,7},{8,9},{10,11},{12,13},{14,15},{16,17},{18,... | collective-permute-start | bytes 872 | tf_op jit(solution)/shard_map/ppermute | solution.py:39
  89.7 4.2 %collective-permute-start.17 = (f32[12,6,1]{2,0,1:T(8,128)S(1)}, f32[12,6,1]{2,0,1:T(8,128)S(1)}, u32[]{:S(2)}, u32[]{:S(2)}) collective-permute-start(f32[12,6,1]{2,0,1:T(8,128)S(1)} %get-tuple-element.138), channel_id=1, source_target_pairs={{1,0},{3,2},{5,4},{7,6},{9,8},{11,10},{13,12},{15,14},{17,16},{19,... | collective-permute-start | bytes 872 | tf_op jit(solution)/shard_map/ppermute | solution.py:42
  (7 other events, 9.8 us)
where the time goes:
time: 96.6 us; the launch traced here: 95 us
  starting transfers between devices  39 us (40%)
  local copies, waits for them, and re-layouts  22.3 us (23%)
  waiting for transfers between devices  18.2 us (19%)
  other arithmetic  11.9 us (12%)
  matrix products  2.35 us (2%)
  between operations  1.35 us (1%)
    ppermute x9, starting transfers between devices, padded(): lax.ppermute(lax.slice_in_dim(block, block.shape[dim] - width, None, axis...  27.4 us
    ppermute x9, waiting for transfers between devices, padded(): lax.ppermute(lax.slice_in_dim(block, 0, width, axis=dim), axis, backward)  18.1 us
    ppermute x9, starting transfers between devices, padded(): lax.ppermute(lax.slice_in_dim(block, 0, width, axis=dim), axis, backward)  11.6 us
    unnamed x47, local copies, waits for them, and re-layouts  7.38 us
    slice x8, local copies, waits for them, and re-layouts, padded(): lax.slice_in_dim(block, block.shape[dim] - width, None, axis=dim)  3.82 us
    slice x2, local copies, waits for them, and re-layouts, padded(): lax.slice_in_dim(block, 0, width, axis=dim)  3.02 us
    add_any x1, other arithmetic, collide(): flow_x = moment(populations, 0) / density  2.81 us
    concatenate x6, other arithmetic, padded(): block = jnp.concatenate([low, block, high], axis=dim)  2.48 us
  transfers between devices with their start and end apart: 18, of which 5 were waited for; matrix products, arithmetic and copies ran while one was open for 14% of the time, Pallas kernels for 0%

commit v1 on v0

v1 whole, which is shorter than its diff:
```python
import functools

import jax
import jax.numpy as jnp
import numpy as np
from jax import lax
from jax.experimental import pallas as pl
from jax.experimental.pallas import tpu as pltpu
from jax.sharding import PartitionSpec as P

VELOCITY = (
    (0, 0, 0),
    (1, 0, 0),
    (-1, 0, 0),
    (0, 1, 0),
    (0, -1, 0),
    (0, 0, 1),
    (0, 0, -1),
    (1, 1, 0),
    (-1, -1, 0),
    (1, -1, 0),
    (-1, 1, 0),
    (1, 0, 1),
    (-1, 0, -1),
    (1, 0, -1),
    (-1, 0, 1),
    (0, 1, 1),
    (0, -1, -1),
    (0, 1, -1),
    (0, -1, 1),
)
OPPOSITE = (0, 2, 1, 4, 3, 6, 5, 8, 7, 10, 9, 12, 11, 14, 13, 16, 15, 18, 17)
highest = lax.Precision.HIGHEST
f32 = jnp.float32
bf16 = jnp.bfloat16


def going(dimension, sign):
    return [q for q in range(19) if VELOCITY[q][dimension] == sign]


XP, XM = going(0, 1), going(0, -1)
YP, YM = going(1, 1), going(1, -1)
ZP, ZM = going(2, 1), going(2, -1)

FACE, ALPHA, BETA, FIELD, COARSE, BUNDLE = 0, 5, 9, 13, 17, 19


def spline(distance):
    radius = np.abs(distance) / 6.0
    return np.where(radius < 1.0, (1.0 - radius) ** 4 * (1.0 + 4.0 * radius), 0.0)


def kernel_call(body, out_shape, scratch_shapes=(), cost=(0, 0)):
    return pl.pallas_call(
        body,
        out_shape=out_shape,
        scratch_shapes=list(scratch_shapes),
        compiler_params=pltpu.CompilerParams(vmem_limit_bytes=40 * 1024 * 1024),
        cost_estimate=pl.CostEstimate(flops=cost[0], bytes_accessed=cost[1], transcendentals=0),
    )


def iota(dimension):
    return lax.broadcasted_iota(jnp.int32, (8, 128), dimension)


def pulled_z(q, tile, x, columns):
    step = VELOCITY[q][2]
    if step == 0:
        return tile
    slot = (ZP if step > 0 else ZM).index(q) * 32
    group, lane = slot // 128, slot % 128
    lanes = iota(1)
    edge = columns[0 if step > 0 else 1, group]
    if step > 0:
        edge = pltpu.roll(edge, 127 - lane - x, 1)
        return jnp.where(lanes == 127, edge, pltpu.roll(tile, 127, 1))
    edge = pltpu.roll(edge, (128 - lane - x) & 127, 1)
    return jnp.where(lanes == 0, edge, pltpu.roll(tile, 1, 1))


def pulled_y(q, tile, x, rows):
    step = VELOCITY[q][1]
    if step == 0:
        return tile
    slot = (YP if step > 0 else YM).index(q) * 32
    row = rows[0 if step > 0 else 1, pl.ds(slot + x, 1), :]
    edge = jnp.broadcast_to(row, (8, 128))
    sublanes = iota(0)
    if step > 0:
        return jnp.where(sublanes == 7, edge, pltpu.roll(tile, 7, 0))
    return jnp.where(sublanes == 0, edge, pltpu.roll(tile, 1, 0))


def load_columns(core, received, columns):
    for group in range(2):
        tile = received[group]
        columns[0, group] = jnp.where(core == 0, tile, 0.0)
        columns[1, group] = jnp.where(core == 1, tile, 0.0)


def pair_moments(populations):
    sums, diffs = {}, {}
    for q in range(1, 19, 2):
        a, b = populations.get(q), populations.get(q + 1)
        if a is None and b is None:
            continue
        if b is None:
            sums[q], diffs[q] = a, a
        elif a is None:
            sums[q], diffs[q] = b, -b
        else:
            sums[q], diffs[q] = a + b, a - b

    def total(terms):
        value = None
        for sign, table, q in terms:
            if q not in table:
                continue
            item = table[q]
            if value is None:
                value = item if sign > 0 else -item
            else:
                value = value + item if sign > 0 else value - item
        return value

    def plus(a, b):
        return b if a is None else (a if b is None else a + b)

    def twice(a):
        return None if a is None else a + a

    xx = total([(1, sums, 7), (1, sums, 9), (1, sums, 11), (1, sums, 13)])
    edge_yz = total([(1, sums, 15), (1, sums, 17)])
    edge_xy = total([(1, sums, 7), (1, sums, 9)])
    edge_xz = total([(1, sums, 11), (1, sums, 13)])
    sx, sy, sz = (twice(sums.get(q)) for q in (1, 3, 5))
    zeroth = plus(plus(xx, edge_yz), plus(plus(sx, sy), sz))
    if 0 in populations:
        zeroth = zeroth + 12.0 * populations[0]
    mx = plus(twice(diffs.get(1)), total([(1, diffs, 7), (1, diffs, 9), (1, diffs, 11), (1, diffs, 13)]))
    my = plus(twice(diffs.get(3)), total([(1, diffs, 7), (-1, diffs, 9), (1, diffs, 15), (1, diffs, 17)]))
    mz = plus(twice(diffs.get(5)), total([(1, diffs, 11), (-1, diffs, 13), (1, diffs, 15), (-1, diffs, 17)]))
    mxx = plus(sx, xx)
    myy = plus(sy, plus(edge_xy, edge_yz))
    mzz = plus(sz, plus(edge_xz, edge_yz))
    mxy = total([(1, sums, 7), (-1, sums, 9)])
    mxz = total([(1, sums, 11), (-1, sums, 13)])
    myz = total([(1, sums, 15), (-1, sums, 17)])
    return zeroth, (mx, my, mz), (mxx, myy, mzz, mxy, mxz, myz)


def flow_moments(populations):
    sums = {q: populations[q] + populations[q + 1] for q in range(1, 19, 2)}
    diffs = {q: populations[q] - populations[q + 1] for q in range(1, 19, 2)}
    rho = populations[0]
    for q in range(1, 19, 2):
        rho = rho + sums[q]
    jx = (diffs[1] + diffs[7]) + (diffs[9] + diffs[11]) + diffs[13]
    jy = (diffs[3] + diffs[7]) + (diffs[15] - diffs[9]) + diffs[17]
    jz = (diffs[5] + diffs[11]) + (diffs[15] - diffs[13]) - diffs[17]
    return rho, (jx, jy, jz)


def dot3(a, b):
    return a[0] * b[0] + a[1] * b[1] + a[2] * b[2]


def second_times(second, v):
    mxx, myy, mzz, mxy, mxz, myz = second

    def row(terms):
        value = None
        for coefficient, component in terms:
            if coefficient is None:
                continue
            product = coefficient * component
            value = product if value is None else value + product
        return value

    return (
        row([(mxx, v[0]), (mxy, v[1]), (mxz, v[2])]),
        row([(mxy, v[0]), (myy, v[1]), (myz, v[2])]),
        row([(mxz, v[0]), (myz, v[1]), (mzz, v[2])]),
    )


def alpha_beta(moments, flow, flow_mass):
    zeroth, first, second = moments
    scale = flow_mass * (-1.6 / 36.0)
    alpha = scale * 3.0 * dot3(first, flow)
    beta = scale * (9.0 * dot3(second_times(second, flow), flow) - 3.0 * zeroth * dot3(flow, flow))
    return alpha, beta


def pack_z(adjoint, coefficients, out):
    core = lax.axis_index("gz")
    lanes = iota(1)
    count = coefficients.shape[2]
    out[2] = jnp.zeros((8, 128), f32)
    for which, (components, source) in enumerate(((ZM, 127), (ZP, 0))):

        @pl.when(core == which)
        def _():
            tiles = [jnp.zeros((8, 128), f32) for _ in range(2)]
            for k, q in enumerate(components):
                for x in range(32):
                    group, lane = divmod(k * 32 + x, 128)
                    column = pltpu.roll(adjoint[q, x].astype(f32), (lane - source) % 128, 1)
                    tiles[group] = jnp.where(lanes == lane, column, tiles[group])
            out[0] = tiles[0]
            out[1] = tiles[1]
            for j in range(2):
                start = 2 * count * j + count * which
                out[2, :, start : start + count] = coefficients[:, j, :]


def pack_y(directions, adjoint, sent, received, *refs):
    outs, (columns, plane, rows) = refs[:-3], refs[-3:]
    core = lax.axis_index("gz")
    load_columns(core, received, columns)
    coarse = sent[2] + received[2]
    high = coarse.astype(bf16)
    rest = coarse - high.astype(f32)
    middle = rest.astype(bf16)
    low = (rest - middle.astype(f32)).astype(bf16)

    def emit(components, row, out):
        for k, q in enumerate(components):

            def step(x, carry):
                tile = pulled_z(q, adjoint[q, x].astype(f32), x, columns)
                plane[pl.ds(pl.multiple_of(x * 8, 8), 8), :] = tile
                return carry

            lax.fori_loop(0, 32, step, 0, unroll=8)
            out[k * 32 : k * 32 + 32, :] = plane[pl.ds(row, 32, stride=8), :].astype(bf16)
        out[160:176, :] = jnp.concatenate([high, middle], axis=0)
        out[176:192, :] = jnp.concatenate([low, jnp.zeros((8, 128), bf16)], axis=0)

    if directions == 1:
        side = lax.axis_index("gy")
        pl.when(side == 0)(lambda: emit(YM, 7, outs[0]))
        pl.when(side == 1)(lambda: emit(YP, 0, outs[0]))
    else:
        emit(YM, 7, outs[0])
        emit(YP, 0, outs[1])


def pull_zy(directions, adjoint, forward, kind, sent_z, received_z, *refs):
    received_y = refs[:directions]
    pulled, to_low, to_high, columns, rows, coarse_ref = refs[directions:]
    core = lax.axis_index("gz")
    load_columns(core, received_z, columns)
    if directions == 1:
        side = lax.axis_index("gy")
        values = received_y[0][...].astype(f32)
        from_high = jnp.where(side == 0, values, 0.0)
        from_low = jnp.where(side == 1, values, 0.0)
    else:
        from_low = received_y[0][...].astype(f32)
        from_high = received_y[1][...].astype(f32)
    rows[0] = from_high
    rows[1] = from_low

    def coarse_of(values):
        return values[160:168] + values[168:176] + values[176:184]

    lanes = iota(1)
    rim = jnp.where(
        lanes < 64, pltpu.roll(coarse_of(from_low), 64, 1), pltpu.roll(coarse_of(from_high), 64, 1)
    )
    own = sent_z[2] + received_z[2]
    for out in (to_low, to_high):
        out[COARSE] = own
        out[COARSE + 1] = rim

    def step(x, carry):
        for q in range(19):
            if VELOCITY[q][1] == 0 and VELOCITY[q][2] == 0:
                pulled[q, x] = adjoint[q, x]
                continue
            tile = pulled_z(q, adjoint[q, x].astype(f32), x, columns)
            pulled[q, x] = pulled_y(q, tile, x, rows).astype(bf16)
        return carry

    lax.fori_loop(0, 32, step, 0)

    for out, base, faces, boundary in ((to_low, 0, XP, 0), (to_high, 28, XM, 31)):
        for k, q in enumerate(faces):
            out[FACE + k] = pulled[q, boundary].astype(f32)

        def edge(position, carry):
            x = base + position
            values = {}
            for q in range(19):
                target = x + VELOCITY[q][0]
                if VELOCITY[q][0] == 0:
                    values[q] = pulled[q, x].astype(f32)
                else:
                    inside = jnp.logical_and(target >= 0, target < 32)
                    tile = pulled[q, jnp.clip(target, 0, 31)].astype(f32)
                    values[q] = jnp.where(inside, tile, 0.0)
            rho, mass = flow_moments([forward[q, x].astype(f32) for q in range(19)])
            inverse = 1.0 / rho
            flow = tuple(component * inverse for component in mass)
            fluid_mass = jnp.where(kind[x] == 0, rho, 0.0)
            alpha, beta = alpha_beta(pair_moments(values), flow, fluid_mass)
            out[ALPHA + position] = alpha
            out[BETA + position] = beta

            @pl.when(x == boundary)
            def _():
                for dimension in range(3):
                    out[FIELD + dimension] = flow[dimension]
                out[FIELD + 3] = fluid_mass

            return carry

        lax.fori_loop(0, 4, edge, 0)


def collide_back(
    pulled, forward, kind, own, low, high, basis_z, basis_y, fold_y, fold_z,
    gradient, fields, window, lines, levels, totals,
):
    core = lax.axis_index("gz")
    zeros = jnp.zeros((16, 128), f32)
    for part in range(2):
        window[part * 16 : part * 16 + 16, :] = zeros
        window[part * 16 : part * 16 + 2, :] = low[COARSE + part, 6:8, :]
        window[part * 16 + 2 : part * 16 + 10, :] = own[COARSE + part]
        window[part * 16 + 10 : part * 16 + 12, :] = high[COARSE + part, 0:2, :]
    lines[...] = jnp.dot(
        window[...], basis_z[core], precision=highest, preferred_element_type=f32
    )
    weights = [basis_y[j] for j in range(4)]
    for i in range(12):
        level = None
        for j, (row, lane) in enumerate(((16, 0), (0, 0), (0, 128), (16, 128))):
            line = jnp.broadcast_to(lines[row + i : row + i + 1, lane : lane + 128], (8, 128))
            term = weights[j] * line
            level = term if level is None else level + term
        levels[i] = level
    totals[...] = jnp.zeros((10, 8, 128), f32)

    def level_set(block, position):
        value = None
        for shift in (-1, 0, 1):
            term = float(spline(position - 4.0 * shift - 1.5)) * levels[block + 2 + shift]
            value = term if value is None else value + term
        return jnp.tanh(4.0 * value)

    def spread(block, position, sensitivity):
        for shift in (-1, 0, 1):
            weight = float(spline(position - 4.0 * shift - 1.5))
            totals[block + 1 + shift] += weight * sensitivity

    def slope_of(bent):
        return -1.8 * (1.0 - bent * bent)

    def plane(x, block, position, fetch):
        bent = level_set(block, position)
        retained = 0.55 + 0.45 * bent
        rho, mass = flow_moments([forward[q, x].astype(f32) for q in range(19)])
        inverse = 1.0 / rho
        flow = tuple(component * inverse for component in mass)
        here = kind[x]
        fluid = here == 0
        share = jnp.where(fluid, retained, 1.0)
        speed = tuple(share * component for component in flow)
        zeroth, first, second = pair_moments({q: fetch(q) for q in range(19)})
        curved = second_times(second, speed)
        slopes = tuple(
            3.0 * first[n] + 9.0 * curved[n] - 3.0 * zeroth * speed[n] for n in range(3)
        )
        along = dot3(slopes, flow)
        value = zeroth + 0.5 * (3.0 * dot3(first, speed) + dot3(slopes, speed))
        factor = jnp.where(fluid, (1.6 / 36.0) * retained, jnp.where(here == 3, inverse * (1.0 / 36.0), 0.0))
        fields[0, x] = jnp.where(fluid, (1.6 / 36.0) * value, 0.0) - factor * along
        for n in range(3):
            fields[1 + n, x] = factor * slopes[n]
        bar = jnp.where(fluid, (-1.6 / 36.0) * rho * along, 0.0)
        spread(block, position, bar * slope_of(bent))

    def inside(q, x):
        return pulled[q, x + VELOCITY[q][0]].astype(f32)

    def at_low(q, x):
        if q in XM:
            return low[FACE + XM.index(q)]
        return inside(q, x)

    def at_high(q, x):
        if q in XP:
            return high[FACE + XP.index(q)]
        return inside(q, x)

    plane(0, 0, 0, lambda q: at_low(q, 0))
    for x in (1, 2, 3):
        plane(x, 0, x, lambda q: inside(q, x))

    def middle(block, carry):
        for position in range(4):
            x = block * 4 + position
            plane(x, block, position, lambda q: inside(q, x))
        return carry

    lax.fori_loop(1, 7, middle, 0)
    for x in (28, 29, 30):
        plane(x, 7, x - 28, lambda q: inside(q, x))
    plane(31, 7, 3, lambda q: at_high(q, 31))

    for ref, block, boundary, faces in ((low, -1, 3, XP), (high, 8, 0, XM)):
        source = 31 if block == 8 else 0
        flow = tuple(ref[FIELD + n] for n in range(3))
        missing = alpha_beta(
            pair_moments({q: pulled[q, source].astype(f32) for q in faces}), flow, ref[FIELD + 3]
        )
        for position in range(4):
            alpha, beta = ref[ALPHA + position], ref[BETA + position]
            if position == boundary:
                alpha, beta = alpha + missing[0], beta + missing[1]
            bent = level_set(block, position)
            sensitivity = (alpha + (0.55 + 0.45 * bent) * beta) * slope_of(bent)
            shift = 1 if block < 0 else -1
            weight = float(spline(position - 4.0 * shift - 1.5))
            totals[block + 1 + shift] += weight * sensitivity

    folded = jnp.dot(
        fold_y[...], totals[1:9].reshape(64, 128), precision=highest, preferred_element_type=f32
    )
    result = jnp.dot(folded, fold_z[core], precision=highest, preferred_element_type=f32)
    for part in range(2):
        for j in range(4):
            gradient[part, j] = result[j * 8 : j * 8 + 8, part * 32 : part * 32 + 32]


def write_prior(pulled, kind, low, high, fields, out):
    def plane(x, fetch):
        here = kind[x]
        solid = here == 1
        keep = jnp.where(here == 0, -0.6, 0.0)
        base, bx, by, bz = (fields[n, x] for n in range(4))
        along = {(0, 0): (base, base)}
        shifts = {}
        for step_x in (-1, 0, 1):
            row = base if step_x == 0 else (base + bx if step_x > 0 else base - bx)
            for step_y in (-1, 0, 1):
                both = row if step_y == 0 else (row + by if step_y > 0 else row - by)
                shifts[step_x, step_y] = both
        values = [fetch(q) for q in range(19)]
        for q in range(19):
            step_x, step_y, step_z = VELOCITY[q]
            shift = shifts[step_x, step_y]
            if step_z:
                shift = shift + bz if step_z > 0 else shift - bz
            kept = jnp.where(solid, values[OPPOSITE[q]], keep * values[q])
            out[q, x] = (kept + shift).astype(bf16)

    def inside(q, x):
        return pulled[q, x + VELOCITY[q][0]].astype(f32)

    plane(0, lambda q: low[FACE + XM.index(q)] if q in XM else inside(q, 0))

    def middle(x, carry):
        plane(x, lambda q: inside(q, x))
        return carry

    lax.fori_loop(1, 31, middle, 0)
    plane(31, lambda q: high[FACE + XP.index(q)] if q in XP else inside(q, 31))


def bases():
    fine = np.arange(128.0)
    basis_z = np.zeros((2, 128, 256))
    fold_z = np.zeros((2, 128, 64))
    for core in range(2):
        full = spline(fine[None, :] + 128 * core - 4.0 * np.arange(64)[:, None] - 1.5)
        basis_z[core, 0:64, 0:128] = full
        basis_z[core, 64:128, 128:256] = full
        fold_z[core, :, 0:32] = full[32 * core : 32 * core + 32].T
        fold_z[core, :, 32:64] = full[32 * (1 - core) : 32 * (1 - core) + 32].T
    across = spline(np.arange(8.0)[None, :] - 4.0 * np.arange(-1, 3)[:, None] - 1.5)
    basis_y = np.broadcast_to(across[:, :, None], (4, 8, 128))
    fold_y = np.zeros((4, 8, 8, 8))
    for i in range(8):
        fold_y[:, i, i, :] = across
    return [
        jnp.asarray(np.ascontiguousarray(a), f32)
        for a in (basis_z, basis_y, fold_y.reshape(32, 64), fold_z)
    ]


def pairs(count, first):
    result = []
    for i in range(first, count - 1, 2):
        result += [(i, i + 1), (i + 1, i)]
    return result


def per_device(forward, adjoint, coefficients, kind):
    count_y = lax.axis_size("gy")
    count_x = lax.axis_size("gx")
    swap = [(0, 1), (1, 0)]
    side = lax.axis_index("gy")
    directions = 1 if count_y == 2 else 2
    tile = (8, 128)

    sent_z = kernel_call(pack_z, jax.ShapeDtypeStruct((3,) + tile, f32))(adjoint, coefficients)
    received_z = lax.ppermute(sent_z, "gz", swap)

    strip = jax.ShapeDtypeStruct((192, 128), bf16)
    sent_y = kernel_call(
        functools.partial(pack_y, directions),
        [strip] * directions,
        [pltpu.VMEM((2, 2) + tile, f32), pltpu.VMEM((256, 128), f32), pltpu.VMEM((32, 128), f32)],
    )(adjoint, sent_z, received_z)
    up = [(i, i + 1) for i in range(count_y - 1)]
    down = [(i + 1, i) for i in range(count_y - 1)]
    if directions == 1:
        received_y = [lax.ppermute(sent_y[0], "gy", swap)]
    else:
        received_y = [lax.ppermute(sent_y[0], "gy", up), lax.ppermute(sent_y[1], "gy", down)]

    bundle = jax.ShapeDtypeStruct((BUNDLE,) + tile, f32)
    pulled, to_low, to_high = kernel_call(
        functools.partial(pull_zy, directions),
        [jax.ShapeDtypeStruct(adjoint.shape, bf16), bundle, bundle],
        [
            pltpu.VMEM((2, 2) + tile, f32),
            pltpu.VMEM((2, 192, 128), f32),
            pltpu.VMEM(tile, f32),
        ],
    )(adjoint, forward, kind, sent_z, received_z, *received_y)
    low = lax.ppermute(to_high, "gx", [(i, i + 1) for i in range(count_x - 1)])
    high = lax.ppermute(to_low, "gx", [(i + 1, i) for i in range(count_x - 1)])

    gradient, fields = kernel_call(
        collide_back,
        [
            jax.ShapeDtypeStruct((2, 4, 8, 32), f32),
            jax.ShapeDtypeStruct((4,) + kind.shape, f32),
        ],
        [
            pltpu.VMEM((32, 128), f32),
            pltpu.VMEM((32, 256), f32),
            pltpu.VMEM((12,) + tile, f32),
            pltpu.VMEM((10,) + tile, f32),
        ],
    )(pulled, forward, kind, to_low, low, high, *bases())

    whole = gradient[0] + lax.ppermute(gradient[1], "gz", swap)
    if directions == 1:
        other = lax.ppermute(jnp.where(side == 0, whole[3], whole[0]), "gy", swap)
        from_low = jnp.where(side == 1, other, 0.0)
        from_high = jnp.where(side == 0, other, 0.0)
    else:
        from_low = lax.ppermute(whole[3], "gy", up)
        from_high = lax.ppermute(whole[0], "gy", down)
    prior = kernel_call(write_prior, jax.ShapeDtypeStruct(adjoint.shape, bf16))(
        pulled, kind, low, high, fields
    )
    return prior, jnp.stack([whole[1] + from_low, whole[2] + from_high], axis=1)


def solution(mesh):
    in_specs = (
        P(None, ("parts", "gx"), "gy", "gz"),
        P(None, ("parts", "gx"), "gy", "gz"),
        P(("parts", "gx"), "gy", "gz"),
        P(("parts", "gx"), "gy", "gz"),
    )
    out_specs = (P(None, ("parts", "gx"), "gy", "gz"), P(("parts", "gx"), "gy", "gz"))
    return jax.shard_map(
        per_device, mesh=mesh, in_specs=in_specs, out_specs=out_specs, check_vma=False
    )
```

time: 96.6 us -> 28.7 us (0.30); the launches traced: 95 us -> 28.4 us
  starting transfers between devices: 39 us -> 11.4 us
  local copies, waits for them, and re-layouts: 22.3 us -> 2.63 us
  waiting for transfers between devices: 18.2 us -> 6.07 us
  other arithmetic: 11.9 us -> 0.02 us
  Pallas kernels: 0 us -> 7.57 us
  matrix products: 2.35 us -> 0 us
    ppermute x18 -> x6, starting transfers between devices: 39 us -> 11.4 us  [the longest x1 4.64 us: per_device(): low = lax.ppermute(to_high, 'gx', [(i, i + 1) for i in range(count_x - 1)])]
    ppermute x18 -> x6, waiting for transfers between devices: 18.2 us -> 6.07 us  [the longest x1 2.07 us: per_device(): received_y = [lax.ppermute(sent_y[0], 'gy', swap)]]
    slice x18 -> x0, local copies, waits for them, and re-layouts: 9.08 us -> none  [the longest x8 3.82 us: padded(): lax.slice_in_dim(block, block.shape[dim] - width, None, axis=dim)]
    pallas_call x0 -> x5, Pallas kernels: none -> 7.57 us  [the longest x1 3.23 us: per_device(): kernel_call(functools.partial(pull_zy, directions), [jax.ShapeDtypeStruct...]
    unnamed x47 -> x17, local copies, waits for them, and re-layouts: 7.38 us -> 2.62 us
    add_any x5 -> x0, other arithmetic: 4.62 us -> none  [the longest x1 2.81 us: collide(): flow_x = moment(populations, 0) / density]
    ppermute x2 -> x0, local copies, waits for them, and re-layouts: 4.24 us -> none  [the longest x1 2.13 us: padded(): lax.ppermute(lax.slice_in_dim(block, block.shape[dim] - width, None, axis...]
    concatenate x6 -> x0, other arithmetic: 2.48 us -> none  [padded(): block = jnp.concatenate([low, block, high], axis=dim)]
  transfers between devices with their start and end apart: 18 -> 6, of which waited for: 5 -> 5; matrix products, arithmetic and copies ran while one was open for 14% -> 0% of each run, Pallas kernels for 0% -> 6%
where the time goes in v1:
time: 28.7 us; the launch traced here: 28.4 us
  starting transfers between devices  11.4 us (40%)
  Pallas kernels  7.57 us (26%)
  waiting for transfers between devices  6.07 us (21%)
  local copies, waits for them, and re-layouts  2.63 us (9%)
  between operations  0.74 us (3%)
    ppermute x1, starting transfers between devices, per_device(): low = lax.ppermute(to_high, 'gx', [(i, i + 1) for i in range(count_x - 1)])  4.64 us
    pallas_call x1, Pallas kernels, per_device(): kernel_call(functools.partial(pull_zy, directions), [jax.ShapeDtypeStruct...  3.23 us
    ppermute x1, starting transfers between devices, per_device(): received_y = [lax.ppermute(sent_y[0], 'gy', swap)]  2.9 us
    unnamed x17, local copies, waits for them, and re-layouts  2.62 us
    ppermute x1, waiting for transfers between devices, per_device(): received_y = [lax.ppermute(sent_y[0], 'gy', swap)]  2.07 us
    ppermute x1, starting transfers between devices, per_device(): other = lax.ppermute(jnp.where(side == 0, whole[3], whole[0]), 'gy', swap)  1.99 us
    pallas_call x1, Pallas kernels, per_device(): kernel_call(write_prior, jax.ShapeDtypeStruct(adjoint.shape, bf16))  1.71 us
    pallas_call x1, Pallas kernels, per_device(): kernel_call(collide_back, [jax.ShapeDtypeStruct((2, 4, 8, 32), f32), jax....  1.61 us
  transfers between devices with their start and end apart: 6, of which 5 were waited for; matrix products, arithmetic and copies ran while one was open for 0% of the time, Pallas kernels for 6%

profile of v1, /device:TPU:0, one launch (start us, length us, event | category | flops | bytes accessed | tf_op | source)
XLA Modules:
  0.0 28.4 jit_solution(10959917610475250408)
XLA Ops:
  0.6 1.3 %copy-done = bf16[19,32,8,128]{3,2,1,0:T(8,128)(2,1)S(1)} copy-done((bf16[19,32,8,128]{3,2,1,0:T(8,128)(2,1)S(1)}, bf16[19,32,8,128]{3,2,1,0:T(8,128)(2,1)}, u32[]{:S(2)}) %copy-start) | copy-done | bytes 1245208
  1.9 0.7 %copy-done.7 = f32[8,2,32]{2,1,0:T(2,128)S(1)} copy-done((f32[8,2,32]{2,1,0:T(2,128)S(1)}, f32[8,2,32]{2,1,0:T(2,128)}, u32[]{:S(2)}) %copy-start.7) | copy-done | bytes 2072
  2.6 0.2 shard_map.95.sent.sent_z
  2.9 0.5 %collective-permute-start = (f32[3,8,128]{2,1,0:T(8,128)S(1)}, f32[3,8,128]{2,1,0:T(8,128)S(1)}, u32[]{:S(2)}, u32[]{:S(2)}) collective-permute-start(f32[3,8,128]{2,1,0:T(8,128)S(1)} %shard_map.95.sent.sent_z), channel_id=1, source_target_pairs={{0,1},{1,0},{2,3},{3,2},{4,5},{5,4},{6,7},{7,6},{8,9},{9,8},{10,11... | collective-permute-start | bytes 36872 | tf_op jit(solution)/shard_map/ppermute | solution.py:512
  3.4 0.8 %collective-permute-done.received.received_z = f32[3,8,128]{2,1,0:T(8,128)S(1)} collective-permute-done((f32[3,8,128]{2,1,0:T(8,128)S(1)}, f32[3,8,128]{2,1,0:T(8,128)S(1)}, u32[]{:S(2)}, u32[]{:S(2)}) %collective-permute-start) | collective-permute-done | bytes 12320 | tf_op jit(solution)/shard_map/ppermute | solution.py:512
  4.2 0.8 %shard_map.96 = bf16[192,128]{1,0:T(8,128)(2,1)S(1)} custom-call(bf16[19,32,8,128]{3,2,1,0:T(8,128)(2,1)S(1)} %copy-done, f32[3,8,128]{2,1,0:T(8,128)S(1)} %shard_map.95.sent.sent_z, f32[3,8,128]{2,1,0:T(8,128)S(1)} %collective-permute-done.received.received_z), custom_call_target="tpu_custom_call" | custom-call | tf_op jit(solution)/shard_map/pallas_call | solution.py:515
  5.0 0.0 copy-start.3
  5.0 0.0 copy-start.4
  5.0 0.0 copy-start.5
  5.0 0.0 copy-start.6
  5.1 2.9 %collective-permute-start.1 = (bf16[192,128]{1,0:T(8,128)(2,1)S(1)}, bf16[192,128]{1,0:T(8,128)(2,1)S(1)}, u32[]{:S(2)}, u32[]{:S(2)}) collective-permute-start(bf16[192,128]{1,0:T(8,128)(2,1)S(1)} %shard_map.96), channel_id=1, source_target_pairs={{0,2},{2,0},{1,3},{3,1},{4,6},{6,4},{5,7},{7,5},{8,10},{10,8},{9,1... | collective-permute-start | bytes 147464 | tf_op jit(solution)/shard_map/ppermute | solution.py:523
  8.0 2.1 %collective-permute-done.1.refs_0_ = bf16[192,128]{1,0:T(8,128)(2,1)S(1)} collective-permute-done((bf16[192,128]{1,0:T(8,128)(2,1)S(1)}, bf16[192,128]{1,0:T(8,128)(2,1)S(1)}, u32[]{:S(2)}, u32[]{:S(2)}) %collective-permute-start.1) | collective-permute-done | bytes 49184 | tf_op jit(solution)/shard_map/ppermute | solution.py:523
  10.0 3.2 %shard_map.97 = (bf16[19,32,8,128]{3,2,1,0:T(8,128)(2,1)S(1)}, f32[19,8,128]{2,1,0:T(8,128)S(1)}, f32[19,8,128]{2,1,0:T(8,128)S(1)}) custom-call(bf16[19,32,8,128]{3,2,1,0:T(8,128)(2,1)S(1)} %copy-done, bf16[19,32,8,128]{3,2,1,0:T(8,128)(2,1)S(1)} %copy-done.1, s32[32,8,128]{2,1,0:T(8,128)S(1)} %copy-done.2, f32[3,8,128]{2,1,0:T(8,128)S(1)} %shard_map.95.sent.sent_z, ...), custom_call_target="tpu_custom_call" | custom-call | tf_op jit(solution)/shard_map/pallas_call | solution.py:528
  13.3 1.3 %collective-permute-start.3 = (f32[19,8,128]{2,1,0:T(8,128)S(1)}, f32[19,8,128]{2,1,0:T(8,128)S(1)}, u32[]{:S(2)}, u32[]{:S(2)}) collective-permute-start(f32[19,8,128]{2,1,0:T(8,128)S(1)} %get-tuple-element.9.own), channel_id=1, source_target_pairs={{4,0},{8,4},{12,8},{5,1},{9,5},{13,9},{6,2},{10,6},{14,10},{7,3},{... | collective-permute-start | bytes 233480 | tf_op jit(solution)/shard_map/ppermute | solution.py:538
  14.6 4.6 %collective-permute-start.2 = (f32[19,8,128]{2,1,0:T(8,128)S(1)}, f32[19,8,128]{2,1,0:T(8,128)S(1)}, u32[]{:S(2)}, u32[]{:S(2)}) collective-permute-start(f32[19,8,128]{2,1,0:T(8,128)S(1)} %get-tuple-element.8), channel_id=1, source_target_pairs={{0,4},{4,8},{8,12},{1,5},{5,9},{9,13},{2,6},{6,10},{10,14},{3,7},{... | collective-permute-start | bytes 233480 | tf_op jit(solution)/shard_map/ppermute | solution.py:537
  19.2 0.4 %collective-permute-done.3.high = f32[19,8,128]{2,1,0:T(8,128)S(1)} collective-permute-done((f32[19,8,128]{2,1,0:T(8,128)S(1)}, f32[19,8,128]{2,1,0:T(8,128)S(1)}, u32[]{:S(2)}, u32[]{:S(2)}) %collective-permute-start.3) | collective-permute-done | bytes 77856 | tf_op jit(solution)/shard_map/ppermute | solution.py:538
  19.7 1.6 %collective-permute-done.2.low = f32[19,8,128]{2,1,0:T(8,128)S(1)} collective-permute-done((f32[19,8,128]{2,1,0:T(8,128)S(1)}, f32[19,8,128]{2,1,0:T(8,128)S(1)}, u32[]{:S(2)}, u32[]{:S(2)}) %collective-permute-start.2) | collective-permute-done | bytes 77856 | tf_op jit(solution)/shard_map/ppermute | solution.py:537
  21.2 1.6 %shard_map.98 = (f32[2,4,8,32]{3,2,1,0:T(8,128)S(1)}, f32[4,32,8,128]{3,2,1,0:T(8,128)S(1)}) custom-call(bf16[19,32,8,128]{3,2,1,0:T(8,128)(2,1)S(1)} %get-tuple-element.7.pulled, bf16[19,32,8,128]{3,2,1,0:T(8,128)(2,1)S(1)} %copy-done.1, s32[32,8,128]{2,1,0:T(8,128)S(1)} %copy-done.2, f32[19,8,128]{2,1,0:T(8,128)S(1)} %get-tuple-element.9.own, ...), custom_call_target="tpu_custom_call" | custom-call | tf_op jit(solution)/shard_map/pallas_call | solution.py:540
  22.9 0.1 collective-permute-start.4
  22.9 1.2 %collective-permute-done.4 = f32[4,8,32]{2,1,0:T(8,128)S(1)} collective-permute-done((f32[4,8,32]{2,1,0:T(8,128)S(1)}, f32[4,8,32]{2,1,0:T(8,128)S(1)}, u32[]{:S(2)}, u32[]{:S(2)}) %collective-permute-start.4) | collective-permute-done | bytes 4128 | tf_op jit(solution)/shard_map/ppermute | solution.py:554
  24.1 2.0 %collective-permute-start.5 = (f32[8,32]{1,0:T(8,128)S(1)}, f32[8,32]{1,0:T(8,128)S(1)}, u32[]{:S(2)}, u32[]{:S(2)}) collective-permute-start(f32[8,32]{1,0:T(8,128)S(1)} %fusion.2), channel_id=1, source_target_pairs={{0,2},{2,0},{1,3},{3,1},{4,6},{6,4},{5,7},{7,5},{8,10},{10,8},{9,1... | collective-permute-start | bytes 3080 | tf_op jit(solution)/shard_map/ppermute | solution.py:556
  26.1 1.7 %shard_map.99 = bf16[19,32,8,128]{3,2,1,0:T(8,128)(2,1)} custom-call(bf16[19,32,8,128]{3,2,1,0:T(8,128)(2,1)S(1)} %get-tuple-element.7.pulled, s32[32,8,128]{2,1,0:T(8,128)S(1)} %copy-done.2, f32[19,8,128]{2,1,0:T(8,128)S(1)} %collective-permute-done.2.low, f32[19,8,128]{2,1,0:T(8,128)S(1)} %collective-permute-done.3.high, ...), custom_call_target="tpu_custom_call" | custom-call | tf_op jit(solution)/shard_map/pallas_call | solution.py:562
  27.8 0.0 collective-permute-done.5
  27.8 0.6 %copy.10 = f32[8,2,32]{2,1,0:T(2,128)} copy(f32[8,2,32]{2,0,1:T(8,128)S(1)} %pad_maximum_fusion) | data formatting | bytes 4096
  (15 shorter events, 0.0 us)
Async XLA Ops:
  0.6 1.3 %copy-start = (bf16[19,32,8,128]{3,2,1,0:T(8,128)(2,1)S(1)}, bf16[19,32,8,128]{3,2,1,0:T(8,128)(2,1)}, u32[]{:S(2)}) copy-start(bf16[19,32,8,128]{3,2,1,0:T(8,128)(2,1)} %adjoint.5) | copy-start | bytes 3735556
  1.9 0.7 %copy-start.7 = (f32[8,2,32]{2,1,0:T(2,128)S(1)}, f32[8,2,32]{2,1,0:T(2,128)}, u32[]{:S(2)}) copy-start(f32[8,2,32]{2,1,0:T(2,128)} %coefficients.1) | copy-start | bytes 6148
  2.6 7.4 %copy-start.1 = (bf16[19,32,8,128]{3,2,1,0:T(8,128)(2,1)S(1)}, bf16[19,32,8,128]{3,2,1,0:T(8,128)(2,1)}, u32[]{:S(2)}) copy-start(bf16[19,32,8,128]{3,2,1,0:T(8,128)(2,1)} %forward.3) | copy-start | bytes 3735556
  2.6 7.4 %copy-start.2 = (s32[32,8,128]{2,1,0:T(8,128)S(1)}, s32[32,8,128]{2,1,0:T(8,128)}, u32[]{:S(2)}) copy-start(s32[32,8,128]{2,1,0:T(8,128)} %kind.5) | copy-start | bytes 393220
  2.9 1.3 %collective-permute-start = (f32[3,8,128]{2,1,0:T(8,128)S(1)}, f32[3,8,128]{2,1,0:T(8,128)S(1)}, u32[]{:S(2)}, u32[]{:S(2)}) collective-permute-start(f32[3,8,128]{2,1,0:T(8,128)S(1)} %shard_map.95.sent.sent_z), channel_id=1, source_target_pairs={{0,1},{1,0},{2,3},{3,2},{4,5},{5,4},{6,7},{7,6},{8,9},{9,8},{10,11... | collective-permute-start | bytes 36872 | tf_op jit(solution)/shard_map/ppermute | solution.py:512
  5.0 16.2 %copy-start.3 = (f32[2,128,256]{2,1,0:T(8,128)S(1)}, f32[2,128,256]{2,1,0:T(8,128)}, u32[]{:S(2)}) copy-start(f32[2,128,256]{2,1,0:T(8,128)} %constant.18.clone.basis_z) | copy-start | bytes 786436
  5.0 16.2 %copy-start.4 = (f32[2,128,64]{2,1,0:T(8,128)S(1)}, f32[2,128,64]{2,1,0:T(8,128)}, u32[]{:S(2)}) copy-start(f32[2,128,64]{2,1,0:T(8,128)} %constant.21.clone.fold_z) | copy-start | bytes 196612
  5.0 16.2 %copy-start.5 = (f32[4,8,128]{2,1,0:T(8,128)S(1)}, f32[4,8,128]{2,1,0:T(8,128)}, u32[]{:S(2)}) copy-start(f32[4,8,128]{2,1,0:T(8,128)} %constant.19.clone.basis_y) | copy-start | bytes 49156
  5.0 16.2 %copy-start.6 = (f32[32,64]{1,0:T(8,128)S(1)}, f32[32,64]{1,0:T(8,128)}, u32[]{:S(2)}) copy-start(f32[32,64]{1,0:T(8,128)} %constant.20.clone.fold_y) | copy-start | bytes 24580
  5.1 5.0 %collective-permute-start.1 = (bf16[192,128]{1,0:T(8,128)(2,1)S(1)}, bf16[192,128]{1,0:T(8,128)(2,1)S(1)}, u32[]{:S(2)}, u32[]{:S(2)}) collective-permute-start(bf16[192,128]{1,0:T(8,128)(2,1)S(1)} %shard_map.96), channel_id=1, source_target_pairs={{0,2},{2,0},{1,3},{3,1},{4,6},{6,4},{5,7},{7,5},{8,10},{10,8},{9,1... | collective-permute-start | bytes 147464 | tf_op jit(solution)/shard_map/ppermute | solution.py:523
  13.3 6.4 %collective-permute-start.3 = (f32[19,8,128]{2,1,0:T(8,128)S(1)}, f32[19,8,128]{2,1,0:T(8,128)S(1)}, u32[]{:S(2)}, u32[]{:S(2)}) collective-permute-start(f32[19,8,128]{2,1,0:T(8,128)S(1)} %get-tuple-element.9.own), channel_id=1, source_target_pairs={{4,0},{8,4},{12,8},{5,1},{9,5},{13,9},{6,2},{10,6},{14,10},{7,3},{... | collective-permute-start | bytes 233480 | tf_op jit(solution)/shard_map/ppermute | solution.py:538
  14.6 6.6 %collective-permute-start.2 = (f32[19,8,128]{2,1,0:T(8,128)S(1)}, f32[19,8,128]{2,1,0:T(8,128)S(1)}, u32[]{:S(2)}, u32[]{:S(2)}) collective-permute-start(f32[19,8,128]{2,1,0:T(8,128)S(1)} %get-tuple-element.8), channel_id=1, source_target_pairs={{0,4},{4,8},{8,12},{1,5},{5,9},{9,13},{2,6},{6,10},{10,14},{3,7},{... | collective-permute-start | bytes 233480 | tf_op jit(solution)/shard_map/ppermute | solution.py:537
  22.9 1.2 %collective-permute-start.4 = (f32[4,8,32]{2,1,0:T(8,128)S(1)}, f32[4,8,32]{2,1,0:T(8,128)S(1)}, u32[]{:S(2)}, u32[]{:S(2)}) collective-permute-start(f32[4,8,32]{2,1,0:T(8,128)S(1)} %slice_bitcast_fusion), channel_id=1, source_target_pairs={{0,1},{1,0},{2,3},{3,2},{4,5},{5,4},{6,7},{7,6},{8,9},{9,8},{10,11... | collective-permute-start | bytes 12296 | tf_op jit(solution)/shard_map/ppermute | solution.py:554
  24.1 3.7 %collective-permute-start.5 = (f32[8,32]{1,0:T(8,128)S(1)}, f32[8,32]{1,0:T(8,128)S(1)}, u32[]{:S(2)}, u32[]{:S(2)}) collective-permute-start(f32[8,32]{1,0:T(8,128)S(1)} %fusion.2), channel_id=1, source_target_pairs={{0,2},{2,0},{1,3},{3,1},{4,6},{6,4},{5,7},{7,5},{8,10},{10,8},{9,1... | collective-permute-start | bytes 3080 | tf_op jit(solution)/shard_map/ppermute | solution.py:556

commit v2 on v1

v2 whole, which is shorter than its diff:
```python
import functools

import jax
import jax.numpy as jnp
import numpy as np
from jax import lax
from jax.experimental import pallas as pl
from jax.experimental.pallas import tpu as pltpu
from jax.sharding import PartitionSpec as P

VELOCITY = (
    (0, 0, 0),
    (1, 0, 0),
    (-1, 0, 0),
    (0, 1, 0),
    (0, -1, 0),
    (0, 0, 1),
    (0, 0, -1),
    (1, 1, 0),
    (-1, -1, 0),
    (1, -1, 0),
    (-1, 1, 0),
    (1, 0, 1),
    (-1, 0, -1),
    (1, 0, -1),
    (-1, 0, 1),
    (0, 1, 1),
    (0, -1, -1),
    (0, 1, -1),
    (0, -1, 1),
)
OPPOSITE = (0, 2, 1, 4, 3, 6, 5, 8, 7, 10, 9, 12, 11, 14, 13, 16, 15, 18, 17)
highest = lax.Precision.HIGHEST
f32 = jnp.float32
bf16 = jnp.bfloat16


def going(dimension, sign):
    return [q for q in range(19) if VELOCITY[q][dimension] == sign]


XP, XM = going(0, 1), going(0, -1)
YP, YM = going(1, 1), going(1, -1)
ZP, ZM = going(2, 1), going(2, -1)

FACE, ALPHA, BETA, FIELD, LEVEL, BUNDLE = 0, 5, 9, 13, 17, 19
COARSE_ROWS, STRIP = 160, 192
MASS, INVERSE = 3, 4
EDGE_PLANES = (0, 1, 2, 3, 28, 29, 30, 31)


def spline(distance):
    radius = np.abs(distance) / 6.0
    return np.where(radius < 1.0, (1.0 - radius) ** 4 * (1.0 + 4.0 * radius), 0.0)


def kernel_call(body, out_shape, scratch_shapes=(), aliases=None, **specs):
    return pl.pallas_call(
        body,
        out_shape=out_shape,
        scratch_shapes=list(scratch_shapes),
        compiler_params=pltpu.CompilerParams(vmem_limit_bytes=12 * 1024 * 1024),
        input_output_aliases=aliases or {},
        **specs,
    )


def iota(dimension):
    return lax.broadcasted_iota(jnp.int32, (8, 128), dimension)


def pulled_z(q, tile, x, columns):
    step = VELOCITY[q][2]
    if step == 0:
        return tile
    slot = (ZP if step > 0 else ZM).index(q) * 32
    group, lane = slot // 128, slot % 128
    lanes = iota(1)
    edge = columns[0 if step > 0 else 1, group]
    if step > 0:
        edge = pltpu.roll(edge, 127 - lane - x, 1)
        return jnp.where(lanes == 127, edge, pltpu.roll(tile, 127, 1))
    edge = pltpu.roll(edge, (128 - lane - x) & 127, 1)
    return jnp.where(lanes == 0, edge, pltpu.roll(tile, 1, 1))


def load_columns(core, received, columns):
    for group in range(2):
        tile = received[group]
        columns[0, group] = jnp.where(core == 0, tile, 0.0)
        columns[1, group] = jnp.where(core == 1, tile, 0.0)


def pair_moments(populations):
    sums, diffs = {}, {}
    for q in range(1, 19, 2):
        a, b = populations.get(q), populations.get(q + 1)
        if a is None and b is None:
            continue
        if b is None:
            sums[q], diffs[q] = a, a
        elif a is None:
            sums[q], diffs[q] = b, -b
        else:
            sums[q], diffs[q] = a + b, a - b

    def total(terms):
        value = None
        for sign, table, q in terms:
            if q not in table:
                continue
            item = table[q]
            if value is None:
                value = item if sign > 0 else -item
            else:
                value = value + item if sign > 0 else value - item
        return value

    def plus(a, b):
        return b if a is None else (a if b is None else a + b)

    def twice(a):
        return None if a is None else a + a

    xx = total([(1, sums, 7), (1, sums, 9), (1, sums, 11), (1, sums, 13)])
    edge_yz = total([(1, sums, 15), (1, sums, 17)])
    edge_xy = total([(1, sums, 7), (1, sums, 9)])
    edge_xz = total([(1, sums, 11), (1, sums, 13)])
    sx, sy, sz = (twice(sums.get(q)) for q in (1, 3, 5))
    zeroth = plus(plus(xx, edge_yz), plus(plus(sx, sy), sz))
    if 0 in populations:
        zeroth = zeroth + 12.0 * populations[0]
    mx = plus(twice(diffs.get(1)), total([(1, diffs, 7), (1, diffs, 9), (1, diffs, 11), (1, diffs, 13)]))
    my = plus(twice(diffs.get(3)), total([(1, diffs, 7), (-1, diffs, 9), (1, diffs, 15), (1, diffs, 17)]))
    mz = plus(twice(diffs.get(5)), total([(1, diffs, 11), (-1, diffs, 13), (1, diffs, 15), (-1, diffs, 17)]))
    mxx = plus(sx, xx)
    myy = plus(sy, plus(edge_xy, edge_yz))
    mzz = plus(sz, plus(edge_xz, edge_yz))
    mxy = total([(1, sums, 7), (-1, sums, 9)])
    mxz = total([(1, sums, 11), (-1, sums, 13)])
    myz = total([(1, sums, 15), (-1, sums, 17)])
    return zeroth, (mx, my, mz), (mxx, myy, mzz, mxy, mxz, myz)


def flow_moments(populations):
    sums = {q: populations[q] + populations[q + 1] for q in range(1, 19, 2)}
    diffs = {q: populations[q] - populations[q + 1] for q in range(1, 19, 2)}
    rho = populations[0]
    for q in range(1, 19, 2):
        rho = rho + sums[q]
    jx = (diffs[1] + diffs[7]) + (diffs[9] + diffs[11]) + diffs[13]
    jy = (diffs[3] + diffs[7]) + (diffs[15] - diffs[9]) + diffs[17]
    jz = (diffs[5] + diffs[11]) + (diffs[15] - diffs[13]) - diffs[17]
    return rho, (jx, jy, jz)


def dot3(a, b):
    return a[0] * b[0] + a[1] * b[1] + a[2] * b[2]


def second_times(second, v):
    mxx, myy, mzz, mxy, mxz, myz = second

    def row(terms):
        value = None
        for coefficient, component in terms:
            if coefficient is None:
                continue
            product = coefficient * component
            value = product if value is None else value + product
        return value

    return (
        row([(mxx, v[0]), (mxy, v[1]), (mxz, v[2])]),
        row([(mxy, v[0]), (myy, v[1]), (myz, v[2])]),
        row([(mxz, v[0]), (myz, v[1]), (mzz, v[2])]),
    )


def alpha_beta(moments, flow, flow_mass):
    zeroth, first, second = moments
    scale = flow_mass * (-1.6 / 36.0)
    alpha = scale * 3.0 * dot3(first, flow)
    beta = scale * (9.0 * dot3(second_times(second, flow), flow) - 3.0 * zeroth * dot3(flow, flow))
    return alpha, beta


def rows_of(x):
    return pl.ds(pl.multiple_of(x * 8, 8), 8) if not isinstance(x, int) else slice(x * 8, x * 8 + 8)


def pack_z(adjoint, coefficients, out, faces, coarse, semaphores):
    core = lax.axis_index("gz")
    copies = [pltpu.make_async_copy(coefficients, coarse, semaphores.at[5])]
    for k in range(5):
        q = ZM[k] + core * (ZP[k] - ZM[k])
        copies.append(pltpu.make_async_copy(adjoint.at[q], faces.at[k], semaphores.at[k]))
    for copy in copies:
        copy.start()
    lanes = iota(1)
    count = coefficients.shape[2]
    out[2] = jnp.zeros((8, 128), f32)
    out[3] = jnp.zeros((8, 128), f32)
    for copy in copies:
        copy.wait()
    for which, source in enumerate((127, 0)):

        @pl.when(core == which)
        def _():
            for j in range(2):
                out[2 + j, :, count * which : count * which + count] = coarse[:, j, :]
            chains = {}
            for k in range(5):
                for x in range(32):
                    group, lane = divmod(k * 32 + x, 128)
                    column = pltpu.roll(faces[k, x].astype(f32), (lane - source) % 128, 1)
                    chain = group, lane // 16
                    if chain in chains:
                        column = jnp.where(lanes >= lane, column, chains[chain])
                    chains[chain] = column
            for group in range(2):
                tile = chains[group, 0]
                for part in range(1, 8 if group == 0 else 2):
                    tile = jnp.where(lanes >= part * 16, chains[group, part], tile)
                out[group] = tile


def y_sides(directions):
    return ((YM, 7), (YP, 0))


def gather_rows(directions, adjoint, *refs):
    outs, plane = refs[:-1], refs[-1]
    lanes = lax.broadcasted_iota(jnp.int32, (32, 128), 1)

    def emit(components, row, out):
        for k, q in enumerate(components):
            for x in range(32):
                plane[x * 8 : x * 8 + 8, :] = adjoint[q, x].astype(f32)
            rows = plane[pl.ds(row, 32, stride=8), :]
            step = VELOCITY[q][2]
            if step > 0:
                rows = jnp.where(lanes == 127, 0.0, pltpu.roll(rows, 127, 1))
            elif step < 0:
                rows = jnp.where(lanes == 0, 0.0, pltpu.roll(rows, 1, 1))
            out[k * 32 : k * 32 + 32, :] = rows

    sides = y_sides(directions)
    if directions == 1:
        side = lax.axis_index("gy")
        for n in range(2):
            pl.when(side == n)(functools.partial(emit, *sides[n], outs[0]))
    else:
        for n in range(2):
            emit(*sides[n], outs[n])


def pack_y(directions, sent, received, *refs):
    sources, outs = refs[:directions], refs[directions:]
    core = lax.axis_index("gz")
    lanes = lax.broadcasted_iota(jnp.int32, (32, 128), 1)
    sublanes = lax.broadcasted_iota(jnp.int32, (32, 128), 0)

    def emit(components, row, coarse_row, source, out):
        for k, q in enumerate(components):
            rows = source[k * 32 : k * 32 + 32, :]
            step = VELOCITY[q][2]
            if step:
                slot = (ZP if step > 0 else ZM).index(q) * 32
                group, lane = slot // 128, slot % 128
                spread = jnp.broadcast_to(received[group, row : row + 1, :], (32, 128))
                column = jnp.sum(jnp.where(lanes == sublanes + lane, spread, 0.0), axis=1, keepdims=True)
                column = jnp.where(core == (0 if step > 0 else 1), column, 0.0)
                rows = rows + jnp.where(lanes == (127 if step > 0 else 0), column, 0.0)
            out[k * 32 : k * 32 + 32, :] = rows.astype(bf16)
        coarse = sent[coarse_row] + received[coarse_row]
        high = coarse.astype(bf16)
        rest = coarse - high.astype(f32)
        middle = rest.astype(bf16)
        low = (rest - middle.astype(f32)).astype(bf16)
        out[COARSE_ROWS : COARSE_ROWS + 16, :] = jnp.concatenate([high, middle], axis=0)
        out[COARSE_ROWS + 16 : STRIP, :] = jnp.concatenate([low, jnp.zeros((8, 128), bf16)], axis=0)

    sides = y_sides(directions)
    if directions == 1:
        side = lax.axis_index("gy")
        for n in range(2):
            pl.when(side == n)(functools.partial(emit, *sides[n], 3 - n, sources[0], outs[0]))
    else:
        for n in range(2):
            emit(*sides[n], 3 - n, sources[n], outs[n])


def pull_zy(adjoint, forward, kind, sent, received, basis_z, pulled, flows, lines, columns):
    core = lax.axis_index("gz")
    load_columns(core, received, columns)
    sublanes = iota(0)
    coarse = jnp.concatenate([sent[2] + received[2], sent[3] + received[3]], axis=0)
    lines[...] = jnp.dot(coarse, basis_z[core], precision=highest, preferred_element_type=f32)

    def step(x, carry):
        for q in range(19):
            tile = pulled_z(q, adjoint[q, x].astype(f32), x, columns)
            step_y = VELOCITY[q][1]
            if step_y > 0:
                tile = jnp.where(sublanes == 7, 0.0, pltpu.roll(tile, 7, 0))
            elif step_y < 0:
                tile = jnp.where(sublanes == 0, 0.0, pltpu.roll(tile, 1, 0))
            pulled[q, rows_of(x), :] = tile
        rho, mass = flow_moments([forward[q, x].astype(f32) for q in range(19)])
        inverse = 1.0 / rho
        for n in range(3):
            flows[n, x] = mass[n] * inverse
        flows[MASS, x] = jnp.where(kind[x] == 0, rho, 0.0)
        flows[INVERSE, x] = inverse
        return carry

    lax.fori_loop(0, 32, step, 0, unroll=4)


def pack_x(directions, unpatched, flows, lines, basis_z, basis_y, *refs):
    received = refs[:directions]
    pulled, out_a, out_b, edges, levels, extra = refs[directions:]
    del unpatched
    core = lax.axis_index("gz")
    side = lax.axis_index("gy")
    even = lax.rem(lax.axis_index("gx"), 2) == 0

    def patch(components, row, strip):
        for k, q in enumerate(components):
            pulled[q, pl.ds(row, 32, stride=8), :] = strip[k * 32 : k * 32 + 32, :].astype(f32)

    def outer_line(strip):
        parts = strip[COARSE_ROWS:STRIP, :].astype(f32)
        coarse = parts[0:8] + parts[8:16] + parts[16:24]
        return jnp.dot(coarse, basis_z[core], precision=highest, preferred_element_type=f32)

    if directions == 1:
        pl.when(side == 0)(lambda: patch(YP, 7, received[0]))
        pl.when(side == 1)(lambda: patch(YM, 0, received[0]))
        outer = [(outer_line(received[0]), basis_y[3 - 3 * side])]
    else:
        patch(YM, 0, received[0])
        patch(YP, 7, received[1])
        outer = [(outer_line(received[0]), basis_y[0]), (outer_line(received[1]), basis_y[3])]
    terms = [(lines[0:8, :], basis_y[1]), (lines[8:16, :], basis_y[2])] + outer
    for n, (line, _) in enumerate(terms):
        extra[n * 8 : n * 8 + 8, :] = line
    for i in range(8):
        level = None
        for n, (_, weight) in enumerate(terms):
            term = weight * jnp.broadcast_to(extra[n * 8 + i : n * 8 + i + 1, :], (8, 128))
            level = term if level is None else level + term
        levels[i] = level

    def put(slot, low, high):
        out_a[slot] = jnp.where(even, high, low)
        out_b[slot] = jnp.where(even, low, high)

    for k in range(5):
        put(FACE + k, pulled[XP[k], rows_of(0), :], pulled[XM[k], rows_of(31), :])
    for n in range(4):
        put(FIELD + n, flows[n, 0], flows[n, 31])
    for n in range(2):
        put(LEVEL + n, levels[n], levels[6 + n])
    results = []
    for x in EDGE_PLANES:
        values = {}
        for q in range(19):
            target = x + VELOCITY[q][0]
            if 0 <= target < 32:
                values[q] = pulled[q, rows_of(target), :]
        flow = tuple(flows[n, x] for n in range(3))
        results.append(alpha_beta(pair_moments(values), flow, flows[MASS, x]))
    for position in range(4):
        for n, slot in enumerate((ALPHA, BETA)):
            low, high = results[position][n], results[4 + position][n]
            edges[n, position] = low
            edges[n, 4 + position] = high
            put(slot + position, low, high)


def slope_of(bent):
    return -1.8 * (1.0 - bent * bent)


def bent_level(around, position):
    value = None
    for shift, level in zip((-1, 0, 1), around):
        term = float(spline(position - 4.0 * shift - 1.5)) * level
        value = term if value is None else value + term
    return jnp.tanh(4.0 * value)


def weight_of(position, shift):
    return float(spline(position - 4.0 * shift - 1.5))


def prior_fields(bent, here, flow, inverse, moments):
    zeroth, first, second = moments
    fluid = here == 0
    retained = 0.55 + 0.45 * bent
    share = jnp.where(fluid, retained, 1.0)
    speed = tuple(share * component for component in flow)
    curved = second_times(second, speed)
    slopes = tuple(3.0 * first[n] + 9.0 * curved[n] - 3.0 * zeroth * speed[n] for n in range(3))
    along = dot3(slopes, flow)
    value = zeroth + 0.5 * (3.0 * dot3(first, speed) + dot3(slopes, speed))
    factor = jnp.where(
        fluid, (1.6 / 36.0) * retained, jnp.where(here == 3, inverse * (1.0 / 36.0), 0.0)
    )
    base = jnp.where(fluid, (1.6 / 36.0) * value, 0.0) - factor * along
    return (base,) + tuple(factor * slope for slope in slopes), along


def emit_prior(stage, slot, here, values, result):
    solid = here == 1
    keep = jnp.where(here == 0, -0.6, 0.0)
    base, bx, by, bz = result
    shifts = {}
    for step_x in (-1, 0, 1):
        row = base if step_x == 0 else (base + bx if step_x > 0 else base - bx)
        for step_y in (-1, 0, 1):
            both = row if step_y == 0 else (row + by if step_y > 0 else row - by)
            shifts[step_x, step_y] = both
    for q in range(19):
        step_x, step_y, step_z = VELOCITY[q]
        shift = shifts[step_x, step_y]
        if step_z:
            shift = shift + bz if step_z > 0 else shift - bz
        kept = jnp.where(solid, values[OPPOSITE[q]], keep * values[q])
        stage[q, slot] = (kept + shift).astype(bf16)


def collide_inside(pulled, flows, kind, levels, out, totals, stage, semaphores):
    totals[...] = jnp.zeros((8, 8, 128), f32)

    def middle(block, carry):
        around = [levels[block - 1], levels[block], levels[block + 1]]
        sums = [None] * 3
        for position in range(4):
            x = block * 4 + position
            bent = bent_level(around, position)
            flow = tuple(flows[n, x] for n in range(3))
            values = {q: pulled[q, rows_of(x + VELOCITY[q][0]), :] for q in range(19)}
            result, along = prior_fields(bent, kind[x], flow, flows[INVERSE, x], pair_moments(values))
            emit_prior(stage, x - 4, kind[x], values, result)
            sensitivity = (-1.6 / 36.0) * flows[MASS, x] * along * slope_of(bent)
            for n in range(3):
                term = weight_of(position, n - 1) * sensitivity
                sums[n] = term if sums[n] is None else sums[n] + term
        for n in range(3):
            totals[block + n - 1] += sums[n]
        return carry

    copies = []
    for part in range(3):
        lax.fori_loop(1 + 2 * part, 3 + 2 * part, middle, 0)
        copies.append(
            pltpu.make_async_copy(
                stage.at[:, pl.ds(8 * part, 8)], out.at[:, pl.ds(4 + 8 * part, 8)], semaphores.at[part]
            )
        )
        copies[part].start()
    for copy in copies:
        copy.wait()


def along_x(received_a, received_b):
    even = lax.rem(lax.axis_index("gx"), 2) == 0

    def low(slot):
        return jnp.where(even, received_b[slot], received_a[slot])

    def high(slot):
        return jnp.where(even, received_a[slot], received_b[slot])

    return low, high


def project(pulled, flows, edges, levels, received_a, received_b, inner, fold_y, fold_z, gradient):
    core = lax.axis_index("gz")
    low, high = along_x(received_a, received_b)
    totals = [inner[i] for i in range(8)]
    lower = [low(LEVEL), low(LEVEL + 1)] + [levels[i] for i in range(3)]
    upper = [levels[i] for i in range(5, 8)] + [high(LEVEL), high(LEVEL + 1)]

    def add(block, position, alpha, beta):
        start = block + 1 if block < 4 else block - 6
        around = (lower if block < 4 else upper)[start : start + 3]
        bent = bent_level(around, position)
        sensitivity = (alpha + (0.55 + 0.45 * bent) * beta) * slope_of(bent)
        for shift in (-1, 0, 1):
            if 0 <= block + shift < 8:
                totals[block + shift] = totals[block + shift] + weight_of(position, shift) * sensitivity

    def faces(ref, components):
        return pair_moments({q: ref(FACE + k) for k, q in enumerate(components)})

    def own(x, components):
        return pair_moments({q: pulled[q, rows_of(x), :] for q in components})

    def flow_at(x):
        return tuple(flows[n, x] for n in range(3))

    missing = {
        (0, 0): alpha_beta(faces(low, XM), flow_at(0), flows[MASS, 0]),
        (7, 3): alpha_beta(faces(high, XP), flow_at(31), flows[MASS, 31]),
        (-1, 3): alpha_beta(own(0, XP), tuple(low(FIELD + n) for n in range(3)), low(FIELD + 3)),
        (8, 0): alpha_beta(own(31, XM), tuple(high(FIELD + n) for n in range(3)), high(FIELD + 3)),
    }
    for block in (-1, 0, 7, 8):
        for position in range(4):
            if block in (0, 7):
                index = position + (4 if block else 0)
                alpha, beta = edges[0, index], edges[1, index]
            else:
                ref = low if block < 0 else high
                alpha, beta = ref(ALPHA + position), ref(BETA + position)
            if (block, position) in missing:
                more = missing[block, position]
                alpha, beta = alpha + more[0], beta + more[1]
            add(block, position, alpha, beta)
    stacked = jnp.concatenate(totals, axis=0)
    folded = jnp.dot(fold_y[...], stacked, precision=highest, preferred_element_type=f32)
    result = jnp.dot(folded, fold_z[core], precision=highest, preferred_element_type=f32)
    for part in range(2):
        for j in range(4):
            gradient[part, j] = result[j * 8 : j * 8 + 8, part * 32 : part * 32 + 32]


def collide_outside(pulled, flows, kind, levels, received_a, received_b, inner, out, stage, semaphores):
    del inner
    low, high = along_x(received_a, received_b)
    copies = []
    for part, planes in enumerate((EDGE_PLANES[:4], EDGE_PLANES[4:])):
        for slot, x in enumerate(planes):
            values = {}
            for q in range(19):
                target = x + VELOCITY[q][0]
                if target < 0:
                    values[q] = low(FACE + XM.index(q))
                elif target > 31:
                    values[q] = high(FACE + XP.index(q))
                else:
                    values[q] = pulled[q, rows_of(target), :]
            around = (
                [levels[6], levels[7], high(LEVEL)] if part else [low(LEVEL + 1), levels[0], levels[1]]
            )
            flow = tuple(flows[n, x] for n in range(3))
            result, _ = prior_fields(
                bent_level(around, slot), kind[x], flow, flows[INVERSE, x], pair_moments(values)
            )
            emit_prior(stage, 4 * part + slot, kind[x], values, result)
        copies.append(
            pltpu.make_async_copy(
                stage.at[:, pl.ds(4 * part, 4)], out.at[:, pl.ds(28 * part, 4)], semaphores.at[part]
            )
        )
        copies[part].start()
    for copy in copies:
        copy.wait()


def bases():
    fine = np.arange(128.0)
    basis_z = np.zeros((2, 128, 128))
    fold_z = np.zeros((2, 128, 64))
    for core in range(2):
        full = spline(fine[None, :] + 128 * core - 4.0 * np.arange(64)[:, None] - 1.5)
        basis_z[core, 0:64] = full
        fold_z[core, :, 0:32] = full[32 * core : 32 * core + 32].T
        fold_z[core, :, 32:64] = full[32 * (1 - core) : 32 * (1 - core) + 32].T
    across = spline(np.arange(8.0)[None, :] - 4.0 * np.arange(-1, 3)[:, None] - 1.5)
    basis_y = np.broadcast_to(across[:, :, None], (4, 8, 128))
    fold_y = np.zeros((4, 8, 8, 8))
    for i in range(8):
        fold_y[:, i, i, :] = across
    return [
        jnp.asarray(np.ascontiguousarray(a), f32)
        for a in (basis_z, basis_y, fold_y.reshape(32, 64), fold_z)
    ]


def pairs(count, first):
    result = []
    for i in range(first, count - 1, 2):
        result += [(i, i + 1), (i + 1, i)]
    return result


def per_device(forward, adjoint, coefficients, kind):
    count_y = lax.axis_size("gy")
    count_x = lax.axis_size("gx")
    swap = [(0, 1), (1, 0)]
    side = lax.axis_index("gy")
    directions = 1 if count_y == 2 else 2
    tile = (8, 128)
    shape = jax.ShapeDtypeStruct
    basis_z, basis_y, fold_y, fold_z = bases()
    up = [(i, i + 1) for i in range(count_y - 1)]
    down = [(i + 1, i) for i in range(count_y - 1)]

    sent_z = kernel_call(
        pack_z,
        shape((4,) + tile, f32),
        [
            pltpu.VMEM((5,) + adjoint.shape[1:], bf16),
            pltpu.VMEM(coefficients.shape, f32),
            pltpu.SemaphoreType.DMA((6,)),
        ],
        in_specs=[pl.BlockSpec(memory_space=pltpu.HBM)] * 2,
    )(*(pltpu.with_memory_space_constraint(a, pltpu.HBM) for a in (adjoint, coefficients)))
    received_z = lax.ppermute(sent_z, "gz", swap)
    rows = kernel_call(
        functools.partial(gather_rows, directions),
        [shape((COARSE_ROWS, 128), f32)] * directions,
        [pltpu.VMEM((256, 128), f32)],
    )(adjoint)
    sent_y = kernel_call(
        functools.partial(pack_y, directions), [shape((STRIP, 128), bf16)] * directions
    )(sent_z, received_z, *rows)
    if directions == 1:
        received_y = [lax.ppermute(sent_y[0], "gy", swap)]
    else:
        received_y = [lax.ppermute(sent_y[0], "gy", up), lax.ppermute(sent_y[1], "gy", down)]

    pulled, flows, lines = kernel_call(
        pull_zy,
        [shape((19, 256, 128), f32), shape((5,) + kind.shape, f32), shape((16, 128), f32)],
        [pltpu.VMEM((2, 2) + tile, f32)],
    )(adjoint, forward, kind, sent_z, received_z, basis_z)

    bundle = shape((BUNDLE,) + tile, f32)
    pulled, sent_a, sent_b, edges, levels = kernel_call(
        functools.partial(pack_x, directions),
        [pulled, bundle, bundle, shape((2, 8) + tile, f32), shape((8,) + tile, f32)],
        [pltpu.VMEM((32, 128), f32)],
        aliases={0: 0},
    )(pulled, flows, lines, basis_z, basis_y, *received_y)
    received_b = lax.ppermute(sent_b, "gx", pairs(count_x, 1))
    received_a = lax.ppermute(sent_a, "gx", pairs(count_x, 0))

    prior, totals = kernel_call(
        collide_inside,
        [shape(adjoint.shape, bf16), shape((8,) + tile, f32)],
        [pltpu.VMEM((19, 24) + tile, bf16), pltpu.SemaphoreType.DMA((3,))],
        out_specs=[pl.BlockSpec(memory_space=pltpu.HBM), pl.BlockSpec(memory_space=pltpu.VMEM)],
    )(pulled, flows, kind, levels)
    gradient = kernel_call(project, shape((2, 4, 8, 32), f32))(
        pulled, flows, edges, levels, received_a, received_b, totals, fold_y, fold_z
    )

    whole = gradient[0] + lax.ppermute(gradient[1], "gz", swap)
    if directions == 1:
        other = lax.ppermute(jnp.where(side == 0, whole[3], whole[0]), "gy", swap)
        from_low = jnp.where(side == 1, other, 0.0)
        from_high = jnp.where(side == 0, other, 0.0)
    else:
        from_low = lax.ppermute(whole[3], "gy", up)
        from_high = lax.ppermute(whole[0], "gy", down)
    in_hbm = pl.BlockSpec(memory_space=pltpu.HBM)
    prior = kernel_call(
        collide_outside,
        shape(adjoint.shape, bf16),
        [pltpu.VMEM((19, 8) + tile, bf16), pltpu.SemaphoreType.DMA((2,))],
        aliases={6: 0},
        in_specs=[pl.BlockSpec(memory_space=pltpu.VMEM)] * 6 + [in_hbm],
        out_specs=in_hbm,
    )(pulled, flows, kind, levels, received_a, received_b, prior)
    return prior, jnp.stack([whole[1] + from_low, whole[2] + from_high], axis=1)


def solution(mesh):
    in_specs = (
        P(None, ("parts", "gx"), "gy", "gz"),
        P(None, ("parts", "gx"), "gy", "gz"),
        P(("parts", "gx"), "gy", "gz"),
        P(("parts", "gx"), "gy", "gz"),
    )
    out_specs = (P(None, ("parts", "gx"), "gy", "gz"), P(("parts", "gx"), "gy", "gz"))
    return jax.shard_map(
        per_device, mesh=mesh, in_specs=in_specs, out_specs=out_specs, check_vma=False
    )
```

time: 28.7 us -> 21.9 us (0.76)
  the two profiles are of different devices: /device:TPU:0 before, /device:TPU:16 now
where the time goes in v2:
time: 21.9 us; the launch traced here: 21.7 us
  waiting for transfers between devices  7.14 us (33%)
  starting transfers between devices  6.8 us (31%)
  Pallas kernels  6.34 us (29%)
  between operations  0.78 us (4%)
  local copies, waits for them, and re-layouts  0.65 us (3%)
    ppermute x1, waiting for transfers between devices, per_device(): received_b = lax.ppermute(sent_b, 'gx', pairs(count_x, 1))  2.72 us
    ppermute x1, starting transfers between devices, per_device(): received_b = lax.ppermute(sent_b, 'gx', pairs(count_x, 1))  1.91 us
    ppermute x1, starting transfers between devices, per_device(): received_a = lax.ppermute(sent_a, 'gx', pairs(count_x, 0))  1.64 us
    pallas_call x1, Pallas kernels, per_device(): kernel_call(collide_inside, [shape(adjoint.shape, bf16), shape((8,) + til...  1.6 us
    ppermute x1, starting transfers between devices, per_device(): received_y = [lax.ppermute(sent_y[0], 'gy', swap)]  1.56 us
    ppermute x1, starting transfers between devices, per_device(): other = lax.ppermute(jnp.where(side == 0, whole[3], whole[0]), 'gy', swap)  1.55 us
    pallas_call x1, Pallas kernels, per_device(): kernel_call(pull_zy, [shape((19, 256, 128), f32), shape((5,) + kind.shape...  1.48 us
    pallas_call x1, Pallas kernels, per_device(): kernel_call(pack_z, shape((4,) + tile, f32), [pltpu.VMEM((5,) + adjoint.s...  1.39 us
  transfers between devices with their start and end apart: 6, of which 5 were waited for; matrix products, arithmetic and copies ran while one was open for 0% of the time, Pallas kernels for 19%

profile of v2, /device:TPU:16, one launch (start us, length us, event | category | flops | bytes accessed | tf_op | source)
XLA Modules:
  0.0 21.7 jit_solution(162370454665032955)
XLA Ops:
  0.6 0.0 copy-start.3
  0.7 1.4 %shard_map.95.sent = f32[4,8,128]{2,1,0:T(8,128)S(1)} custom-call(bf16[19,32,8,128]{3,2,1,0:T(8,128)(2,1)} %adjoint.5, f32[8,2,32]{2,1,0:T(2,128)} %coefficients.1), custom_call_target="tpu_custom_call" | custom-call | tf_op jit(solution)/shard_map/pallas_call | solution.py:604
  2.1 0.1 collective-permute-start
  2.2 0.2 shard_map.97.refs_0_
  2.3 1.0 %collective-permute-done.received = f32[4,8,128]{2,1,0:T(8,128)S(1)} collective-permute-done((f32[4,8,128]{2,1,0:T(8,128)S(1)}, f32[4,8,128]{2,1,0:T(8,128)S(1)}, u32[]{:S(2)}, u32[]{:S(2)}) %collective-permute-start) | collective-permute-done | bytes 16416 | tf_op jit(solution)/shard_map/ppermute | solution.py:614
  3.3 0.1 shard_map.98
  3.4 1.6 %collective-permute-start.1 = (bf16[192,128]{1,0:T(8,128)(2,1)S(1)}, bf16[192,128]{1,0:T(8,128)(2,1)S(1)}, u32[]{:S(2)}, u32[]{:S(2)}) collective-permute-start(bf16[192,128]{1,0:T(8,128)(2,1)S(1)} %shard_map.98), channel_id=1, source_target_pairs={{0,2},{2,0},{1,3},{3,1},{4,6},{6,4},{5,7},{7,5},{8,10},{10,8},{9,1... | collective-permute-start | bytes 147464 | tf_op jit(solution)/shard_map/ppermute | solution.py:624
  5.0 1.5 %shard_map.96 = (f32[19,256,128]{2,1,0:T(8,128)S(1)}, f32[5,32,8,128]{3,2,1,0:T(8,128)S(1)}, f32[16,128]{1,0:T(8,128)S(1)}) custom-call(bf16[19,32,8,128]{3,2,1,0:T(8,128)(2,1)S(1)} %copy-done, bf16[19,32,8,128]{3,2,1,0:T(8,128)(2,1)S(1)} %copy-done.1, s32[32,8,128]{2,1,0:T(8,128)S(1)} %copy-done.2, f32[4,8,128]{2,1,0:T(8,128)S(1)} %shard_map.95.sent, ...), custom_call_target="tpu_custom_call" | custom-call | tf_op jit(solution)/shard_map/pallas_call | solution.py:628
  6.5 1.1 %collective-permute-done.1.refs_0_ = bf16[192,128]{1,0:T(8,128)(2,1)S(1)} collective-permute-done((bf16[192,128]{1,0:T(8,128)(2,1)S(1)}, bf16[192,128]{1,0:T(8,128)(2,1)S(1)}, u32[]{:S(2)}, u32[]{:S(2)}) %collective-permute-start.1) | collective-permute-done | bytes 49184 | tf_op jit(solution)/shard_map/ppermute | solution.py:624
  7.6 0.2 %shard_map.99 = (f32[19,256,128]{2,1,0:T(8,128)S(1)}, f32[19,8,128]{2,1,0:T(8,128)S(1)}, f32[19,8,128]{2,1,0:T(8,128)S(1)}, f32[2,8,8,128]{3,2,1,0:T(8,128)S(1)}, f32[8,8,128]{2,1,0:T(8,128)S(1)}) custom-call(f32[19,256,128]{2,1,0:T(8,128)S(1)} %get-tuple-element.12.unpatched, ...), custom_call_target="tpu_custom_call", output_to_operand_aliasing={{0}: (0, {})} | custom-call | tf_op jit(solution)/shard_map/pallas_call | solution.py:635
  7.8 1.6 %collective-permute-start.2 = (f32[19,8,128]{2,1,0:T(8,128)S(1)}, f32[19,8,128]{2,1,0:T(8,128)S(1)}, u32[]{:S(2)}, u32[]{:S(2)}) collective-permute-start(f32[19,8,128]{2,1,0:T(8,128)S(1)} %get-tuple-element.17), channel_id=1, source_target_pairs={{0,4},{4,0},{8,12},{12,8},{1,5},{5,1},{9,13},{13,9},{2,6},{6,2},{1... | collective-permute-start | bytes 233480 | tf_op jit(solution)/shard_map/ppermute | solution.py:642
  9.5 1.9 %collective-permute-start.3 = (f32[19,8,128]{2,1,0:T(8,128)S(1)}, f32[19,8,128]{2,1,0:T(8,128)S(1)}, u32[]{:S(2)}, u32[]{:S(2)}) collective-permute-start(f32[19,8,128]{2,1,0:T(8,128)S(1)} %get-tuple-element.18), channel_id=1, source_target_pairs={{4,8},{8,4},{5,9},{9,5},{6,10},{10,6},{7,11},{11,7},{20,24},{24,20... | collective-permute-start | bytes 233480 | tf_op jit(solution)/shard_map/ppermute | solution.py:641
  11.4 0.0 copy-start.4
  11.4 0.0 copy-start.5
  11.4 1.6 %shard_map.100 = (bf16[19,32,8,128]{3,2,1,0:T(8,128)(2,1)}, f32[8,8,128]{2,1,0:T(8,128)S(1)}) custom-call(f32[19,256,128]{2,1,0:T(8,128)S(1)} %get-tuple-element.15.pulled, f32[5,32,8,128]{3,2,1,0:T(8,128)S(1)} %get-tuple-element.13.flows, s32[32,8,128]{2,1,0:T(8,128)S(1)} %copy-done.2, f32[8,8,128]{2,1,0:T(8,128)S(1)} %get-tuple-element.16.levels), custom_call_target="tpu_custom_call" | custom-call | tf_op jit(solution)/shard_map/pallas_call | solution.py:644
  13.0 0.0 collective-permute-done.2.received_a
  13.0 2.7 %collective-permute-done.3.received_b = f32[19,8,128]{2,1,0:T(8,128)S(1)} collective-permute-done((f32[19,8,128]{2,1,0:T(8,128)S(1)}, f32[19,8,128]{2,1,0:T(8,128)S(1)}, u32[]{:S(2)}, u32[]{:S(2)}) %collective-permute-start.3) | collective-permute-done | bytes 77856 | tf_op jit(solution)/shard_map/ppermute | solution.py:641
  15.7 0.4 %shard_map.102 = f32[2,4,8,32]{3,2,1,0:T(8,128)S(1)} custom-call(f32[19,256,128]{2,1,0:T(8,128)S(1)} %get-tuple-element.15.pulled, f32[5,32,8,128]{3,2,1,0:T(8,128)S(1)} %get-tuple-element.13.flows, f32[2,8,8,128]{3,2,1,0:T(8,128)S(1)} %get-tuple-element.20.edges, f32[8,8,128]{2,1,0:T(8,128)S(1)} %get-tuple-element.16.levels, ...), custom_call_target="tpu_custom_call" | custom-call | tf_op jit(solution)/shard_map/pallas_call | solution.py:650
  16.2 0.1 collective-permute-start.4
  16.3 1.2 %collective-permute-done.4 = f32[4,8,32]{2,1,0:T(8,128)S(1)} collective-permute-done((f32[4,8,32]{2,1,0:T(8,128)S(1)}, f32[4,8,32]{2,1,0:T(8,128)S(1)}, u32[]{:S(2)}, u32[]{:S(2)}) %collective-permute-start.4) | collective-permute-done | bytes 4128 | tf_op jit(solution)/shard_map/ppermute | solution.py:654
  17.4 1.6 %collective-permute-start.5 = (f32[8,32]{1,0:T(8,128)S(1)}, f32[8,32]{1,0:T(8,128)S(1)}, u32[]{:S(2)}, u32[]{:S(2)}) collective-permute-start(f32[8,32]{1,0:T(8,128)S(1)} %fusion.3), channel_id=1, source_target_pairs={{0,2},{2,0},{1,3},{3,1},{4,6},{6,4},{5,7},{7,5},{8,10},{10,8},{9,1... | collective-permute-start | bytes 3080 | tf_op jit(solution)/shard_map/ppermute | solution.py:656
  19.0 1.0 %shard_map.101 = bf16[19,32,8,128]{3,2,1,0:T(8,128)(2,1)} custom-call(f32[19,256,128]{2,1,0:T(8,128)S(1)} %get-tuple-element.15.pulled, f32[5,32,8,128]{3,2,1,0:T(8,128)S(1)} %get-tuple-element.13.flows, s32[32,8,128]{2,1,0:T(8,128)S(1)} %copy-done.2, f32[8,8,128]{2,1,0:T(8,128)S(1)} %get-tuple-element.16.levels, ...), custom_call_target="tpu_custom_call", output_to_operand_aliasing={{}: (6, {})} | custom-call | tf_op jit(solution)/shard_map/pallas_call | solution.py:663
  20.0 1.1 %collective-permute-done.5 = f32[8,32]{1,0:T(8,128)S(1)} collective-permute-done((f32[8,32]{1,0:T(8,128)S(1)}, f32[8,32]{1,0:T(8,128)S(1)}, u32[]{:S(2)}, u32[]{:S(2)}) %collective-permute-start.5) | collective-permute-done | bytes 1056 | tf_op jit(solution)/shard_map/ppermute | solution.py:656
  21.1 0.6 %copy.12 = f32[8,2,32]{2,1,0:T(2,128)} copy(f32[8,2,32]{2,0,1:T(8,128)S(1)} %pad_maximum_fusion) | data formatting | bytes 4096
  (16 shorter events, 0.1 us)
Async XLA Ops:
  0.6 1.5 %copy-start = (bf16[19,32,8,128]{3,2,1,0:T(8,128)(2,1)S(1)}, bf16[19,32,8,128]{3,2,1,0:T(8,128)(2,1)}, u32[]{:S(2)}) copy-start(bf16[19,32,8,128]{3,2,1,0:T(8,128)(2,1)} %adjoint.5) | copy-start | bytes 3735556
  0.6 4.3 %copy-start.3 = (f32[2,128,128]{2,1,0:T(8,128)S(1)}, f32[2,128,128]{2,1,0:T(8,128)}, u32[]{:S(2)}) copy-start(f32[2,128,128]{2,1,0:T(8,128)} %constant.18.clone.basis_z) | copy-start | bytes 393220
  0.7 4.3 %copy-start.2 = (s32[32,8,128]{2,1,0:T(8,128)S(1)}, s32[32,8,128]{2,1,0:T(8,128)}, u32[]{:S(2)}) copy-start(s32[32,8,128]{2,1,0:T(8,128)} %kind.5) | copy-start | bytes 393220
  0.7 4.3 %copy-start.1 = (bf16[19,32,8,128]{3,2,1,0:T(8,128)(2,1)S(1)}, bf16[19,32,8,128]{3,2,1,0:T(8,128)(2,1)}, u32[]{:S(2)}) copy-start(bf16[19,32,8,128]{3,2,1,0:T(8,128)(2,1)} %forward.1) | copy-start | bytes 3735556
  2.1 1.2 %collective-permute-start = (f32[4,8,128]{2,1,0:T(8,128)S(1)}, f32[4,8,128]{2,1,0:T(8,128)S(1)}, u32[]{:S(2)}, u32[]{:S(2)}) collective-permute-start(f32[4,8,128]{2,1,0:T(8,128)S(1)} %shard_map.95.sent), channel_id=1, source_target_pairs={{0,1},{1,0},{2,3},{3,2},{4,5},{5,4},{6,7},{7,6},{8,9},{9,8},{10,11... | collective-permute-start | bytes 49160 | tf_op jit(solution)/shard_map/ppermute | solution.py:614
  3.4 4.2 %copy-start.6 = (f32[4,8,128]{2,1,0:T(8,128)S(1)}, f32[4,8,128]{2,1,0:T(8,128)}, u32[]{:S(2)}) copy-start(f32[4,8,128]{2,1,0:T(8,128)} %constant.19.clone.basis_y) | copy-start | bytes 49156
  3.4 4.2 %collective-permute-start.1 = (bf16[192,128]{1,0:T(8,128)(2,1)S(1)}, bf16[192,128]{1,0:T(8,128)(2,1)S(1)}, u32[]{:S(2)}, u32[]{:S(2)}) collective-permute-start(bf16[192,128]{1,0:T(8,128)(2,1)S(1)} %shard_map.98), channel_id=1, source_target_pairs={{0,2},{2,0},{1,3},{3,1},{4,6},{6,4},{5,7},{7,5},{8,10},{10,8},{9,1... | collective-permute-start | bytes 147464 | tf_op jit(solution)/shard_map/ppermute | solution.py:624
  7.8 5.2 %collective-permute-start.2 = (f32[19,8,128]{2,1,0:T(8,128)S(1)}, f32[19,8,128]{2,1,0:T(8,128)S(1)}, u32[]{:S(2)}, u32[]{:S(2)}) collective-permute-start(f32[19,8,128]{2,1,0:T(8,128)S(1)} %get-tuple-element.17), channel_id=1, source_target_pairs={{0,4},{4,0},{8,12},{12,8},{1,5},{5,1},{9,13},{13,9},{2,6},{6,2},{1... | collective-permute-start | bytes 233480 | tf_op jit(solution)/shard_map/ppermute | solution.py:642
  9.5 6.3 %collective-permute-start.3 = (f32[19,8,128]{2,1,0:T(8,128)S(1)}, f32[19,8,128]{2,1,0:T(8,128)S(1)}, u32[]{:S(2)}, u32[]{:S(2)}) collective-permute-start(f32[19,8,128]{2,1,0:T(8,128)S(1)} %get-tuple-element.18), channel_id=1, source_target_pairs={{4,8},{8,4},{5,9},{9,5},{6,10},{10,6},{7,11},{11,7},{20,24},{24,20... | collective-permute-start | bytes 233480 | tf_op jit(solution)/shard_map/ppermute | solution.py:641
  11.4 4.4 %copy-start.4 = (f32[2,128,64]{2,1,0:T(8,128)S(1)}, f32[2,128,64]{2,1,0:T(8,128)}, u32[]{:S(2)}) copy-start(f32[2,128,64]{2,1,0:T(8,128)} %constant.21.clone.fold_z) | copy-start | bytes 196612
  11.4 4.4 %copy-start.5 = (f32[32,64]{1,0:T(8,128)S(1)}, f32[32,64]{1,0:T(8,128)}, u32[]{:S(2)}) copy-start(f32[32,64]{1,0:T(8,128)} %constant.20.clone.fold_y) | copy-start | bytes 24580
  16.2 1.2 %collective-permute-start.4 = (f32[4,8,32]{2,1,0:T(8,128)S(1)}, f32[4,8,32]{2,1,0:T(8,128)S(1)}, u32[]{:S(2)}, u32[]{:S(2)}) collective-permute-start(f32[4,8,32]{2,1,0:T(8,128)S(1)} %slice_bitcast_fusion), channel_id=1, source_target_pairs={{0,1},{1,0},{2,3},{3,2},{4,5},{5,4},{6,7},{7,6},{8,9},{9,8},{10,11... | collective-permute-start | bytes 12296 | tf_op jit(solution)/shard_map/ppermute | solution.py:654
  17.4 3.7 %collective-permute-start.5 = (f32[8,32]{1,0:T(8,128)S(1)}, f32[8,32]{1,0:T(8,128)S(1)}, u32[]{:S(2)}, u32[]{:S(2)}) collective-permute-start(f32[8,32]{1,0:T(8,128)S(1)} %fusion.3), channel_id=1, source_target_pairs={{0,2},{2,0},{1,3},{3,1},{4,6},{6,4},{5,7},{7,5},{8,10},{10,8},{9,1... | collective-permute-start | bytes 3080 | tf_op jit(solution)/shard_map/ppermute | solution.py:656

commit v3 on v2

--- a/solution.py
+++ b/solution.py
@@ -467,13 +467,15 @@
 
 
 def along_x(received_a, received_b):
-    even = lax.rem(lax.axis_index("gx"), 2) == 0
+    place = lax.axis_index("gx")
+    even = lax.rem(place, 2) == 0
+    has_low, has_high = place > 0, place < lax.axis_size("gx") - 1
 
     def low(slot):
-        return jnp.where(even, received_b[slot], received_a[slot])
+        return jnp.where(has_low, jnp.where(even, received_b[slot], received_a[slot]), 0.0)
 
     def high(slot):
-        return jnp.where(even, received_a[slot], received_b[slot])
+        return jnp.where(has_high, jnp.where(even, received_a[slot], received_b[slot]), 0.0)
 
     return low, high
 
@@ -583,9 +585,14 @@
 
 
 def pairs(count, first):
+    partner = {}
+    for i in range(first, count - 1, 2):
+        partner[i], partner[i + 1] = i + 1, i
     result = []
-    for i in range(first, count - 1, 2):
-        result += [(i, i + 1), (i + 1, i)]
+    for i in range(count):
+        for core in range(2):
+            target = (partner[i], core) if i in partner else (i, 1 - core)
+            result.append((i * 2 + core, target[0] * 2 + target[1]))
     return result
 
 
@@ -638,8 +645,8 @@
         [pltpu.VMEM((32, 128), f32)],
         aliases={0: 0},
     )(pulled, flows, lines, basis_z, basis_y, *received_y)
-    received_b = lax.ppermute(sent_b, "gx", pairs(count_x, 1))
-    received_a = lax.ppermute(sent_a, "gx", pairs(count_x, 0))
+    received_b = lax.ppermute(sent_b, ("gx", "gz"), pairs(count_x, 1))
+    received_a = lax.ppermute(sent_a, ("gx", "gz"), pairs(count_x, 0))
 
     prior, totals = kernel_call(
         collide_inside,

time: 21.9 us -> 20 us (0.913)
  starting transfers between devices: 6.8 us -> 4.89 us
    ppermute x2, starting transfers between devices: 3.55 us -> 1.64 us  [the longest x1 1.64 us: per_device(): received_a = lax.ppermute(sent_a, ('gx', 'gz'), pairs(count_x, 0))]
  transfers between devices with their start and end apart: 6 -> 6, of which waited for: 5 -> 6; matrix products, arithmetic and copies ran while one was open for 0% -> 0% of each run, Pallas kernels for 19% -> 21%
where the time goes in v3:
time: 20 us; the launch traced here: 19.9 us
  waiting for transfers between devices  7.2 us (36%)
  Pallas kernels  6.34 us (32%)
  starting transfers between devices  4.89 us (24%)
  between operations  0.75 us (4%)
  local copies, waits for them, and re-layouts  0.64 us (3%)
    ppermute x1, starting transfers between devices, per_device(): received_a = lax.ppermute(sent_a, ('gx', 'gz'), pairs(count_x, 0))  1.64 us
    pallas_call x1, Pallas kernels, per_device(): kernel_call(collide_inside, [shape(adjoint.shape, bf16), shape((8,) + til...  1.59 us
    ppermute x1, waiting for transfers between devices, per_device(): received_b = lax.ppermute(sent_b, ('gx', 'gz'), pairs(count_x, 1))  1.58 us
    ppermute x1, starting transfers between devices, per_device(): received_y = [lax.ppermute(sent_y[0], 'gy', swap)]  1.56 us
    ppermute x1, starting transfers between devices, per_device(): other = lax.ppermute(jnp.where(side == 0, whole[3], whole[0]), 'gy', swap)  1.55 us
    pallas_call x1, Pallas kernels, per_device(): kernel_call(pull_zy, [shape((19, 256, 128), f32), shape((5,) + kind.shape...  1.48 us
    pallas_call x1, Pallas kernels, per_device(): kernel_call(pack_z, shape((4,) + tile, f32), [pltpu.VMEM((5,) + adjoint.s...  1.39 us
    ppermute x1, waiting for transfers between devices, per_device(): received_a = lax.ppermute(sent_a, ('gx', 'gz'), pairs(count_x, 0))  1.21 us
  transfers between devices with their start and end apart: 6, of which 6 were waited for; matrix products, arithmetic and copies ran while one was open for 0% of the time, Pallas kernels for 21%

profile of v3, /device:TPU:16, one launch (start us, length us, event | category | flops | bytes accessed | tf_op | source)
XLA Modules:
  0.0 19.9 jit_solution(5838733136959031734)
XLA Ops:
  0.6 0.0 copy-start.3
  0.7 1.4 %shard_map.95.sent = f32[4,8,128]{2,1,0:T(8,128)S(1)} custom-call(bf16[19,32,8,128]{3,2,1,0:T(8,128)(2,1)} %adjoint.5, f32[8,2,32]{2,1,0:T(2,128)} %coefficients.1), custom_call_target="tpu_custom_call" | custom-call | tf_op jit(solution)/shard_map/pallas_call | solution.py:611
  2.1 0.1 collective-permute-start
  2.2 0.2 shard_map.97.refs_0_
  2.3 1.0 %collective-permute-done.received = f32[4,8,128]{2,1,0:T(8,128)S(1)} collective-permute-done((f32[4,8,128]{2,1,0:T(8,128)S(1)}, f32[4,8,128]{2,1,0:T(8,128)S(1)}, u32[]{:S(2)}, u32[]{:S(2)}) %collective-permute-start) | collective-permute-done | bytes 16416 | tf_op jit(solution)/shard_map/ppermute | solution.py:621
  3.3 0.1 shard_map.98
  3.4 1.6 %collective-permute-start.1 = (bf16[192,128]{1,0:T(8,128)(2,1)S(1)}, bf16[192,128]{1,0:T(8,128)(2,1)S(1)}, u32[]{:S(2)}, u32[]{:S(2)}) collective-permute-start(bf16[192,128]{1,0:T(8,128)(2,1)S(1)} %shard_map.98), channel_id=1, source_target_pairs={{0,2},{2,0},{1,3},{3,1},{4,6},{6,4},{5,7},{7,5},{8,10},{10,8},{9,1... | collective-permute-start | bytes 147464 | tf_op jit(solution)/shard_map/ppermute | solution.py:631
  5.0 0.0 copy-done.3
  5.0 1.5 %shard_map.96 = (f32[19,256,128]{2,1,0:T(8,128)S(1)}, f32[5,32,8,128]{3,2,1,0:T(8,128)S(1)}, f32[16,128]{1,0:T(8,128)S(1)}) custom-call(bf16[19,32,8,128]{3,2,1,0:T(8,128)(2,1)S(1)} %copy-done, bf16[19,32,8,128]{3,2,1,0:T(8,128)(2,1)S(1)} %copy-done.1, s32[32,8,128]{2,1,0:T(8,128)S(1)} %copy-done.2, f32[4,8,128]{2,1,0:T(8,128)S(1)} %shard_map.95.sent, ...), custom_call_target="tpu_custom_call" | custom-call | tf_op jit(solution)/shard_map/pallas_call | solution.py:635
  6.5 1.1 %collective-permute-done.1.refs_0_ = bf16[192,128]{1,0:T(8,128)(2,1)S(1)} collective-permute-done((bf16[192,128]{1,0:T(8,128)(2,1)S(1)}, bf16[192,128]{1,0:T(8,128)(2,1)S(1)}, u32[]{:S(2)}, u32[]{:S(2)}) %collective-permute-start.1) | collective-permute-done | bytes 49184 | tf_op jit(solution)/shard_map/ppermute | solution.py:631
  7.6 0.2 %shard_map.99 = (f32[19,256,128]{2,1,0:T(8,128)S(1)}, f32[19,8,128]{2,1,0:T(8,128)S(1)}, f32[19,8,128]{2,1,0:T(8,128)S(1)}, f32[2,8,8,128]{3,2,1,0:T(8,128)S(1)}, f32[8,8,128]{2,1,0:T(8,128)S(1)}) custom-call(f32[19,256,128]{2,1,0:T(8,128)S(1)} %get-tuple-element.12.unpatched, ...), custom_call_target="tpu_custom_call", output_to_operand_aliasing={{0}: (0, {})} | custom-call | tf_op jit(solution)/shard_map/pallas_call | solution.py:642
  7.8 1.6 %collective-permute-start.2 = (f32[19,8,128]{2,1,0:T(8,128)S(1)}, f32[19,8,128]{2,1,0:T(8,128)S(1)}, u32[]{:S(2)}, u32[]{:S(2)}) collective-permute-start(f32[19,8,128]{2,1,0:T(8,128)S(1)} %get-tuple-element.17), channel_id=1, source_target_pairs={{0,4},{1,5},{4,0},{5,1},{8,12},{9,13},{12,8},{13,9},{2,6},{3,7},{6... | collective-permute-start | bytes 233480 | tf_op jit(solution)/shard_map/ppermute | solution.py:649
  9.5 0.0 collective-permute-start.3
  9.5 1.6 %shard_map.100 = (bf16[19,32,8,128]{3,2,1,0:T(8,128)(2,1)}, f32[8,8,128]{2,1,0:T(8,128)S(1)}) custom-call(f32[19,256,128]{2,1,0:T(8,128)S(1)} %get-tuple-element.15.pulled, f32[5,32,8,128]{3,2,1,0:T(8,128)S(1)} %get-tuple-element.13.flows, s32[32,8,128]{2,1,0:T(8,128)S(1)} %copy-done.2, f32[8,8,128]{2,1,0:T(8,128)S(1)} %get-tuple-element.16.levels), custom_call_target="tpu_custom_call" | custom-call | tf_op jit(solution)/shard_map/pallas_call | solution.py:651
  11.1 1.2 %collective-permute-done.2.received_a = f32[19,8,128]{2,1,0:T(8,128)S(1)} collective-permute-done((f32[19,8,128]{2,1,0:T(8,128)S(1)}, f32[19,8,128]{2,1,0:T(8,128)S(1)}, u32[]{:S(2)}, u32[]{:S(2)}) %collective-permute-start.2) | collective-permute-done | bytes 77856 | tf_op jit(solution)/shard_map/ppermute | solution.py:649
  12.3 1.6 %collective-permute-done.3.received_b = f32[19,8,128]{2,1,0:T(8,128)S(1)} collective-permute-done((f32[19,8,128]{2,1,0:T(8,128)S(1)}, f32[19,8,128]{2,1,0:T(8,128)S(1)}, u32[]{:S(2)}, u32[]{:S(2)}) %collective-permute-start.3) | collective-permute-done | bytes 77856 | tf_op jit(solution)/shard_map/ppermute | solution.py:648
  13.8 0.0 copy-done.4
  13.9 0.4 %shard_map.102 = f32[2,4,8,32]{3,2,1,0:T(8,128)S(1)} custom-call(f32[19,256,128]{2,1,0:T(8,128)S(1)} %get-tuple-element.15.pulled, f32[5,32,8,128]{3,2,1,0:T(8,128)S(1)} %get-tuple-element.13.flows, f32[2,8,8,128]{3,2,1,0:T(8,128)S(1)} %get-tuple-element.20.edges, f32[8,8,128]{2,1,0:T(8,128)S(1)} %get-tuple-element.16.levels, ...), custom_call_target="tpu_custom_call" | custom-call | tf_op jit(solution)/shard_map/pallas_call | solution.py:657
  14.3 0.1 collective-permute-start.4
  14.4 1.2 %collective-permute-done.4 = f32[4,8,32]{2,1,0:T(8,128)S(1)} collective-permute-done((f32[4,8,32]{2,1,0:T(8,128)S(1)}, f32[4,8,32]{2,1,0:T(8,128)S(1)}, u32[]{:S(2)}, u32[]{:S(2)}) %collective-permute-start.4) | collective-permute-done | bytes 4128 | tf_op jit(solution)/shard_map/ppermute | solution.py:661
  15.6 1.6 %collective-permute-start.5 = (f32[8,32]{1,0:T(8,128)S(1)}, f32[8,32]{1,0:T(8,128)S(1)}, u32[]{:S(2)}, u32[]{:S(2)}) collective-permute-start(f32[8,32]{1,0:T(8,128)S(1)} %fusion.3), channel_id=1, source_target_pairs={{0,2},{2,0},{1,3},{3,1},{4,6},{6,4},{5,7},{7,5},{8,10},{10,8},{9,1... | collective-permute-start | bytes 3080 | tf_op jit(solution)/shard_map/ppermute | solution.py:663
  17.1 1.0 %shard_map.101 = bf16[19,32,8,128]{3,2,1,0:T(8,128)(2,1)} custom-call(f32[19,256,128]{2,1,0:T(8,128)S(1)} %get-tuple-element.15.pulled, f32[5,32,8,128]{3,2,1,0:T(8,128)S(1)} %get-tuple-element.13.flows, s32[32,8,128]{2,1,0:T(8,128)S(1)} %copy-done.2, f32[8,8,128]{2,1,0:T(8,128)S(1)} %get-tuple-element.16.levels, ...), custom_call_target="tpu_custom_call", output_to_operand_aliasing={{}: (6, {})} | custom-call | tf_op jit(solution)/shard_map/pallas_call | solution.py:670
  18.1 1.1 %collective-permute-done.5 = f32[8,32]{1,0:T(8,128)S(1)} collective-permute-done((f32[8,32]{1,0:T(8,128)S(1)}, f32[8,32]{1,0:T(8,128)S(1)}, u32[]{:S(2)}, u32[]{:S(2)}) %collective-permute-start.5) | collective-permute-done | bytes 1056 | tf_op jit(solution)/shard_map/ppermute | solution.py:663
  19.2 0.6 %copy.12 = f32[8,2,32]{2,1,0:T(2,128)} copy(f32[8,2,32]{2,0,1:T(8,128)S(1)} %pad_maximum_fusion) | data formatting | bytes 4096
  (16 shorter events, 0.1 us)
Async XLA Ops:
  0.6 1.5 %copy-start = (bf16[19,32,8,128]{3,2,1,0:T(8,128)(2,1)S(1)}, bf16[19,32,8,128]{3,2,1,0:T(8,128)(2,1)}, u32[]{:S(2)}) copy-start(bf16[19,32,8,128]{3,2,1,0:T(8,128)(2,1)} %adjoint.5) | copy-start | bytes 3735556
  0.6 4.3 %copy-start.3 = (f32[2,128,128]{2,1,0:T(8,128)S(1)}, f32[2,128,128]{2,1,0:T(8,128)}, u32[]{:S(2)}) copy-start(f32[2,128,128]{2,1,0:T(8,128)} %constant.18.clone.basis_z) | copy-start | bytes 393220
  0.7 4.3 %copy-start.2 = (s32[32,8,128]{2,1,0:T(8,128)S(1)}, s32[32,8,128]{2,1,0:T(8,128)}, u32[]{:S(2)}) copy-start(s32[32,8,128]{2,1,0:T(8,128)} %kind.5) | copy-start | bytes 393220
  0.7 4.3 %copy-start.1 = (bf16[19,32,8,128]{3,2,1,0:T(8,128)(2,1)S(1)}, bf16[19,32,8,128]{3,2,1,0:T(8,128)(2,1)}, u32[]{:S(2)}) copy-start(bf16[19,32,8,128]{3,2,1,0:T(8,128)(2,1)} %forward.1) | copy-start | bytes 3735556
  2.1 1.2 %collective-permute-start = (f32[4,8,128]{2,1,0:T(8,128)S(1)}, f32[4,8,128]{2,1,0:T(8,128)S(1)}, u32[]{:S(2)}, u32[]{:S(2)}) collective-permute-start(f32[4,8,128]{2,1,0:T(8,128)S(1)} %shard_map.95.sent), channel_id=1, source_target_pairs={{0,1},{1,0},{2,3},{3,2},{4,5},{5,4},{6,7},{7,6},{8,9},{9,8},{10,11... | collective-permute-start | bytes 49160 | tf_op jit(solution)/shard_map/ppermute | solution.py:621
  3.4 4.2 %copy-start.6 = (f32[4,8,128]{2,1,0:T(8,128)S(1)}, f32[4,8,128]{2,1,0:T(8,128)}, u32[]{:S(2)}) copy-start(f32[4,8,128]{2,1,0:T(8,128)} %constant.19.clone.basis_y) | copy-start | bytes 49156
  3.4 4.2 %collective-permute-start.1 = (bf16[192,128]{1,0:T(8,128)(2,1)S(1)}, bf16[192,128]{1,0:T(8,128)(2,1)S(1)}, u32[]{:S(2)}, u32[]{:S(2)}) collective-permute-start(bf16[192,128]{1,0:T(8,128)(2,1)S(1)} %shard_map.98), channel_id=1, source_target_pairs={{0,2},{2,0},{1,3},{3,1},{4,6},{6,4},{5,7},{7,5},{8,10},{10,8},{9,1... | collective-permute-start | bytes 147464 | tf_op jit(solution)/shard_map/ppermute | solution.py:631
  7.8 4.5 %collective-permute-start.2 = (f32[19,8,128]{2,1,0:T(8,128)S(1)}, f32[19,8,128]{2,1,0:T(8,128)S(1)}, u32[]{:S(2)}, u32[]{:S(2)}) collective-permute-start(f32[19,8,128]{2,1,0:T(8,128)S(1)} %get-tuple-element.17), channel_id=1, source_target_pairs={{0,4},{1,5},{4,0},{5,1},{8,12},{9,13},{12,8},{13,9},{2,6},{3,7},{6... | collective-permute-start | bytes 233480 | tf_op jit(solution)/shard_map/ppermute | solution.py:649
  9.5 4.4 %collective-permute-start.3 = (f32[19,8,128]{2,1,0:T(8,128)S(1)}, f32[19,8,128]{2,1,0:T(8,128)S(1)}, u32[]{:S(2)}, u32[]{:S(2)}) collective-permute-start(f32[19,8,128]{2,1,0:T(8,128)S(1)} %get-tuple-element.18), channel_id=1, source_target_pairs={{0,1},{1,0},{4,8},{5,9},{8,4},{9,5},{12,13},{13,12},{2,3},{3,2},{6... | collective-permute-start | bytes 233480 | tf_op jit(solution)/shard_map/ppermute | solution.py:648
  9.5 4.4 %copy-start.4 = (f32[2,128,64]{2,1,0:T(8,128)S(1)}, f32[2,128,64]{2,1,0:T(8,128)}, u32[]{:S(2)}) copy-start(f32[2,128,64]{2,1,0:T(8,128)} %constant.21.clone.fold_z) | copy-start | bytes 196612
  9.5 4.4 %copy-start.5 = (f32[32,64]{1,0:T(8,128)S(1)}, f32[32,64]{1,0:T(8,128)}, u32[]{:S(2)}) copy-start(f32[32,64]{1,0:T(8,128)} %constant.20.clone.fold_y) | copy-start | bytes 24580
  14.3 1.2 %collective-permute-start.4 = (f32[4,8,32]{2,1,0:T(8,128)S(1)}, f32[4,8,32]{2,1,0:T(8,128)S(1)}, u32[]{:S(2)}, u32[]{:S(2)}) collective-permute-start(f32[4,8,32]{2,1,0:T(8,128)S(1)} %slice_bitcast_fusion), channel_id=1, source_target_pairs={{0,1},{1,0},{2,3},{3,2},{4,5},{5,4},{6,7},{7,6},{8,9},{9,8},{10,11... | collective-permute-start | bytes 12296 | tf_op jit(solution)/shard_map/ppermute | solution.py:661
  15.6 3.7 %collective-permute-start.5 = (f32[8,32]{1,0:T(8,128)S(1)}, f32[8,32]{1,0:T(8,128)S(1)}, u32[]{:S(2)}, u32[]{:S(2)}) collective-permute-start(f32[8,32]{1,0:T(8,128)S(1)} %fusion.3), channel_id=1, source_target_pairs={{0,2},{2,0},{1,3},{3,1},{4,6},{6,4},{5,7},{7,5},{8,10},{10,8},{9,1... | collective-permute-start | bytes 3080 | tf_op jit(solution)/shard_map/ppermute | solution.py:663

commit v4 on v3

--- a/solution.py
+++ b/solution.py
@@ -43,8 +43,9 @@
 YP, YM = going(1, 1), going(1, -1)
 ZP, ZM = going(2, 1), going(2, -1)
 
-FACE, ALPHA, BETA, FIELD, LEVEL, BUNDLE = 0, 5, 9, 13, 17, 19
-COARSE_ROWS, STRIP = 160, 192
+FACE, NEAR, FAR, FIELD, LEVEL, BUNDLE = 0, 5, 9, 15, 19, 23
+SLOTS = 3
+COARSE_ROWS, STRIP = 160, 176
 MASS, INVERSE = 3, 4
 EDGE_PLANES = (0, 1, 2, 3, 28, 29, 30, 31)
 
@@ -275,11 +276,9 @@
             out[k * 32 : k * 32 + 32, :] = rows.astype(bf16)
         coarse = sent[coarse_row] + received[coarse_row]
         high = coarse.astype(bf16)
-        rest = coarse - high.astype(f32)
-        middle = rest.astype(bf16)
-        low = (rest - middle.astype(f32)).astype(bf16)
-        out[COARSE_ROWS : COARSE_ROWS + 16, :] = jnp.concatenate([high, middle], axis=0)
-        out[COARSE_ROWS + 16 : STRIP, :] = jnp.concatenate([low, jnp.zeros((8, 128), bf16)], axis=0)
+        out[COARSE_ROWS:STRIP, :] = jnp.concatenate(
+            [high, (coarse - high.astype(f32)).astype(bf16)], axis=0
+        )
 
     sides = y_sides(directions)
     if directions == 1:
@@ -291,7 +290,17 @@
             emit(*sides[n], 3 - n, sources[n], outs[n])
 
 
-def pull_zy(adjoint, forward, kind, sent, received, basis_z, pulled, flows, lines, columns):
+def pull_zy(
+    adjoint, forward_far, kind, sent, received, basis_z, pulled, flows, lines, columns, forward, semaphores
+):
+    copies = [
+        pltpu.make_async_copy(
+            forward_far.at[:, pl.ds(8 * n, 8)], forward.at[:, pl.ds(8 * n, 8)], semaphores.at[n]
+        )
+        for n in range(4)
+    ]
+    for copy in copies:
+        copy.start()
     core = lax.axis_index("gz")
     load_columns(core, received, columns)
     sublanes = iota(0)
@@ -307,6 +316,9 @@
             elif step_y < 0:
                 tile = jnp.where(sublanes == 0, 0.0, pltpu.roll(tile, 1, 0))
             pulled[q, rows_of(x), :] = tile
+        return carry
+
+    def flow(x, carry):
         rho, mass = flow_moments([forward[q, x].astype(f32) for q in range(19)])
         inverse = 1.0 / rho
         for n in range(3):
@@ -316,15 +328,18 @@
         return carry
 
     lax.fori_loop(0, 32, step, 0, unroll=4)
+    for n, copy in enumerate(copies):
+        copy.wait()
+        lax.fori_loop(8 * n, 8 * n + 8, flow, 0, unroll=4)
 
 
 def pack_x(directions, unpatched, flows, lines, basis_z, basis_y, *refs):
     received = refs[:directions]
-    pulled, out_a, out_b, edges, levels, extra = refs[directions:]
+    pulled, *outs, edges, levels, extra = refs[directions:]
     del unpatched
     core = lax.axis_index("gz")
     side = lax.axis_index("gy")
-    even = lax.rem(lax.axis_index("gx"), 2) == 0
+    place = lax.rem(lax.axis_index("gx"), SLOTS)
 
     def patch(components, row, strip):
         for k, q in enumerate(components):
@@ -332,7 +347,7 @@
 
     def outer_line(strip):
         parts = strip[COARSE_ROWS:STRIP, :].astype(f32)
-        coarse = parts[0:8] + parts[8:16] + parts[16:24]
+        coarse = parts[0:8] + parts[8:16]
         return jnp.dot(coarse, basis_z[core], precision=highest, preferred_element_type=f32)
 
     if directions == 1:
@@ -354,15 +369,19 @@
         levels[i] = level
 
     def put(slot, low, high):
-        out_a[slot] = jnp.where(even, high, low)
-        out_b[slot] = jnp.where(even, low, high)
+        for n, out in enumerate(outs):
+            out[slot] = jnp.where(place == n, high, low).astype(bf16)
+
+    def put_split(slot, low, high):
+        put(slot, low, high)
+        put(slot + 2, low - low.astype(bf16).astype(f32), high - high.astype(bf16).astype(f32))
 
     for k in range(5):
         put(FACE + k, pulled[XP[k], rows_of(0), :], pulled[XM[k], rows_of(31), :])
     for n in range(4):
         put(FIELD + n, flows[n, 0], flows[n, 31])
     for n in range(2):
-        put(LEVEL + n, levels[n], levels[6 + n])
+        put_split(LEVEL + n, levels[n], levels[7 - n])
     results = []
     for x in EDGE_PLANES:
         values = {}
@@ -372,12 +391,15 @@
                 values[q] = pulled[q, rows_of(target), :]
         flow = tuple(flows[n, x] for n in range(3))
         results.append(alpha_beta(pair_moments(values), flow, flows[MASS, x]))
-    for position in range(4):
-        for n, slot in enumerate((ALPHA, BETA)):
-            low, high = results[position][n], results[4 + position][n]
-            edges[n, position] = low
-            edges[n, 4 + position] = high
-            put(slot + position, low, high)
+    for away in range(4):
+        for n in range(2):
+            low, high = results[away][n], results[7 - away][n]
+            edges[n, away] = low
+            edges[n, 7 - away] = high
+            if away == 0:
+                put_split(NEAR + n, low, high)
+            else:
+                put(FAR + 2 * (away - 1) + n, low, high)
 
 
 def slope_of(bent):
@@ -466,26 +488,40 @@
         copy.wait()
 
 
-def along_x(received_a, received_b):
+def along_x(received):
     place = lax.axis_index("gx")
-    even = lax.rem(place, 2) == 0
     has_low, has_high = place > 0, place < lax.axis_size("gx") - 1
-
-    def low(slot):
-        return jnp.where(has_low, jnp.where(even, received_b[slot], received_a[slot]), 0.0)
-
-    def high(slot):
-        return jnp.where(has_high, jnp.where(even, received_a[slot], received_b[slot]), 0.0)
-
-    return low, high
-
-
-def project(pulled, flows, edges, levels, received_a, received_b, inner, fold_y, fold_z, gradient):
+    turn = lax.rem(place, SLOTS)
+
+    def reader(present, first):
+        def read(slot):
+            value = received[first][slot].astype(f32)
+            for n in range(1, SLOTS):
+                value = jnp.where(turn == n, received[(n + first) % SLOTS][slot].astype(f32), value)
+            return jnp.where(present, value, 0.0)
+
+        return read
+
+    return reader(has_low, SLOTS - 1), reader(has_high, 0)
+
+
+def levels_along_x(read):
+    return [read(LEVEL + n) + read(LEVEL + 2 + n) for n in range(2)]
+
+
+def in_parts(values, axis):
+    high = values.astype(bf16)
+    low = (values - high.astype(f32)).astype(bf16)
+    return jnp.concatenate([high, high, low] if axis == 0 else [high, low, high], axis=axis)
+
+
+def project(pulled, flows, edges, levels, *refs):
+    inner, fold_y, fold_z, gradient = refs[SLOTS:]
     core = lax.axis_index("gz")
-    low, high = along_x(received_a, received_b)
+    low, high = along_x(refs[:SLOTS])
     totals = [inner[i] for i in range(8)]
-    lower = [low(LEVEL), low(LEVEL + 1)] + [levels[i] for i in range(3)]
-    upper = [levels[i] for i in range(5, 8)] + [high(LEVEL), high(LEVEL + 1)]
+    lower = levels_along_x(low)[::-1] + [levels[i] for i in range(3)]
+    upper = [levels[i] for i in range(5, 8)] + levels_along_x(high)
 
     def add(block, position, alpha, beta):
         start = block + 1 if block < 4 else block - 6
@@ -517,23 +553,26 @@
                 index = position + (4 if block else 0)
                 alpha, beta = edges[0, index], edges[1, index]
             else:
-                ref = low if block < 0 else high
-                alpha, beta = ref(ALPHA + position), ref(BETA + position)
+                ref, away = (low, 3 - position) if block < 0 else (high, position)
+                alpha, beta = (
+                    ref(NEAR + n) + ref(NEAR + 2 + n) if away == 0 else ref(FAR + 2 * (away - 1) + n)
+                    for n in range(2)
+                )
             if (block, position) in missing:
                 more = missing[block, position]
                 alpha, beta = alpha + more[0], beta + more[1]
             add(block, position, alpha, beta)
     stacked = jnp.concatenate(totals, axis=0)
-    folded = jnp.dot(fold_y[...], stacked, precision=highest, preferred_element_type=f32)
-    result = jnp.dot(folded, fold_z[core], precision=highest, preferred_element_type=f32)
+    folded = jnp.dot(fold_y[...], in_parts(stacked, 0), preferred_element_type=f32)
+    result = jnp.dot(in_parts(folded, 1), fold_z[core], preferred_element_type=f32)
     for part in range(2):
         for j in range(4):
             gradient[part, j] = result[j * 8 : j * 8 + 8, part * 32 : part * 32 + 32]
 
 
-def collide_outside(pulled, flows, kind, levels, received_a, received_b, inner, out, stage, semaphores):
-    del inner
-    low, high = along_x(received_a, received_b)
+def collide_outside(pulled, flows, kind, levels, *refs):
+    out, stage, semaphores = refs[SLOTS + 1 :]
+    low, high = along_x(refs[:SLOTS])
     copies = []
     for part, planes in enumerate((EDGE_PLANES[:4], EDGE_PLANES[4:])):
         for slot, x in enumerate(planes):
@@ -547,7 +586,9 @@
                 else:
                     values[q] = pulled[q, rows_of(target), :]
             around = (
-                [levels[6], levels[7], high(LEVEL)] if part else [low(LEVEL + 1), levels[0], levels[1]]
+                [levels[6], levels[7], levels_along_x(high)[0]]
+                if part
+                else [levels_along_x(low)[0], levels[0], levels[1]]
             )
             flow = tuple(flows[n, x] for n in range(3))
             result, _ = prior_fields(
@@ -578,15 +619,19 @@
     fold_y = np.zeros((4, 8, 8, 8))
     for i in range(8):
         fold_y[:, i, i, :] = across
-    return [
-        jnp.asarray(np.ascontiguousarray(a), f32)
-        for a in (basis_z, basis_y, fold_y.reshape(32, 64), fold_z)
+    parts = []
+    for values, axis in ((fold_y.reshape(32, 64), 1), (fold_z, 1)):
+        high = values.astype(bf16)
+        low = (values - high.astype(np.float64)).astype(bf16)
+        parts.append(np.concatenate([high, low, high] if values.ndim == 2 else [high, high, low], axis=axis))
+    return [jnp.asarray(np.ascontiguousarray(a), f32) for a in (basis_z, basis_y)] + [
+        jnp.asarray(a) for a in parts
     ]
 
 
-def pairs(count, first):
+def pairs(count, slot):
     partner = {}
-    for i in range(first, count - 1, 2):
+    for i in range(slot, count - 1, SLOTS):
         partner[i], partner[i + 1] = i + 1, i
     result = []
     for i in range(count):
@@ -635,18 +680,34 @@
     pulled, flows, lines = kernel_call(
         pull_zy,
         [shape((19, 256, 128), f32), shape((5,) + kind.shape, f32), shape((16, 128), f32)],
-        [pltpu.VMEM((2, 2) + tile, f32)],
-    )(adjoint, forward, kind, sent_z, received_z, basis_z)
-
-    bundle = shape((BUNDLE,) + tile, f32)
-    pulled, sent_a, sent_b, edges, levels = kernel_call(
+        [
+            pltpu.VMEM((2, 2) + tile, f32),
+            pltpu.VMEM(forward.shape, bf16),
+            pltpu.SemaphoreType.DMA((4,)),
+        ],
+        in_specs=[
+            pl.BlockSpec(memory_space=pltpu.HBM if n == 1 else pltpu.VMEM) for n in range(6)
+        ],
+    )(
+        adjoint,
+        pltpu.with_memory_space_constraint(forward, pltpu.HBM),
+        kind,
+        sent_z,
+        received_z,
+        basis_z,
+    )
+
+    pulled, *sent_x, edges, levels = kernel_call(
         functools.partial(pack_x, directions),
-        [pulled, bundle, bundle, shape((2, 8) + tile, f32), shape((8,) + tile, f32)],
+        [pulled]
+        + [shape((BUNDLE,) + tile, bf16)] * SLOTS
+        + [shape((2, 8) + tile, f32), shape((8,) + tile, f32)],
         [pltpu.VMEM((32, 128), f32)],
         aliases={0: 0},
     )(pulled, flows, lines, basis_z, basis_y, *received_y)
-    received_b = lax.ppermute(sent_b, ("gx", "gz"), pairs(count_x, 1))
-    received_a = lax.ppermute(sent_a, ("gx", "gz"), pairs(count_x, 0))
+    received_x = [
+        lax.ppermute(sent, ("gx", "gz"), pairs(count_x, slot)) for slot, sent in enumerate(sent_x)
+    ]
 
     prior, totals = kernel_call(
         collide_inside,
@@ -655,7 +716,7 @@
         out_specs=[pl.BlockSpec(memory_space=pltpu.HBM), pl.BlockSpec(memory_space=pltpu.VMEM)],
     )(pulled, flows, kind, levels)
     gradient = kernel_call(project, shape((2, 4, 8, 32), f32))(
-        pulled, flows, edges, levels, received_a, received_b, totals, fold_y, fold_z
+        pulled, flows, edges, levels, *received_x, totals, fold_y, fold_z
     )
 
     whole = gradient[0] + lax.ppermute(gradient[1], "gz", swap)
@@ -671,10 +732,10 @@
         collide_outside,
         shape(adjoint.shape, bf16),
         [pltpu.VMEM((19, 8) + tile, bf16), pltpu.SemaphoreType.DMA((2,))],
-        aliases={6: 0},
-        in_specs=[pl.BlockSpec(memory_space=pltpu.VMEM)] * 6 + [in_hbm],
+        aliases={4 + SLOTS: 0},
+        in_specs=[pl.BlockSpec(memory_space=pltpu.VMEM)] * (4 + SLOTS) + [in_hbm],
         out_specs=in_hbm,
-    )(pulled, flows, kind, levels, received_a, received_b, prior)
+    )(pulled, flows, kind, levels, *received_x, prior)
     return prior, jnp.stack([whole[1] + from_low, whole[2] + from_high], axis=1)
 
 

time: 20 us -> 19.1 us (0.955)
  the two profiles are of different devices: /device:TPU:16 before, /device:TPU:0 now
where the time goes in v4:
time: 19.1 us; the launch traced here: 19 us
  starting transfers between devices  8.01 us (42%)
  Pallas kernels  6.48 us (34%)
  waiting for transfers between devices  3.04 us (16%)
  between operations  0.77 us (4%)
  local copies, waits for them, and re-layouts  0.64 us (3%)
    ppermute x1, starting transfers between devices, per_device(): received_y = [lax.ppermute(sent_y[0], 'gy', swap)]  2.89 us
    ppermute x3, starting transfers between devices, per_device(): lax.ppermute(sent, ('gx', 'gz'), pairs(count_x, slot))  2.68 us
    ppermute x1, starting transfers between devices, per_device(): other = lax.ppermute(jnp.where(side == 0, whole[3], whole[0]), 'gy', swap)  1.9 us
    pallas_call x1, Pallas kernels, per_device(): kernel_call(pull_zy, [shape((19, 256, 128), f32), shape((5,) + kind.shape...  1.63 us
    pallas_call x1, Pallas kernels, per_device(): kernel_call(collide_inside, [shape(adjoint.shape, bf16), shape((8,) + til...  1.59 us
    pallas_call x1, Pallas kernels, per_device(): kernel_call(pack_z, shape((4,) + tile, f32), [pltpu.VMEM((5,) + adjoint.s...  1.35 us
    ppermute x1, waiting for transfers between devices, per_device(): whole = gradient[0] + lax.ppermute(gradient[1], 'gz', swap)  1.16 us
    pallas_call x1, Pallas kernels, per_device(): kernel_call(collide_outside, shape(adjoint.shape, bf16), [pltpu.VMEM((19,...  0.97 us
  transfers between devices with their start and end apart: 7, of which 4 were waited for; matrix products, arithmetic and copies ran while one was open for 0% of the time, Pallas kernels for 23%

profile of v4, /device:TPU:0, one launch (start us, length us, event | category | flops | bytes accessed | tf_op | source)
XLA Modules:
  0.0 19.0 jit_solution(12455087257350011767)
XLA Ops:
  0.6 0.0 copy-start.2
  0.7 1.4 %shard_map.95.sent = f32[4,8,128]{2,1,0:T(8,128)S(1)} custom-call(bf16[19,32,8,128]{3,2,1,0:T(8,128)(2,1)} %adjoint.5, f32[8,2,32]{2,1,0:T(2,128)} %coefficients.1), custom_call_target="tpu_custom_call" | custom-call | tf_op jit(solution)/shard_map/pallas_call | solution.py:656
  2.0 0.5 %collective-permute-start = (f32[4,8,128]{2,1,0:T(8,128)S(1)}, f32[4,8,128]{2,1,0:T(8,128)S(1)}, u32[]{:S(2)}, u32[]{:S(2)}) collective-permute-start(f32[4,8,128]{2,1,0:T(8,128)S(1)} %shard_map.95.sent), channel_id=1, source_target_pairs={{0,1},{1,0},{2,3},{3,2},{4,5},{5,4},{6,7},{7,6},{8,9},{9,8},{10,11... | collective-permute-start | bytes 49160 | tf_op jit(solution)/shard_map/ppermute | solution.py:666
  2.5 0.1 shard_map.97.refs_0_
  2.7 0.7 %collective-permute-done.received = f32[4,8,128]{2,1,0:T(8,128)S(1)} collective-permute-done((f32[4,8,128]{2,1,0:T(8,128)S(1)}, f32[4,8,128]{2,1,0:T(8,128)S(1)}, u32[]{:S(2)}, u32[]{:S(2)}) %collective-permute-start) | collective-permute-done | bytes 16416 | tf_op jit(solution)/shard_map/ppermute | solution.py:666
  3.4 0.1 shard_map.98
  3.5 2.9 %collective-permute-start.1 = (bf16[176,128]{1,0:T(8,128)(2,1)S(1)}, bf16[176,128]{1,0:T(8,128)(2,1)S(1)}, u32[]{:S(2)}, u32[]{:S(2)}) collective-permute-start(bf16[176,128]{1,0:T(8,128)(2,1)S(1)} %shard_map.98), channel_id=1, source_target_pairs={{0,2},{2,0},{1,3},{3,1},{4,6},{6,4},{5,7},{7,5},{8,10},{10,8},{9,1... | collective-permute-start | bytes 135176 | tf_op jit(solution)/shard_map/ppermute | solution.py:676
  6.4 1.6 %shard_map.96 = (f32[19,256,128]{2,1,0:T(8,128)S(1)}, f32[5,32,8,128]{3,2,1,0:T(8,128)S(1)}, f32[16,128]{1,0:T(8,128)S(1)}) custom-call(bf16[19,32,8,128]{3,2,1,0:T(8,128)(2,1)S(1)} %copy-done, bf16[19,32,8,128]{3,2,1,0:T(8,128)(2,1)} %forward_far.1, s32[32,8,128]{2,1,0:T(8,128)S(1)} %copy-done.1, f32[4,8,128]{2,1,0:T(8,128)S(1)} %shard_map.95.sent, ...), custom_call_target="tpu_custom_call" | custom-call | tf_op jit(solution)/shard_map/pallas_call | solution.py:680
  8.0 0.4 %collective-permute-done.1.refs_0_ = bf16[176,128]{1,0:T(8,128)(2,1)S(1)} collective-permute-done((bf16[176,128]{1,0:T(8,128)(2,1)S(1)}, bf16[176,128]{1,0:T(8,128)(2,1)S(1)}, u32[]{:S(2)}, u32[]{:S(2)}) %collective-permute-start.1) | collective-permute-done | bytes 45088 | tf_op jit(solution)/shard_map/ppermute | solution.py:676
  8.4 0.2 %shard_map.99 = (f32[19,256,128]{2,1,0:T(8,128)S(1)}, bf16[23,8,128]{2,1,0:T(8,128)(2,1)S(1)}, bf16[23,8,128]{2,1,0:T(8,128)(2,1)S(1)}, bf16[23,8,128]{2,1,0:T(8...) custom-call(f32[19,256,128]{2,1,0:T(8,128)S(1)} %get-tuple-element.13.unpa, ...), custom_call_target="tpu_custom_call", output_to_operand_aliasing={{0}: (0, {})} | custom-call | tf_op jit(solution)/shard_map/pallas_call | solution.py:700
  8.7 2.2 %collective-permute-start.2 = (bf16[23,8,128]{2,1,0:T(8,128)(2,1)S(1)}, bf16[23,8,128]{2,1,0:T(8,128)(2,1)S(1)}, u32[]{:S(2)}, u32[]{:S(2)}) collective-permute-start(bf16[23,8,128]{2,1,0:T(8,128)(2,1)S(1)} %get-tuple-element.18), channel_id=1, source_target_pairs={{0,4},{1,5},{4,0},{5,1},{8,9},{9,8},{12,13},{13,12},{2,6},{3,7},{6... | collective-permute-start | bytes 141320 | tf_op jit(solution)/shard_map/ppermute | solution.py:709
  10.8 0.0 collective-permute-start.3
  10.8 0.5 %collective-permute-start.4 = (bf16[23,8,128]{2,1,0:T(8,128)(2,1)S(1)}, bf16[23,8,128]{2,1,0:T(8,128)(2,1)S(1)}, u32[]{:S(2)}, u32[]{:S(2)}) collective-permute-start(bf16[23,8,128]{2,1,0:T(8,128)(2,1)S(1)} %get-tuple-element.20), channel_id=1, source_target_pairs={{0,1},{1,0},{4,5},{5,4},{8,12},{9,13},{12,8},{13,9},{2,3},{3,2},{6... | collective-permute-start | bytes 141320 | tf_op jit(solution)/shard_map/ppermute | solution.py:709
  11.3 1.6 %shard_map.100 = (bf16[19,32,8,128]{3,2,1,0:T(8,128)(2,1)}, f32[8,8,128]{2,1,0:T(8,128)S(1)}) custom-call(f32[19,256,128]{2,1,0:T(8,128)S(1)} %get-tuple-element.16.pulled, f32[5,32,8,128]{3,2,1,0:T(8,128)S(1)} %get-tuple-element.14.flows, s32[32,8,128]{2,1,0:T(8,128)S(1)} %copy-done.1, f32[8,8,128]{2,1,0:T(8,128)S(1)} %get-tuple-element.17.levels), custom_call_target="tpu_custom_call" | custom-call | tf_op jit(solution)/shard_map/pallas_call | solution.py:712
  12.9 0.0 collective-permute-done.2.refs_0_
  13.0 0.0 collective-permute-done.3.refs_1_
  13.0 0.0 collective-permute-done.4.refs_2_
  13.0 0.5 %shard_map.102 = f32[2,4,8,32]{3,2,1,0:T(8,128)S(1)} custom-call(f32[19,256,128]{2,1,0:T(8,128)S(1)} %get-tuple-element.16.pulled, f32[5,32,8,128]{3,2,1,0:T(8,128)S(1)} %get-tuple-element.14.flows, f32[2,8,8,128]{3,2,1,0:T(8,128)S(1)} %get-tuple-element.22.edges, f32[8,8,128]{2,1,0:T(8,128)S(1)} %get-tuple-element.17.levels, ...), custom_call_target="tpu_custom_call" | custom-call | tf_op jit(solution)/shard_map/pallas_call | solution.py:718
  13.5 0.0 collective-permute-start.5
  13.5 1.2 %collective-permute-done.5 = f32[4,8,32]{2,1,0:T(8,128)S(1)} collective-permute-done((f32[4,8,32]{2,1,0:T(8,128)S(1)}, f32[4,8,32]{2,1,0:T(8,128)S(1)}, u32[]{:S(2)}, u32[]{:S(2)}) %collective-permute-start.5) | collective-permute-done | bytes 4128 | tf_op jit(solution)/shard_map/ppermute | solution.py:722
  14.7 1.9 %collective-permute-start.6 = (f32[8,32]{1,0:T(8,128)S(1)}, f32[8,32]{1,0:T(8,128)S(1)}, u32[]{:S(2)}, u32[]{:S(2)}) collective-permute-start(f32[8,32]{1,0:T(8,128)S(1)} %fusion.3), channel_id=1, source_target_pairs={{0,2},{2,0},{1,3},{3,1},{4,6},{6,4},{5,7},{7,5},{8,10},{10,8},{9,1... | collective-permute-start | bytes 3080 | tf_op jit(solution)/shard_map/ppermute | solution.py:724
  16.6 1.0 %shard_map.101 = bf16[19,32,8,128]{3,2,1,0:T(8,128)(2,1)} custom-call(f32[19,256,128]{2,1,0:T(8,128)S(1)} %get-tuple-element.16.pulled, f32[5,32,8,128]{3,2,1,0:T(8,128)S(1)} %get-tuple-element.14.flows, s32[32,8,128]{2,1,0:T(8,128)S(1)} %copy-done.1, f32[8,8,128]{2,1,0:T(8,128)S(1)} %get-tuple-element.17.levels, ...), custom_call_target="tpu_custom_call", output_to_operand_aliasing={{}: (7, {})} | custom-call | tf_op jit(solution)/shard_map/pallas_call | solution.py:731
  17.5 0.8 %collective-permute-done.6 = f32[8,32]{1,0:T(8,128)S(1)} collective-permute-done((f32[8,32]{1,0:T(8,128)S(1)}, f32[8,32]{1,0:T(8,128)S(1)}, u32[]{:S(2)}, u32[]{:S(2)}) %collective-permute-start.6) | collective-permute-done | bytes 1056 | tf_op jit(solution)/shard_map/ppermute | solution.py:724
  18.4 0.6 %copy.12 = f32[8,2,32]{2,1,0:T(2,128)} copy(f32[8,2,32]{2,0,1:T(8,128)S(1)} %pad_maximum_fusion) | data formatting | bytes 4096
  (16 shorter events, 0.1 us)
Async XLA Ops:
  0.6 1.9 %copy-start = (bf16[19,32,8,128]{3,2,1,0:T(8,128)(2,1)S(1)}, bf16[19,32,8,128]{3,2,1,0:T(8,128)(2,1)}, u32[]{:S(2)}) copy-start(bf16[19,32,8,128]{3,2,1,0:T(8,128)(2,1)} %adjoint.5) | copy-start | bytes 3735556
  0.6 5.7 %copy-start.2 = (f32[2,128,128]{2,1,0:T(8,128)S(1)}, f32[2,128,128]{2,1,0:T(8,128)}, u32[]{:S(2)}) copy-start(f32[2,128,128]{2,1,0:T(8,128)} %constant.18.clone.basis_z) | copy-start | bytes 393220
  0.7 5.7 %copy-start.1 = (s32[32,8,128]{2,1,0:T(8,128)S(1)}, s32[32,8,128]{2,1,0:T(8,128)}, u32[]{:S(2)}) copy-start(s32[32,8,128]{2,1,0:T(8,128)} %kind.5) | copy-start | bytes 393220
  2.0 1.4 %collective-permute-start = (f32[4,8,128]{2,1,0:T(8,128)S(1)}, f32[4,8,128]{2,1,0:T(8,128)S(1)}, u32[]{:S(2)}, u32[]{:S(2)}) collective-permute-start(f32[4,8,128]{2,1,0:T(8,128)S(1)} %shard_map.95.sent), channel_id=1, source_target_pairs={{0,1},{1,0},{2,3},{3,2},{4,5},{5,4},{6,7},{7,6},{8,9},{9,8},{10,11... | collective-permute-start | bytes 49160 | tf_op jit(solution)/shard_map/ppermute | solution.py:666
  3.5 4.9 %copy-start.5 = (f32[4,8,128]{2,1,0:T(8,128)S(1)}, f32[4,8,128]{2,1,0:T(8,128)}, u32[]{:S(2)}) copy-start(f32[4,8,128]{2,1,0:T(8,128)} %constant.19.clone.basis_y) | copy-start | bytes 49156
  3.5 4.9 %collective-permute-start.1 = (bf16[176,128]{1,0:T(8,128)(2,1)S(1)}, bf16[176,128]{1,0:T(8,128)(2,1)S(1)}, u32[]{:S(2)}, u32[]{:S(2)}) collective-permute-start(bf16[176,128]{1,0:T(8,128)(2,1)S(1)} %shard_map.98), channel_id=1, source_target_pairs={{0,2},{2,0},{1,3},{3,1},{4,6},{6,4},{5,7},{7,5},{8,10},{10,8},{9,1... | collective-permute-start | bytes 135176 | tf_op jit(solution)/shard_map/ppermute | solution.py:676
  8.7 4.3 %collective-permute-start.2 = (bf16[23,8,128]{2,1,0:T(8,128)(2,1)S(1)}, bf16[23,8,128]{2,1,0:T(8,128)(2,1)S(1)}, u32[]{:S(2)}, u32[]{:S(2)}) collective-permute-start(bf16[23,8,128]{2,1,0:T(8,128)(2,1)S(1)} %get-tuple-element.18), channel_id=1, source_target_pairs={{0,4},{1,5},{4,0},{5,1},{8,9},{9,8},{12,13},{13,12},{2,6},{3,7},{6... | collective-permute-start | bytes 141320 | tf_op jit(solution)/shard_map/ppermute | solution.py:709
  10.8 2.1 %collective-permute-start.3 = (bf16[23,8,128]{2,1,0:T(8,128)(2,1)S(1)}, bf16[23,8,128]{2,1,0:T(8,128)(2,1)S(1)}, u32[]{:S(2)}, u32[]{:S(2)}) collective-permute-start(bf16[23,8,128]{2,1,0:T(8,128)(2,1)S(1)} %get-tuple-element.19), channel_id=1, source_target_pairs={{0,1},{1,0},{4,8},{5,9},{8,4},{9,5},{12,13},{13,12},{2,3},{3,2},{6... | collective-permute-start | bytes 141320 | tf_op jit(solution)/shard_map/ppermute | solution.py:709
  10.8 2.1 %collective-permute-start.4 = (bf16[23,8,128]{2,1,0:T(8,128)(2,1)S(1)}, bf16[23,8,128]{2,1,0:T(8,128)(2,1)S(1)}, u32[]{:S(2)}, u32[]{:S(2)}) collective-permute-start(bf16[23,8,128]{2,1,0:T(8,128)(2,1)S(1)} %get-tuple-element.20), channel_id=1, source_target_pairs={{0,1},{1,0},{4,5},{5,4},{8,12},{9,13},{12,8},{13,9},{2,3},{3,2},{6... | collective-permute-start | bytes 141320 | tf_op jit(solution)/shard_map/ppermute | solution.py:709
  11.3 1.6 %copy-start.3 = (bf16[2,384,64]{2,1,0:T(8,128)(2,1)S(1)}, bf16[2,384,64]{2,1,0:T(8,128)(2,1)}, u32[]{:S(2)}) copy-start(bf16[2,384,64]{2,1,0:T(8,128)(2,1)} %constant.21.clone.refs_5_) | copy-start | bytes 294916
  11.3 1.6 %copy-start.4 = (bf16[32,192]{1,0:T(8,128)(2,1)S(1)}, bf16[32,192]{1,0:T(8,128)(2,1)}, u32[]{:S(2)}) copy-start(bf16[32,192]{1,0:T(8,128)(2,1)} %constant.20.clone.refs_4_) | copy-start | bytes 36868
  13.5 1.2 %collective-permute-start.5 = (f32[4,8,32]{2,1,0:T(8,128)S(1)}, f32[4,8,32]{2,1,0:T(8,128)S(1)}, u32[]{:S(2)}, u32[]{:S(2)}) collective-permute-start(f32[4,8,32]{2,1,0:T(8,128)S(1)} %slice_bitcast_fusion), channel_id=1, source_target_pairs={{0,1},{1,0},{2,3},{3,2},{4,5},{5,4},{6,7},{7,6},{8,9},{9,8},{10,11... | collective-permute-start | bytes 12296 | tf_op jit(solution)/shard_map/ppermute | solution.py:722
  14.7 3.7 %collective-permute-start.6 = (f32[8,32]{1,0:T(8,128)S(1)}, f32[8,32]{1,0:T(8,128)S(1)}, u32[]{:S(2)}, u32[]{:S(2)}) collective-permute-start(f32[8,32]{1,0:T(8,128)S(1)} %fusion.3), channel_id=1, source_target_pairs={{0,2},{2,0},{1,3},{3,1},{4,6},{6,4},{5,7},{7,5},{8,10},{10,8},{9,1... | collective-permute-start | bytes 3080 | tf_op jit(solution)/shard_map/ppermute | solution.py:724

commit v5 on v4

--- a/solution.py
+++ b/solution.py
@@ -45,14 +45,35 @@
 
 FACE, NEAR, FAR, FIELD, LEVEL, BUNDLE = 0, 5, 9, 15, 19, 23
 SLOTS = 3
-COARSE_ROWS, STRIP = 160, 176
+LINE_ROWS, STRIP = 160, 176
 MASS, INVERSE = 3, 4
 EDGE_PLANES = (0, 1, 2, 3, 28, 29, 30, 31)
+INNER = 16
 
 
 def spline(distance):
     radius = np.abs(distance) / 6.0
     return np.where(radius < 1.0, (1.0 - radius) ** 4 * (1.0 + 4.0 * radius), 0.0)
+
+
+def spline_along(dimension, shape, position):
+    distance = lax.broadcasted_iota(jnp.int32, shape, dimension).astype(f32) - position
+    radius = jnp.abs(distance) * (1.0 / 6.0)
+    square = (1.0 - radius) * (1.0 - radius)
+    return jnp.where(radius < 1.0, square * square * (1.0 + 4.0 * radius), 0.0)
+
+
+def basis_along_z(count):
+    places = lax.broadcasted_iota(jnp.int32, (count, 128), 0).astype(f32)
+    return spline_along(1, (count, 128), 4.0 * places + 1.5)
+
+
+def rim_along_z(core, count):
+    return spline_along(1, (8, 128), jnp.where(core == 0, 4.0 * count + 1.5, -2.5))
+
+
+def basis_along_y(j):
+    return spline_along(0, (8, 128), 4.0 * j + 1.5)
 
 
 def kernel_call(body, out_shape, scratch_shapes=(), aliases=None, **specs):
@@ -204,12 +225,12 @@
     out[3] = jnp.zeros((8, 128), f32)
     for copy in copies:
         copy.wait()
+    for j in range(2):
+        out[2 + j, :, 0:count] = coarse[:, j, :]
     for which, source in enumerate((127, 0)):
 
         @pl.when(core == which)
         def _():
-            for j in range(2):
-                out[2 + j, :, count * which : count * which + count] = coarse[:, j, :]
             chains = {}
             for k in range(5):
                 for x in range(32):
@@ -230,8 +251,14 @@
     return ((YM, 7), (YP, 0))
 
 
-def gather_rows(directions, adjoint, *refs):
-    outs, plane = refs[:-1], refs[-1]
+def gather_rows(directions, count, adjoint, sent, *refs):
+    *outs, lines, plane = refs
+    lines[...] = jnp.dot(
+        jnp.concatenate([sent[2], sent[3]], axis=0),
+        jnp.concatenate([basis_along_z(count), jnp.zeros((128 - count, 128), f32)], axis=0),
+        precision=highest,
+        preferred_element_type=f32,
+    )
     lanes = lax.broadcasted_iota(jnp.int32, (32, 128), 1)
 
     def emit(components, row, out):
@@ -256,13 +283,18 @@
             emit(*sides[n], outs[n])
 
 
-def pack_y(directions, sent, received, *refs):
-    sources, outs = refs[:directions], refs[directions:]
+def pack_y(directions, count, received, own_lines, *refs):
+    sources, outs, lines = refs[:directions], refs[directions:-1], refs[-1]
     core = lax.axis_index("gz")
     lanes = lax.broadcasted_iota(jnp.int32, (32, 128), 1)
     sublanes = lax.broadcasted_iota(jnp.int32, (32, 128), 0)
-
-    def emit(components, row, coarse_row, source, out):
+    rim_z = rim_along_z(core, count)
+    at_rim = iota(1) == core * (count - 1)
+    for j in range(2):
+        rim = jnp.sum(jnp.where(at_rim, received[2 + j], 0.0), axis=1, keepdims=True)
+        lines[8 * j : 8 * j + 8, :] = own_lines[8 * j : 8 * j + 8, :] + rim * rim_z
+
+    def emit(components, row, j, source, out):
         for k, q in enumerate(components):
             rows = source[k * 32 : k * 32 + 32, :]
             step = VELOCITY[q][2]
@@ -274,24 +306,24 @@
                 column = jnp.where(core == (0 if step > 0 else 1), column, 0.0)
                 rows = rows + jnp.where(lanes == (127 if step > 0 else 0), column, 0.0)
             out[k * 32 : k * 32 + 32, :] = rows.astype(bf16)
-        coarse = sent[coarse_row] + received[coarse_row]
-        high = coarse.astype(bf16)
-        out[COARSE_ROWS:STRIP, :] = jnp.concatenate(
-            [high, (coarse - high.astype(f32)).astype(bf16)], axis=0
+        line = lines[8 * j : 8 * j + 8, :]
+        high = line.astype(bf16)
+        out[LINE_ROWS:STRIP, :] = jnp.concatenate(
+            [high, (line - high.astype(f32)).astype(bf16)], axis=0
         )
 
     sides = y_sides(directions)
     if directions == 1:
         side = lax.axis_index("gy")
         for n in range(2):
-            pl.when(side == n)(functools.partial(emit, *sides[n], 3 - n, sources[0], outs[0]))
+            pl.when(side == n)(functools.partial(emit, *sides[n], 1 - n, sources[0], outs[0]))
     else:
         for n in range(2):
-            emit(*sides[n], 3 - n, sources[n], outs[n])
+            emit(*sides[n], 1 - n, sources[n], outs[n])
 
 
 def pull_zy(
-    adjoint, forward_far, kind, sent, received, basis_z, pulled, flows, lines, columns, forward, semaphores
+    adjoint, forward_far, kind, received, pulled, flows, columns, forward, semaphores
 ):
     copies = [
         pltpu.make_async_copy(
@@ -304,8 +336,6 @@
     core = lax.axis_index("gz")
     load_columns(core, received, columns)
     sublanes = iota(0)
-    coarse = jnp.concatenate([sent[2] + received[2], sent[3] + received[3]], axis=0)
-    lines[...] = jnp.dot(coarse, basis_z[core], precision=highest, preferred_element_type=f32)
 
     def step(x, carry):
         for q in range(19):
@@ -333,11 +363,10 @@
         lax.fori_loop(8 * n, 8 * n + 8, flow, 0, unroll=4)
 
 
-def pack_x(directions, unpatched, flows, lines, basis_z, basis_y, *refs):
+def pack_x(directions, unpatched, flows, lines, *refs):
     received = refs[:directions]
     pulled, *outs, edges, levels, extra = refs[directions:]
     del unpatched
-    core = lax.axis_index("gz")
     side = lax.axis_index("gy")
     place = lax.rem(lax.axis_index("gx"), SLOTS)
 
@@ -346,19 +375,18 @@
             pulled[q, pl.ds(row, 32, stride=8), :] = strip[k * 32 : k * 32 + 32, :].astype(f32)
 
     def outer_line(strip):
-        parts = strip[COARSE_ROWS:STRIP, :].astype(f32)
-        coarse = parts[0:8] + parts[8:16]
-        return jnp.dot(coarse, basis_z[core], precision=highest, preferred_element_type=f32)
+        parts = strip[LINE_ROWS:STRIP, :].astype(f32)
+        return parts[0:8] + parts[8:16]
 
     if directions == 1:
         pl.when(side == 0)(lambda: patch(YP, 7, received[0]))
         pl.when(side == 1)(lambda: patch(YM, 0, received[0]))
-        outer = [(outer_line(received[0]), basis_y[3 - 3 * side])]
+        outer = [(outer_line(received[0]), basis_along_y(jnp.where(side == 0, 2.0, -1.0)))]
     else:
         patch(YM, 0, received[0])
         patch(YP, 7, received[1])
-        outer = [(outer_line(received[0]), basis_y[0]), (outer_line(received[1]), basis_y[3])]
-    terms = [(lines[0:8, :], basis_y[1]), (lines[8:16, :], basis_y[2])] + outer
+        outer = [(outer_line(received[0]), basis_along_y(-1)), (outer_line(received[1]), basis_along_y(2))]
+    terms = [(lines[0:8, :], basis_along_y(0)), (lines[8:16, :], basis_along_y(1))] + outer
     for n, (line, _) in enumerate(terms):
         extra[n * 8 : n * 8 + 8, :] = line
     for i in range(8):
@@ -457,7 +485,7 @@
 def collide_inside(pulled, flows, kind, levels, out, totals, stage, semaphores):
     totals[...] = jnp.zeros((8, 8, 128), f32)
 
-    def middle(block, carry):
+    def middle(with_prior, block, carry):
         around = [levels[block - 1], levels[block], levels[block + 1]]
         sums = [None] * 3
         for position in range(4):
@@ -465,9 +493,15 @@
             bent = bent_level(around, position)
             flow = tuple(flows[n, x] for n in range(3))
             values = {q: pulled[q, rows_of(x + VELOCITY[q][0]), :] for q in range(19)}
-            result, along = prior_fields(bent, kind[x], flow, flows[INVERSE, x], pair_moments(values))
-            emit_prior(stage, x - 4, kind[x], values, result)
-            sensitivity = (-1.6 / 36.0) * flows[MASS, x] * along * slope_of(bent)
+            moments = pair_moments(values)
+            if with_prior:
+                result, along = prior_fields(bent, kind[x], flow, flows[INVERSE, x], moments)
+                emit_prior(stage, x - 4, kind[x], values, result)
+                sensitivity = (-1.6 / 36.0) * flows[MASS, x] * along
+            else:
+                alpha, beta = alpha_beta(moments, flow, flows[MASS, x])
+                sensitivity = alpha + (0.55 + 0.45 * bent) * beta
+            sensitivity = sensitivity * slope_of(bent)
             for n in range(3):
                 term = weight_of(position, n - 1) * sensitivity
                 sums[n] = term if sums[n] is None else sums[n] + term
@@ -476,14 +510,15 @@
         return carry
 
     copies = []
-    for part in range(3):
-        lax.fori_loop(1 + 2 * part, 3 + 2 * part, middle, 0)
+    for part in range(INNER // 8):
+        lax.fori_loop(1 + 2 * part, 3 + 2 * part, functools.partial(middle, True), 0)
         copies.append(
             pltpu.make_async_copy(
                 stage.at[:, pl.ds(8 * part, 8)], out.at[:, pl.ds(4 + 8 * part, 8)], semaphores.at[part]
             )
         )
         copies[part].start()
+    lax.fori_loop(1 + INNER // 4, 7, functools.partial(middle, False), 0)
     for copy in copies:
         copy.wait()
 
@@ -509,14 +544,24 @@
     return [read(LEVEL + n) + read(LEVEL + 2 + n) for n in range(2)]
 
 
-def in_parts(values, axis):
-    high = values.astype(bf16)
-    low = (values - high.astype(f32)).astype(bf16)
-    return jnp.concatenate([high, high, low] if axis == 0 else [high, low, high], axis=axis)
+def fold_rows(tiles, weight):
+    sublanes = iota(0)
+    tiles = [weight * tile for tile in tiles]
+    for bit in (4, 2, 1):
+        half = len(tiles) // 2
+        tiles = [
+            jnp.where(
+                sublanes & bit == 0,
+                tiles[i] + pltpu.roll(tiles[i], 8 - bit, 0),
+                tiles[i + half] + pltpu.roll(tiles[i + half], bit, 0),
+            )
+            for i in range(half)
+        ]
+    return tiles[0]
 
 
 def project(pulled, flows, edges, levels, *refs):
-    inner, fold_y, fold_z, gradient = refs[SLOTS:]
+    inner, folded, rim = refs[SLOTS:]
     core = lax.axis_index("gz")
     low, high = along_x(refs[:SLOTS])
     totals = [inner[i] for i in range(8)]
@@ -562,71 +607,77 @@
                 more = missing[block, position]
                 alpha, beta = alpha + more[0], beta + more[1]
             add(block, position, alpha, beta)
-    stacked = jnp.concatenate(totals, axis=0)
-    folded = jnp.dot(fold_y[...], in_parts(stacked, 0), preferred_element_type=f32)
-    result = jnp.dot(in_parts(folded, 1), fold_z[core], preferred_element_type=f32)
-    for part in range(2):
-        for j in range(4):
-            gradient[part, j] = result[j * 8 : j * 8 + 8, part * 32 : part * 32 + 32]
+    lanes = iota(1)
+    count = rim.shape[2]
+    rim_z = rim_along_z(core, count)
+    for j in range(4):
+        sums = fold_rows(totals, basis_along_y(j - 1))
+        folded[8 * j : 8 * j + 8, :] = sums
+        across = jnp.sum(sums * rim_z, axis=1, keepdims=True)
+        rim[j] = jnp.where(lanes == core * (count - 1), across, 0.0)[:, 0:count]
+
+
+def fold_along_z(folded, out):
+    result = lax.dot_general(
+        folded[...],
+        basis_along_z(out.shape[2]),
+        (((1,), (1,)), ((), ())),
+        precision=highest,
+        preferred_element_type=f32,
+    )
+    for j in range(4):
+        out[j] = result[8 * j : 8 * j + 8]
 
 
 def collide_outside(pulled, flows, kind, levels, *refs):
     out, stage, semaphores = refs[SLOTS + 1 :]
     low, high = along_x(refs[:SLOTS])
-    copies = []
-    for part, planes in enumerate((EDGE_PLANES[:4], EDGE_PLANES[4:])):
-        for slot, x in enumerate(planes):
-            values = {}
-            for q in range(19):
-                target = x + VELOCITY[q][0]
-                if target < 0:
-                    values[q] = low(FACE + XM.index(q))
-                elif target > 31:
-                    values[q] = high(FACE + XP.index(q))
-                else:
-                    values[q] = pulled[q, rows_of(target), :]
-            around = (
-                [levels[6], levels[7], levels_along_x(high)[0]]
-                if part
-                else [levels_along_x(low)[0], levels[0], levels[1]]
-            )
-            flow = tuple(flows[n, x] for n in range(3))
-            result, _ = prior_fields(
-                bent_level(around, slot), kind[x], flow, flows[INVERSE, x], pair_moments(values)
-            )
-            emit_prior(stage, 4 * part + slot, kind[x], values, result)
-        copies.append(
-            pltpu.make_async_copy(
-                stage.at[:, pl.ds(4 * part, 4)], out.at[:, pl.ds(28 * part, 4)], semaphores.at[part]
-            )
+    first = 4 + INNER
+
+    def emit(x, slot, around, position, values):
+        flow = tuple(flows[n, x] for n in range(3))
+        result, _ = prior_fields(
+            bent_level(around, position), kind[x], flow, flows[INVERSE, x], pair_moments(values)
         )
-        copies[part].start()
+        emit_prior(stage, slot, kind[x], values, result)
+
+    def middle(block, carry):
+        around = [levels[block - 1], levels[block], levels[block + 1]]
+        for position in range(4):
+            x = block * 4 + position
+            values = {q: pulled[q, rows_of(x + VELOCITY[q][0]), :] for q in range(19)}
+            emit(x, x - first + 4, around, position, values)
+        return carry
+
+    def edge(x, around):
+        values = {}
+        for q in range(19):
+            target = x + VELOCITY[q][0]
+            if target < 0:
+                values[q] = low(FACE + XM.index(q))
+            elif target > 31:
+                values[q] = high(FACE + XP.index(q))
+            else:
+                values[q] = pulled[q, rows_of(target), :]
+        emit(x, x if x < 4 else x - first + 4, around, x % 4, values)
+
+    lowest = [levels_along_x(low)[0], levels[0], levels[1]]
+    highest_levels = [levels[6], levels[7], levels_along_x(high)[0]]
+    lax.fori_loop(1 + INNER // 4, 7, middle, 0)
+    for x in range(28, 32):
+        edge(x, highest_levels)
+    copies = [
+        pltpu.make_async_copy(
+            stage.at[:, pl.ds(4, 32 - first)], out.at[:, pl.ds(first, 32 - first)], semaphores.at[0]
+        ),
+        pltpu.make_async_copy(stage.at[:, pl.ds(0, 4)], out.at[:, pl.ds(0, 4)], semaphores.at[1]),
+    ]
+    copies[0].start()
+    for x in range(4):
+        edge(x, lowest)
+    copies[1].start()
     for copy in copies:
         copy.wait()
-
-
-def bases():
-    fine = np.arange(128.0)
-    basis_z = np.zeros((2, 128, 128))
-    fold_z = np.zeros((2, 128, 64))
-    for core in range(2):
-        full = spline(fine[None, :] + 128 * core - 4.0 * np.arange(64)[:, None] - 1.5)
-        basis_z[core, 0:64] = full
-        fold_z[core, :, 0:32] = full[32 * core : 32 * core + 32].T
-        fold_z[core, :, 32:64] = full[32 * (1 - core) : 32 * (1 - core) + 32].T
-    across = spline(np.arange(8.0)[None, :] - 4.0 * np.arange(-1, 3)[:, None] - 1.5)
-    basis_y = np.broadcast_to(across[:, :, None], (4, 8, 128))
-    fold_y = np.zeros((4, 8, 8, 8))
-    for i in range(8):
-        fold_y[:, i, i, :] = across
-    parts = []
-    for values, axis in ((fold_y.reshape(32, 64), 1), (fold_z, 1)):
-        high = values.astype(bf16)
-        low = (values - high.astype(np.float64)).astype(bf16)
-        parts.append(np.concatenate([high, low, high] if values.ndim == 2 else [high, high, low], axis=axis))
-    return [jnp.asarray(np.ascontiguousarray(a), f32) for a in (basis_z, basis_y)] + [
-        jnp.asarray(a) for a in parts
-    ]
 
 
 def pairs(count, slot):
@@ -649,7 +700,7 @@
     directions = 1 if count_y == 2 else 2
     tile = (8, 128)
     shape = jax.ShapeDtypeStruct
-    basis_z, basis_y, fold_y, fold_z = bases()
+    count = coefficients.shape[2]
     up = [(i, i + 1) for i in range(count_y - 1)]
     down = [(i + 1, i) for i in range(count_y - 1)]
 
@@ -664,37 +715,36 @@
         in_specs=[pl.BlockSpec(memory_space=pltpu.HBM)] * 2,
     )(*(pltpu.with_memory_space_constraint(a, pltpu.HBM) for a in (adjoint, coefficients)))
     received_z = lax.ppermute(sent_z, "gz", swap)
-    rows = kernel_call(
-        functools.partial(gather_rows, directions),
-        [shape((COARSE_ROWS, 128), f32)] * directions,
+    *rows, lines = kernel_call(
+        functools.partial(gather_rows, directions, count),
+        [shape((LINE_ROWS, 128), f32)] * directions + [shape((16, 128), f32)],
         [pltpu.VMEM((256, 128), f32)],
-    )(adjoint)
-    sent_y = kernel_call(
-        functools.partial(pack_y, directions), [shape((STRIP, 128), bf16)] * directions
-    )(sent_z, received_z, *rows)
+    )(adjoint, sent_z)
+    *sent_y, lines = kernel_call(
+        functools.partial(pack_y, directions, count),
+        [shape((STRIP, 128), bf16)] * directions + [shape((16, 128), f32)],
+    )(received_z, lines, *rows)
     if directions == 1:
         received_y = [lax.ppermute(sent_y[0], "gy", swap)]
     else:
         received_y = [lax.ppermute(sent_y[0], "gy", up), lax.ppermute(sent_y[1], "gy", down)]
 
-    pulled, flows, lines = kernel_call(
+    pulled, flows = kernel_call(
         pull_zy,
-        [shape((19, 256, 128), f32), shape((5,) + kind.shape, f32), shape((16, 128), f32)],
+        [shape((19, 256, 128), f32), shape((5,) + kind.shape, f32)],
         [
             pltpu.VMEM((2, 2) + tile, f32),
             pltpu.VMEM(forward.shape, bf16),
             pltpu.SemaphoreType.DMA((4,)),
         ],
         in_specs=[
-            pl.BlockSpec(memory_space=pltpu.HBM if n == 1 else pltpu.VMEM) for n in range(6)
+            pl.BlockSpec(memory_space=pltpu.HBM if n == 1 else pltpu.VMEM) for n in range(4)
         ],
     )(
         adjoint,
         pltpu.with_memory_space_constraint(forward, pltpu.HBM),
         kind,
-        sent_z,
         received_z,
-        basis_z,
     )
 
     pulled, *sent_x, edges, levels = kernel_call(
@@ -704,7 +754,7 @@
         + [shape((2, 8) + tile, f32), shape((8,) + tile, f32)],
         [pltpu.VMEM((32, 128), f32)],
         aliases={0: 0},
-    )(pulled, flows, lines, basis_z, basis_y, *received_y)
+    )(pulled, flows, lines, *received_y)
     received_x = [
         lax.ppermute(sent, ("gx", "gz"), pairs(count_x, slot)) for slot, sent in enumerate(sent_x)
     ]
@@ -712,14 +762,14 @@
     prior, totals = kernel_call(
         collide_inside,
         [shape(adjoint.shape, bf16), shape((8,) + tile, f32)],
-        [pltpu.VMEM((19, 24) + tile, bf16), pltpu.SemaphoreType.DMA((3,))],
+        [pltpu.VMEM((19, INNER) + tile, bf16), pltpu.SemaphoreType.DMA((INNER // 8,))],
         out_specs=[pl.BlockSpec(memory_space=pltpu.HBM), pl.BlockSpec(memory_space=pltpu.VMEM)],
     )(pulled, flows, kind, levels)
-    gradient = kernel_call(project, shape((2, 4, 8, 32), f32))(
-        pulled, flows, edges, levels, *received_x, totals, fold_y, fold_z
+    folded, rim = kernel_call(project, [shape((32, 128), f32), shape((4, 8, count), f32)])(
+        pulled, flows, edges, levels, *received_x, totals
     )
-
-    whole = gradient[0] + lax.ppermute(gradient[1], "gz", swap)
+    other_rim = lax.ppermute(rim, "gz", swap)
+    whole = kernel_call(fold_along_z, shape(rim.shape, f32))(folded) + other_rim
     if directions == 1:
         other = lax.ppermute(jnp.where(side == 0, whole[3], whole[0]), "gy", swap)
         from_low = jnp.where(side == 1, other, 0.0)
@@ -731,7 +781,7 @@
     prior = kernel_call(
         collide_outside,
         shape(adjoint.shape, bf16),
-        [pltpu.VMEM((19, 8) + tile, bf16), pltpu.SemaphoreType.DMA((2,))],
+        [pltpu.VMEM((19, 32 - INNER) + tile, bf16), pltpu.SemaphoreType.DMA((2,))],
         aliases={4 + SLOTS: 0},
         in_specs=[pl.BlockSpec(memory_space=pltpu.VMEM)] * (4 + SLOTS) + [in_hbm],
         out_specs=in_hbm,

time: 19.1 us -> 18.6 us (0.974)
  waiting for transfers between devices: 3.04 us -> 2.69 us
  Pallas kernels: 6.48 us -> 6.28 us
    ppermute x1, waiting for transfers between devices: 0.8 us -> 0.33 us  [per_device(): other = lax.ppermute(jnp.where(side == 0, whole[3], whole[0]), 'gy', swap)]
    pallas_call x1, Pallas kernels: 0.97 us -> 1.26 us  [per_device(): kernel_call(collide_outside, shape(adjoint.shape, bf16), [pltpu.VMEM((19,...]
    pallas_call x1, Pallas kernels: 1.59 us -> 1.31 us  [per_device(): kernel_call(collide_inside, [shape(adjoint.shape, bf16), shape((8,) + til...]
    ppermute x3, waiting for transfers between devices: 0.01 us -> 0.22 us  [per_device(): lax.ppermute(sent, ('gx', 'gz'), pairs(count_x, slot))]
    pallas_call x3 -> x4, Pallas kernels: 0.69 us -> 0.74 us  [the longest x1 0.27 us: per_device(): kernel_call(functools.partial(gather_rows, directions, count), [shape((LI...]
    unnamed x13 -> x5, local copies, waits for them, and re-layouts: 0.63 us -> 0.61 us
  transfers between devices with their start and end apart: 7 -> 7, of which waited for: 4 -> 5; matrix products, arithmetic and copies ran while one was open for 0% -> 0% of each run, Pallas kernels for 23% -> 24%
where the time goes in v5:
time: 18.6 us; the launch traced here: 18.5 us
  starting transfers between devices  8.17 us (44%)
  Pallas kernels  6.28 us (34%)
  waiting for transfers between devices  2.69 us (14%)
  between operations  0.72 us (4%)
  local copies, waits for them, and re-layouts  0.61 us (3%)
    ppermute x1, starting transfers between devices, per_device(): received_y = [lax.ppermute(sent_y[0], 'gy', swap)]  2.96 us
    ppermute x3, starting transfers between devices, per_device(): lax.ppermute(sent, ('gx', 'gz'), pairs(count_x, slot))  2.62 us
    ppermute x1, starting transfers between devices, per_device(): other = lax.ppermute(jnp.where(side == 0, whole[3], whole[0]), 'gy', swap)  2.07 us
    pallas_call x1, Pallas kernels, per_device(): kernel_call(pull_zy, [shape((19, 256, 128), f32), shape((5,) + kind.shape...  1.47 us
    pallas_call x1, Pallas kernels, per_device(): kernel_call(pack_z, shape((4,) + tile, f32), [pltpu.VMEM((5,) + adjoint.s...  1.35 us
    pallas_call x1, Pallas kernels, per_device(): kernel_call(collide_inside, [shape(adjoint.shape, bf16), shape((8,) + til...  1.31 us
    pallas_call x1, Pallas kernels, per_device(): kernel_call(collide_outside, shape(adjoint.shape, bf16), [pltpu.VMEM((19,...  1.26 us
    ppermute x1, waiting for transfers between devices, per_device(): other_rim = lax.ppermute(rim, 'gz', swap)  1.02 us
  transfers between devices with their start and end apart: 7, of which 5 were waited for; matrix products, arithmetic and copies ran while one was open for 0% of the time, Pallas kernels for 24%

profile of v5, /device:TPU:0, one launch (start us, length us, event | category | flops | bytes accessed | tf_op | source)
XLA Modules:
  0.0 18.5 jit_solution(4170399833758338994)
XLA Ops:
  0.7 1.4 %shard_map.59.sent = f32[4,8,128]{2,1,0:T(8,128)S(1)} custom-call(bf16[19,32,8,128]{3,2,1,0:T(8,128)(2,1)} %adjoint.5, f32[8,2,32]{2,1,0:T(2,128)} %coefficients.1), custom_call_target="tpu_custom_call" | custom-call | tf_op jit(solution)/shard_map/pallas_call | solution.py:707
  2.0 0.5 %collective-permute-start = (f32[4,8,128]{2,1,0:T(8,128)S(1)}, f32[4,8,128]{2,1,0:T(8,128)S(1)}, u32[]{:S(2)}, u32[]{:S(2)}) collective-permute-start(f32[4,8,128]{2,1,0:T(8,128)S(1)} %shard_map.59.sent), channel_id=1, source_target_pairs={{0,1},{1,0},{2,3},{3,2},{4,5},{5,4},{6,7},{7,6},{8,9},{9,8},{10,11... | collective-permute-start | bytes 49160 | tf_op jit(solution)/shard_map/ppermute | solution.py:717
  2.5 0.3 %shard_map.61 = (f32[160,128]{1,0:T(8,128)S(1)}, f32[16,128]{1,0:T(8,128)S(1)}) custom-call(bf16[19,32,8,128]{3,2,1,0:T(8,128)(2,1)S(1)} %copy-done, f32[4,8,128]{2,1,0:T(8,128)S(1)} %shard_map.59.sent), custom_call_target="tpu_custom_call" | custom-call | tf_op jit(solution)/shard_map/pallas_call | solution.py:718
  2.8 0.6 %collective-permute-done.received = f32[4,8,128]{2,1,0:T(8,128)S(1)} collective-permute-done((f32[4,8,128]{2,1,0:T(8,128)S(1)}, f32[4,8,128]{2,1,0:T(8,128)S(1)}, u32[]{:S(2)}, u32[]{:S(2)}) %collective-permute-start) | collective-permute-done | bytes 16416 | tf_op jit(solution)/shard_map/ppermute | solution.py:717
  3.4 0.1 shard_map.62
  3.5 3.0 %collective-permute-start.1 = (bf16[176,128]{1,0:T(8,128)(2,1)S(1)}, bf16[176,128]{1,0:T(8,128)(2,1)S(1)}, u32[]{:S(2)}, u32[]{:S(2)}) collective-permute-start(bf16[176,128]{1,0:T(8,128)(2,1)S(1)} %get-tuple-element.23), channel_id=1, source_target_pairs={{0,2},{2,0},{1,3},{3,1},{4,6},{6,4},{5,7},{7,5},{8,10},{10,8},{9,1... | collective-permute-start | bytes 135176 | tf_op jit(solution)/shard_map/ppermute | solution.py:728
  6.4 1.5 %shard_map.60 = (f32[19,256,128]{2,1,0:T(8,128)S(1)}, f32[5,32,8,128]{3,2,1,0:T(8,128)S(1)}) custom-call(bf16[19,32,8,128]{3,2,1,0:T(8,128)(2,1)S(1)} %copy-done, bf16[19,32,8,128]{3,2,1,0:T(8,128)(2,1)} %forward_far.1, s32[32,8,128]{2,1,0:T(8,128)S(1)} %copy-done.1, f32[4,8,128]{2,1,0:T(8,128)S(1)} %collective-permute-done.received), custom_call_target="tpu_custom_call" | custom-call | tf_op jit(solution)/shard_map/pallas_call | solution.py:732
  7.9 0.5 %collective-permute-done.1.refs_0_ = bf16[176,128]{1,0:T(8,128)(2,1)S(1)} collective-permute-done((bf16[176,128]{1,0:T(8,128)(2,1)S(1)}, bf16[176,128]{1,0:T(8,128)(2,1)S(1)}, u32[]{:S(2)}, u32[]{:S(2)}) %collective-permute-start.1) | collective-permute-done | bytes 45088 | tf_op jit(solution)/shard_map/ppermute | solution.py:728
  8.5 0.2 shard_map.63
  8.6 2.1 %collective-permute-start.2 = (bf16[23,8,128]{2,1,0:T(8,128)(2,1)S(1)}, bf16[23,8,128]{2,1,0:T(8,128)(2,1)S(1)}, u32[]{:S(2)}, u32[]{:S(2)}) collective-permute-start(bf16[23,8,128]{2,1,0:T(8,128)(2,1)S(1)} %get-tuple-element.26), channel_id=1, source_target_pairs={{0,4},{1,5},{4,0},{5,1},{8,9},{9,8},{12,13},{13,12},{2,6},{3,7},{6... | collective-permute-start | bytes 141320 | tf_op jit(solution)/shard_map/ppermute | solution.py:759
  10.7 0.0 collective-permute-start.3
  10.7 0.5 %collective-permute-start.4 = (bf16[23,8,128]{2,1,0:T(8,128)(2,1)S(1)}, bf16[23,8,128]{2,1,0:T(8,128)(2,1)S(1)}, u32[]{:S(2)}, u32[]{:S(2)}) collective-permute-start(bf16[23,8,128]{2,1,0:T(8,128)(2,1)S(1)} %get-tuple-element.28), channel_id=1, source_target_pairs={{0,1},{1,0},{4,5},{5,4},{8,12},{9,13},{12,8},{13,9},{2,3},{3,2},{6... | collective-permute-start | bytes 141320 | tf_op jit(solution)/shard_map/ppermute | solution.py:759
  11.2 1.3 %shard_map.64 = (bf16[19,32,8,128]{3,2,1,0:T(8,128)(2,1)}, f32[8,8,128]{2,1,0:T(8,128)S(1)}) custom-call(f32[19,256,128]{2,1,0:T(8,128)S(1)} %get-tuple-element.24.pulled, f32[5,32,8,128]{3,2,1,0:T(8,128)S(1)} %get-tuple-element.19.flows, s32[32,8,128]{2,1,0:T(8,128)S(1)} %copy-done.1, f32[8,8,128]{2,1,0:T(8,128)S(1)} %get-tuple-element.25.levels), custom_call_target="tpu_custom_call" | custom-call | tf_op jit(solution)/shard_map/pallas_call | solution.py:762
  12.6 0.2 %collective-permute-done.2.refs_0_ = bf16[23,8,128]{2,1,0:T(8,128)(2,1)S(1)} collective-permute-done((bf16[23,8,128]{2,1,0:T(8,128)(2,1)S(1)}, bf16[23,8,128]{2,1,0:T(8,128)(2,1)S(1)}, u32[]{:S(2)}, u32[]{:S(2)}) %collective-permute-start.2) | collective-permute-done | bytes 47136 | tf_op jit(solution)/shard_map/ppermute | solution.py:759
  12.8 0.0 collective-permute-done.3.refs_1_
  12.8 0.0 collective-permute-done.4.refs_2_
  12.8 0.2 %shard_map.66 = (f32[32,128]{1,0:T(8,128)S(1)}, f32[4,8,32]{2,1,0:T(8,128)S(1)}) custom-call(f32[19,256,128]{2,1,0:T(8,128)S(1)} %get-tuple-element.24.pulled, f32[5,32,8,128]{3,2,1,0:T(8,128)S(1)} %get-tuple-element.19.flows, f32[2,8,8,128]{3,2,1,0:T(8,128)S(1)} %get-tuple-element.30.edges, f32[8,8,128]{2,1,0:T(8,128)S(1)} %get-tuple-element.25.levels, ...), custom_call_target="tpu_custom_call" | custom-call | tf_op jit(solution)/shard_map/pallas_call | solution.py:768
  13.0 0.0 collective-permute-start.5
  13.0 0.1 shard_map.67
  13.2 1.0 %collective-permute-done.5 = f32[4,8,32]{2,1,0:T(8,128)S(1)} collective-permute-done((f32[4,8,32]{2,1,0:T(8,128)S(1)}, f32[4,8,32]{2,1,0:T(8,128)S(1)}, u32[]{:S(2)}, u32[]{:S(2)}) %collective-permute-start.5) | collective-permute-done | bytes 4128 | tf_op jit(solution)/shard_map/ppermute | solution.py:771
  14.2 2.1 %collective-permute-start.6 = (f32[8,32]{1,0:T(8,128)S(1)}, f32[8,32]{1,0:T(8,128)S(1)}, u32[]{:S(2)}, u32[]{:S(2)}) collective-permute-start(f32[8,32]{1,0:T(8,128)S(1)} %fusion.2), channel_id=1, source_target_pairs={{0,2},{2,0},{1,3},{3,1},{4,6},{6,4},{5,7},{7,5},{8,10},{10,8},{9,1... | collective-permute-start | bytes 3080 | tf_op jit(solution)/shard_map/ppermute | solution.py:774
  16.3 1.3 %shard_map.65 = bf16[19,32,8,128]{3,2,1,0:T(8,128)(2,1)} custom-call(f32[19,256,128]{2,1,0:T(8,128)S(1)} %get-tuple-element.24.pulled, f32[5,32,8,128]{3,2,1,0:T(8,128)S(1)} %get-tuple-element.19.flows, s32[32,8,128]{2,1,0:T(8,128)S(1)} %copy-done.1, f32[8,8,128]{2,1,0:T(8,128)S(1)} %get-tuple-element.25.levels, ...), custom_call_target="tpu_custom_call", output_to_operand_aliasing={{}: (7, {})} | custom-call | tf_op jit(solution)/shard_map/pallas_call | solution.py:781
  17.5 0.3 %collective-permute-done.6 = f32[8,32]{1,0:T(8,128)S(1)} collective-permute-done((f32[8,32]{1,0:T(8,128)S(1)}, f32[8,32]{1,0:T(8,128)S(1)}, u32[]{:S(2)}, u32[]{:S(2)}) %collective-permute-start.6) | collective-permute-done | bytes 1056 | tf_op jit(solution)/shard_map/ppermute | solution.py:774
  17.9 0.6 %copy.8 = f32[8,2,32]{2,1,0:T(2,128)} copy(f32[8,2,32]{2,0,1:T(8,128)S(1)} %pad_maximum_fusion) | data formatting | bytes 4096
  (8 shorter events, 0.0 us)
Async XLA Ops:
  0.6 1.9 %copy-start = (bf16[19,32,8,128]{3,2,1,0:T(8,128)(2,1)S(1)}, bf16[19,32,8,128]{3,2,1,0:T(8,128)(2,1)}, u32[]{:S(2)}) copy-start(bf16[19,32,8,128]{3,2,1,0:T(8,128)(2,1)} %adjoint.5) | copy-start | bytes 3735556
  0.6 5.8 %copy-start.1 = (s32[32,8,128]{2,1,0:T(8,128)S(1)}, s32[32,8,128]{2,1,0:T(8,128)}, u32[]{:S(2)}) copy-start(s32[32,8,128]{2,1,0:T(8,128)} %kind.5) | copy-start | bytes 393220
  2.0 1.4 %collective-permute-start = (f32[4,8,128]{2,1,0:T(8,128)S(1)}, f32[4,8,128]{2,1,0:T(8,128)S(1)}, u32[]{:S(2)}, u32[]{:S(2)}) collective-permute-start(f32[4,8,128]{2,1,0:T(8,128)S(1)} %shard_map.59.sent), channel_id=1, source_target_pairs={{0,1},{1,0},{2,3},{3,2},{4,5},{5,4},{6,7},{7,6},{8,9},{9,8},{10,11... | collective-permute-start | bytes 49160 | tf_op jit(solution)/shard_map/ppermute | solution.py:717
  3.5 5.0 %collective-permute-start.1 = (bf16[176,128]{1,0:T(8,128)(2,1)S(1)}, bf16[176,128]{1,0:T(8,128)(2,1)S(1)}, u32[]{:S(2)}, u32[]{:S(2)}) collective-permute-start(bf16[176,128]{1,0:T(8,128)(2,1)S(1)} %get-tuple-element.23), channel_id=1, source_target_pairs={{0,2},{2,0},{1,3},{3,1},{4,6},{6,4},{5,7},{7,5},{8,10},{10,8},{9,1... | collective-permute-start | bytes 135176 | tf_op jit(solution)/shard_map/ppermute | solution.py:728
  8.6 4.2 %collective-permute-start.2 = (bf16[23,8,128]{2,1,0:T(8,128)(2,1)S(1)}, bf16[23,8,128]{2,1,0:T(8,128)(2,1)S(1)}, u32[]{:S(2)}, u32[]{:S(2)}) collective-permute-start(bf16[23,8,128]{2,1,0:T(8,128)(2,1)S(1)} %get-tuple-element.26), channel_id=1, source_target_pairs={{0,4},{1,5},{4,0},{5,1},{8,9},{9,8},{12,13},{13,12},{2,6},{3,7},{6... | collective-permute-start | bytes 141320 | tf_op jit(solution)/shard_map/ppermute | solution.py:759
  10.7 2.1 %collective-permute-start.3 = (bf16[23,8,128]{2,1,0:T(8,128)(2,1)S(1)}, bf16[23,8,128]{2,1,0:T(8,128)(2,1)S(1)}, u32[]{:S(2)}, u32[]{:S(2)}) collective-permute-start(bf16[23,8,128]{2,1,0:T(8,128)(2,1)S(1)} %get-tuple-element.27), channel_id=1, source_target_pairs={{0,1},{1,0},{4,8},{5,9},{8,4},{9,5},{12,13},{13,12},{2,3},{3,2},{6... | collective-permute-start | bytes 141320 | tf_op jit(solution)/shard_map/ppermute | solution.py:759
  10.7 2.1 %collective-permute-start.4 = (bf16[23,8,128]{2,1,0:T(8,128)(2,1)S(1)}, bf16[23,8,128]{2,1,0:T(8,128)(2,1)S(1)}, u32[]{:S(2)}, u32[]{:S(2)}) collective-permute-start(bf16[23,8,128]{2,1,0:T(8,128)(2,1)S(1)} %get-tuple-element.28), channel_id=1, source_target_pairs={{0,1},{1,0},{4,5},{5,4},{8,12},{9,13},{12,8},{13,9},{2,3},{3,2},{6... | collective-permute-start | bytes 141320 | tf_op jit(solution)/shard_map/ppermute | solution.py:759
  13.0 1.2 %collective-permute-start.5 = (f32[4,8,32]{2,1,0:T(8,128)S(1)}, f32[4,8,32]{2,1,0:T(8,128)S(1)}, u32[]{:S(2)}, u32[]{:S(2)}) collective-permute-start(f32[4,8,32]{2,1,0:T(8,128)S(1)} %get-tuple-element.33), channel_id=1, source_target_pairs={{0,1},{1,0},{2,3},{3,2},{4,5},{5,4},{6,7},{7,6},{8,9},{9,8},{10,11... | collective-permute-start | bytes 12296 | tf_op jit(solution)/shard_map/ppermute | solution.py:771
  14.2 3.7 %collective-permute-start.6 = (f32[8,32]{1,0:T(8,128)S(1)}, f32[8,32]{1,0:T(8,128)S(1)}, u32[]{:S(2)}, u32[]{:S(2)}) collective-permute-start(f32[8,32]{1,0:T(8,128)S(1)} %fusion.2), channel_id=1, source_target_pairs={{0,2},{2,0},{1,3},{3,1},{4,6},{6,4},{5,7},{7,5},{8,10},{10,8},{9,1... | collective-permute-start | bytes 3080 | tf_op jit(solution)/shard_map/ppermute | solution.py:774

commit v6 on v5

--- a/solution.py
+++ b/solution.py
@@ -211,22 +211,40 @@
     return pl.ds(pl.multiple_of(x * 8, 8), 8) if not isinstance(x, int) else slice(x * 8, x * 8 + 8)
 
 
-def pack_z(adjoint, coefficients, out, faces, coarse, semaphores):
-    core = lax.axis_index("gz")
-    copies = [pltpu.make_async_copy(coefficients, coarse, semaphores.at[5])]
+def y_sides():
+    return ((YM, 7), (YP, 0))
+
+
+def pack_z(directions, adjoint, coefficients, out, lines, strips, faces, coarse, semaphores):
+    core, side = lax.axis_index("gz"), lax.axis_index("gy")
+    copies = [pltpu.make_async_copy(coefficients, coarse, semaphores.at[0])]
     for k in range(5):
         q = ZM[k] + core * (ZP[k] - ZM[k])
-        copies.append(pltpu.make_async_copy(adjoint.at[q], faces.at[k], semaphores.at[k]))
+        copies.append(pltpu.make_async_copy(adjoint.at[q], faces.at[k], semaphores.at[1 + k]))
+    for n in range(directions):
+        for k in range(5):
+            q = YM[k] + (side if directions == 1 else n) * (YP[k] - YM[k])
+            slot = 5 * n + k
+            copies.append(
+                pltpu.make_async_copy(adjoint.at[q], strips.at[slot], semaphores.at[6 + slot])
+            )
     for copy in copies:
         copy.start()
     lanes = iota(1)
     count = coefficients.shape[2]
+    copies[0].wait()
     out[2] = jnp.zeros((8, 128), f32)
     out[3] = jnp.zeros((8, 128), f32)
-    for copy in copies:
-        copy.wait()
     for j in range(2):
         out[2 + j, :, 0:count] = coarse[:, j, :]
+    lines[...] = jnp.dot(
+        jnp.concatenate([out[2], out[3]], axis=0),
+        jnp.concatenate([basis_along_z(count), jnp.zeros((128 - count, 128), f32)], axis=0),
+        precision=highest,
+        preferred_element_type=f32,
+    )
+    for copy in copies[1:]:
+        copy.wait()
     for which, source in enumerate((127, 0)):
 
         @pl.when(core == which)
@@ -247,83 +265,49 @@
                 out[group] = tile
 
 
-def y_sides(directions):
-    return ((YM, 7), (YP, 0))
-
-
-def gather_rows(directions, count, adjoint, sent, *refs):
-    *outs, lines, plane = refs
-    lines[...] = jnp.dot(
-        jnp.concatenate([sent[2], sent[3]], axis=0),
-        jnp.concatenate([basis_along_z(count), jnp.zeros((128 - count, 128), f32)], axis=0),
-        precision=highest,
-        preferred_element_type=f32,
-    )
+def pack_y(directions, strips, sent, lines, *refs):
+    outs_y, outs_yz, plane = refs[:directions], refs[directions:-1], refs[-1]
+    core, side = lax.axis_index("gz"), lax.axis_index("gy")
     lanes = lax.broadcasted_iota(jnp.int32, (32, 128), 1)
 
-    def emit(components, row, out):
+    def emit(components, row, j, first, out, out_yz):
+        edges = {}
         for k, q in enumerate(components):
             for x in range(32):
-                plane[x * 8 : x * 8 + 8, :] = adjoint[q, x].astype(f32)
-            rows = plane[pl.ds(row, 32, stride=8), :]
-            step = VELOCITY[q][2]
-            if step > 0:
-                rows = jnp.where(lanes == 127, 0.0, pltpu.roll(rows, 127, 1))
-            elif step < 0:
-                rows = jnp.where(lanes == 0, 0.0, pltpu.roll(rows, 1, 1))
-            out[k * 32 : k * 32 + 32, :] = rows
-
-    sides = y_sides(directions)
-    if directions == 1:
-        side = lax.axis_index("gy")
-        for n in range(2):
-            pl.when(side == n)(functools.partial(emit, *sides[n], outs[0]))
-    else:
-        for n in range(2):
-            emit(*sides[n], outs[n])
-
-
-def pack_y(directions, count, received, own_lines, *refs):
-    sources, outs, lines = refs[:directions], refs[directions:-1], refs[-1]
-    core = lax.axis_index("gz")
-    lanes = lax.broadcasted_iota(jnp.int32, (32, 128), 1)
-    sublanes = lax.broadcasted_iota(jnp.int32, (32, 128), 0)
-    rim_z = rim_along_z(core, count)
-    at_rim = iota(1) == core * (count - 1)
-    for j in range(2):
-        rim = jnp.sum(jnp.where(at_rim, received[2 + j], 0.0), axis=1, keepdims=True)
-        lines[8 * j : 8 * j + 8, :] = own_lines[8 * j : 8 * j + 8, :] + rim * rim_z
-
-    def emit(components, row, j, source, out):
+                plane[k, x * 8 : x * 8 + 8, :] = strips[first + k, x].astype(f32)
         for k, q in enumerate(components):
-            rows = source[k * 32 : k * 32 + 32, :]
+            rows = plane[k, pl.ds(row, 32, stride=8), :]
             step = VELOCITY[q][2]
             if step:
-                slot = (ZP if step > 0 else ZM).index(q) * 32
-                group, lane = slot // 128, slot % 128
-                spread = jnp.broadcast_to(received[group, row : row + 1, :], (32, 128))
-                column = jnp.sum(jnp.where(lanes == sublanes + lane, spread, 0.0), axis=1, keepdims=True)
-                column = jnp.where(core == (0 if step > 0 else 1), column, 0.0)
-                rows = rows + jnp.where(lanes == (127 if step > 0 else 0), column, 0.0)
+                rows = pltpu.roll(rows, 127 if step > 0 else 1, 1)
+                edge = lanes == (127 if step > 0 else 0)
+                edges[step] = jnp.where(edge, rows, 0.0)
+                rows = jnp.where(edge, 0.0, rows)
             out[k * 32 : k * 32 + 32, :] = rows.astype(bf16)
+        out_yz[0:32, :] = jnp.where(core == 1, edges[1], edges[-1])
+        out_yz[32:40, :] = sent[2 + j]
         line = lines[8 * j : 8 * j + 8, :]
         high = line.astype(bf16)
         out[LINE_ROWS:STRIP, :] = jnp.concatenate(
             [high, (line - high.astype(f32)).astype(bf16)], axis=0
         )
 
-    sides = y_sides(directions)
-    if directions == 1:
-        side = lax.axis_index("gy")
-        for n in range(2):
-            pl.when(side == n)(functools.partial(emit, *sides[n], 1 - n, sources[0], outs[0]))
-    else:
-        for n in range(2):
-            emit(*sides[n], 1 - n, sources[n], outs[n])
+    for n, (components, row) in enumerate(y_sides()):
+        if directions == 1:
+            work = functools.partial(emit, components, row, 1 - n, 0, outs_y[0], outs_yz[0])
+            pl.when(side == n)(work)
+        else:
+            emit(components, row, 1 - n, 5 * n, outs_y[n], outs_yz[n])
+
+
+def add_rim(line, coarse, core, count):
+    rim = jnp.sum(jnp.where(iota(1) == core * (count - 1), coarse, 0.0), axis=1, keepdims=True)
+    return line + rim * rim_along_z(core, count)
 
 
 def pull_zy(
-    adjoint, forward_far, kind, received, pulled, flows, columns, forward, semaphores
+    count, adjoint, forward_far, kind_far, received, own_lines,
+    pulled, flows, lines, kind, columns, forward, semaphores,
 ):
     copies = [
         pltpu.make_async_copy(
@@ -331,10 +315,15 @@
         )
         for n in range(4)
     ]
+    copies.append(pltpu.make_async_copy(kind_far, kind, semaphores.at[4]))
     for copy in copies:
         copy.start()
     core = lax.axis_index("gz")
     load_columns(core, received, columns)
+    for j in range(2):
+        lines[8 * j : 8 * j + 8, :] = add_rim(
+            own_lines[8 * j : 8 * j + 8, :], received[2 + j], core, count
+        )
     sublanes = iota(0)
 
     def step(x, carry):
@@ -358,25 +347,33 @@
         return carry
 
     lax.fori_loop(0, 32, step, 0, unroll=4)
-    for n, copy in enumerate(copies):
-        copy.wait()
+    copies[4].wait()
+    for n in range(4):
+        copies[n].wait()
         lax.fori_loop(8 * n, 8 * n + 8, flow, 0, unroll=4)
 
 
-def pack_x(directions, unpatched, flows, lines, *refs):
-    received = refs[:directions]
-    pulled, *outs, edges, levels, extra = refs[directions:]
+def pack_x(directions, count, unpatched, flows, lines, *refs):
+    received = list(zip(refs[:directions], refs[directions : 2 * directions]))
+    pulled, *outs, edges, levels, extra = refs[2 * directions :]
+    core = lax.axis_index("gz")
     del unpatched
     side = lax.axis_index("gy")
     place = lax.rem(lax.axis_index("gx"), SLOTS)
 
-    def patch(components, row, strip):
+    def patch(components, row, buffers):
+        strip, edge = buffers
         for k, q in enumerate(components):
-            pulled[q, pl.ds(row, 32, stride=8), :] = strip[k * 32 : k * 32 + 32, :].astype(f32)
-
-    def outer_line(strip):
+            rows = strip[k * 32 : k * 32 + 32, :].astype(f32)
+            step = VELOCITY[q][2]
+            if step:
+                rows = rows + jnp.where(core == (0 if step > 0 else 1), edge[0:32, :], 0.0)
+            pulled[q, pl.ds(row, 32, stride=8), :] = rows
+
+    def outer_line(buffers):
+        strip, edge = buffers
         parts = strip[LINE_ROWS:STRIP, :].astype(f32)
-        return parts[0:8] + parts[8:16]
+        return add_rim(parts[0:8] + parts[8:16], edge[32:40, :], core, count)
 
     if directions == 1:
         pl.when(side == 0)(lambda: patch(YP, 7, received[0]))
@@ -560,8 +557,8 @@
     return tiles[0]
 
 
-def project(pulled, flows, edges, levels, *refs):
-    inner, folded, rim = refs[SLOTS:]
+def project(count, pulled, flows, edges, levels, *refs):
+    inner, folded, handed = refs[SLOTS:]
     core = lax.axis_index("gz")
     low, high = along_x(refs[:SLOTS])
     totals = [inner[i] for i in range(8)]
@@ -608,25 +605,14 @@
                 alpha, beta = alpha + more[0], beta + more[1]
             add(block, position, alpha, beta)
     lanes = iota(1)
-    count = rim.shape[2]
     rim_z = rim_along_z(core, count)
     for j in range(4):
         sums = fold_rows(totals, basis_along_y(j - 1))
         folded[8 * j : 8 * j + 8, :] = sums
         across = jnp.sum(sums * rim_z, axis=1, keepdims=True)
-        rim[j] = jnp.where(lanes == core * (count - 1), across, 0.0)[:, 0:count]
-
-
-def fold_along_z(folded, out):
-    result = lax.dot_general(
-        folded[...],
-        basis_along_z(out.shape[2]),
-        (((1,), (1,)), ((), ())),
-        precision=highest,
-        preferred_element_type=f32,
-    )
-    for j in range(4):
-        out[j] = result[8 * j : 8 * j + 8]
+        handed[j] = jnp.where(lanes == core * (count - 1), across, 0.0)
+        if j in (0, 3):
+            handed[4 + j // 3] = sums
 
 
 def collide_outside(pulled, flows, kind, levels, *refs):
@@ -680,6 +666,38 @@
         copy.wait()
 
 
+def relay(directions, taken, handed, *outs):
+    if directions == 1:
+        side = lax.axis_index("gy")
+        outs[0][0] = taken[5 - side]
+        outs[0][1] = handed[3 - 3 * side]
+    else:
+        for n in range(2):
+            outs[n][0] = taken[5 - n]
+            outs[n][1] = handed[3 - 3 * n]
+
+
+def finish(folded, rims, *refs):
+    others, out = refs[:-1], refs[-1]
+    count = out.shape[2]
+    if len(others) == 1:
+        side = lax.axis_index("gy")
+        from_low = [jnp.where(side == 1, others[0][n], 0.0) for n in range(2)]
+        from_high = [jnp.where(side == 0, others[0][n], 0.0) for n in range(2)]
+    else:
+        from_low, from_high = [[other[n] for n in range(2)] for other in others]
+    sums = jnp.concatenate([folded[8:16, :] + from_low[0], folded[16:24, :] + from_high[0]], axis=0)
+    result = lax.dot_general(
+        sums,
+        basis_along_z(count),
+        (((1,), (1,)), ((), ())),
+        precision=highest,
+        preferred_element_type=f32,
+    )
+    out[:, 0, :] = result[0:8] + (rims[1] + from_low[1])[:, 0:count]
+    out[:, 1, :] = result[8:16] + (rims[2] + from_high[1])[:, 0:count]
+
+
 def pairs(count, slot):
     partner = {}
     for i in range(slot, count - 1, SLOTS):
@@ -704,57 +722,64 @@
     up = [(i, i + 1) for i in range(count_y - 1)]
     down = [(i + 1, i) for i in range(count_y - 1)]
 
-    sent_z = kernel_call(
-        pack_z,
-        shape((4,) + tile, f32),
+    strips = shape((5 * directions,) + adjoint.shape[1:], bf16)
+    sent_z, lines, strips = kernel_call(
+        functools.partial(pack_z, directions),
+        [shape((4,) + tile, f32), shape((16, 128), f32), strips],
         [
             pltpu.VMEM((5,) + adjoint.shape[1:], bf16),
             pltpu.VMEM(coefficients.shape, f32),
-            pltpu.SemaphoreType.DMA((6,)),
+            pltpu.SemaphoreType.DMA((6 + 5 * directions,)),
         ],
         in_specs=[pl.BlockSpec(memory_space=pltpu.HBM)] * 2,
     )(*(pltpu.with_memory_space_constraint(a, pltpu.HBM) for a in (adjoint, coefficients)))
+    sent = kernel_call(
+        functools.partial(pack_y, directions),
+        [shape((STRIP, 128), bf16)] * directions + [shape((40, 128), f32)] * directions,
+        [pltpu.VMEM((5, 256, 128), f32)],
+    )(strips, sent_z, lines)
     received_z = lax.ppermute(sent_z, "gz", swap)
-    *rows, lines = kernel_call(
-        functools.partial(gather_rows, directions, count),
-        [shape((LINE_ROWS, 128), f32)] * directions + [shape((16, 128), f32)],
-        [pltpu.VMEM((256, 128), f32)],
-    )(adjoint, sent_z)
-    *sent_y, lines = kernel_call(
-        functools.partial(pack_y, directions, count),
-        [shape((STRIP, 128), bf16)] * directions + [shape((16, 128), f32)],
-    )(received_z, lines, *rows)
-    if directions == 1:
-        received_y = [lax.ppermute(sent_y[0], "gy", swap)]
-    else:
-        received_y = [lax.ppermute(sent_y[0], "gy", up), lax.ppermute(sent_y[1], "gy", down)]
-
-    pulled, flows = kernel_call(
-        pull_zy,
-        [shape((19, 256, 128), f32), shape((5,) + kind.shape, f32)],
+    routes = [swap] if directions == 1 else [up, down]
+    crossed = [
+        [(a * 2 + core, b * 2 + 1 - core) for a, b in route for core in range(2)] for route in routes
+    ]
+    received_y = [lax.ppermute(sent[n], "gy", route) for n, route in enumerate(routes)]
+    received_yz = [
+        lax.ppermute(sent[directions + n], ("gy", "gz"), route) for n, route in enumerate(crossed)
+    ]
+
+    pulled, flows, lines, kind = kernel_call(
+        functools.partial(pull_zy, count),
+        [
+            shape((19, 256, 128), f32),
+            shape((5,) + kind.shape, f32),
+            shape((16, 128), f32),
+            shape(kind.shape, jnp.int32),
+        ],
         [
             pltpu.VMEM((2, 2) + tile, f32),
             pltpu.VMEM(forward.shape, bf16),
-            pltpu.SemaphoreType.DMA((4,)),
+            pltpu.SemaphoreType.DMA((5,)),
         ],
         in_specs=[
-            pl.BlockSpec(memory_space=pltpu.HBM if n == 1 else pltpu.VMEM) for n in range(4)
+            pl.BlockSpec(memory_space=pltpu.HBM if n in (1, 2) else pltpu.VMEM) for n in range(5)
         ],
     )(
         adjoint,
         pltpu.with_memory_space_constraint(forward, pltpu.HBM),
-        kind,
+        pltpu.with_memory_space_constraint(kind, pltpu.HBM),
         received_z,
+        lines,
     )
 
     pulled, *sent_x, edges, levels = kernel_call(
-        functools.partial(pack_x, directions),
+        functools.partial(pack_x, directions, count),
         [pulled]
         + [shape((BUNDLE,) + tile, bf16)] * SLOTS
         + [shape((2, 8) + tile, f32), shape((8,) + tile, f32)],
         [pltpu.VMEM((32, 128), f32)],
         aliases={0: 0},
-    )(pulled, flows, lines, *received_y)
+    )(pulled, flows, lines, *received_y, *received_yz)
     received_x = [
         lax.ppermute(sent, ("gx", "gz"), pairs(count_x, slot)) for slot, sent in enumerate(sent_x)
     ]
@@ -765,18 +790,15 @@
         [pltpu.VMEM((19, INNER) + tile, bf16), pltpu.SemaphoreType.DMA((INNER // 8,))],
         out_specs=[pl.BlockSpec(memory_space=pltpu.HBM), pl.BlockSpec(memory_space=pltpu.VMEM)],
     )(pulled, flows, kind, levels)
-    folded, rim = kernel_call(project, [shape((32, 128), f32), shape((4, 8, count), f32)])(
-        pulled, flows, edges, levels, *received_x, totals
-    )
-    other_rim = lax.ppermute(rim, "gz", swap)
-    whole = kernel_call(fold_along_z, shape(rim.shape, f32))(folded) + other_rim
-    if directions == 1:
-        other = lax.ppermute(jnp.where(side == 0, whole[3], whole[0]), "gy", swap)
-        from_low = jnp.where(side == 1, other, 0.0)
-        from_high = jnp.where(side == 0, other, 0.0)
-    else:
-        from_low = lax.ppermute(whole[3], "gy", up)
-        from_high = lax.ppermute(whole[0], "gy", down)
+    folded, handed = kernel_call(
+        functools.partial(project, count), [shape((32, 128), f32), shape((6,) + tile, f32)]
+    )(pulled, flows, edges, levels, *received_x, totals)
+    taken = lax.ppermute(handed, "gz", swap)
+    relayed = kernel_call(
+        functools.partial(relay, directions), [shape((2,) + tile, f32)] * directions
+    )(taken, handed)
+    crossed = [[(a * 2 + c, b * 2 + 1 - c) for a, b in route for c in range(2)] for route in routes]
+    others = [lax.ppermute(sent, ("gy", "gz"), route) for sent, route in zip(relayed, crossed)]
     in_hbm = pl.BlockSpec(memory_space=pltpu.HBM)
     prior = kernel_call(
         collide_outside,
@@ -786,7 +808,10 @@
         in_specs=[pl.BlockSpec(memory_space=pltpu.VMEM)] * (4 + SLOTS) + [in_hbm],
         out_specs=in_hbm,
     )(pulled, flows, kind, levels, *received_x, prior)
-    return prior, jnp.stack([whole[1] + from_low, whole[2] + from_high], axis=1)
+    gradient = kernel_call(finish, shape(coefficients.shape, f32))(
+        folded, taken, *others
+    )
+    return prior, gradient
 
 
 def solution(mesh):

time: 18.6 us -> 18.3 us (0.984)
  starting transfers between devices: 8.17 us -> 6.66 us
  waiting for transfers between devices: 2.69 us -> 3.66 us
  Pallas kernels: 6.28 us -> 7.06 us
  local copies, waits for them, and re-layouts: 0.61 us -> 0.01 us
    pallas_call x7, Pallas kernels: 3.71 us -> 4.49 us  [the longest x1 1.69 us: per_device(): kernel_call(functools.partial(pull_zy, count), [shape((19, 256, 128), f32...]
    ppermute x3 -> x4, starting transfers between devices: 5.03 us -> 4.3 us  [the longest x1 3 us: per_device(): lax.ppermute(sent[n], 'gy', route)]
    unnamed x5 -> x2, local copies, waits for them, and re-layouts: 0.61 us -> 0.01 us
    ppermute x3, starting transfers between devices: 2.62 us -> 2.17 us  [per_device(): lax.ppermute(sent, ('gx', 'gz'), pairs(count_x, slot))]
    ppermute x3, waiting for transfers between devices: 0.22 us -> 0.65 us  [per_device(): lax.ppermute(sent, ('gx', 'gz'), pairs(count_x, slot))]
    ppermute x1, waiting for transfers between devices: 0.57 us -> 0.99 us  [per_device(): received_z = lax.ppermute(sent_z, 'gz', swap)]
    ppermute x1, starting transfers between devices: 0.52 us -> 0.19 us  [per_device(): received_z = lax.ppermute(sent_z, 'gz', swap)]
    ppermute x3 -> x4, waiting for transfers between devices: 1.9 us -> 2.02 us  [the longest x1 1.18 us: per_device(): taken = lax.ppermute(handed, 'gz', swap)]
  transfers between devices with their start and end apart: 7 -> 8, of which waited for: 5 -> 5; matrix products, arithmetic and copies ran while one was open for 0% -> 0% of each run, Pallas kernels for 24% -> 24%
where the time goes in v6:
time: 18.3 us; the launch traced here: 18.1 us
  Pallas kernels  7.06 us (39%)
  starting transfers between devices  6.66 us (36%)
  waiting for transfers between devices  3.66 us (20%)
  between operations  0.7 us (4%)
    ppermute x1, starting transfers between devices, per_device(): lax.ppermute(sent[n], 'gy', route)  3 us
    ppermute x3, starting transfers between devices, per_device(): lax.ppermute(sent, ('gx', 'gz'), pairs(count_x, slot))  2.17 us
    pallas_call x1, Pallas kernels, per_device(): kernel_call(functools.partial(pull_zy, count), [shape((19, 256, 128), f32...  1.69 us
    pallas_call x1, Pallas kernels, per_device(): kernel_call(functools.partial(pack_z, directions), [shape((4,) + tile, f3...  1.53 us
    pallas_call x1, Pallas kernels, per_device(): kernel_call(collide_inside, [shape(adjoint.shape, bf16), shape((8,) + til...  1.31 us
    ppermute x1, starting transfers between devices, per_device(): lax.ppermute(sent, ('gy', 'gz'), route)  1.28 us
    pallas_call x1, Pallas kernels, per_device(): kernel_call(collide_outside, shape(adjoint.shape, bf16), [pltpu.VMEM((19,...  1.27 us
    ppermute x1, waiting for transfers between devices, per_device(): taken = lax.ppermute(handed, 'gz', swap)  1.18 us
  transfers between devices with their start and end apart: 8, of which 5 were waited for; matrix products, arithmetic and copies ran while one was open for 0% of the time, Pallas kernels for 24%

profile of v6, /device:TPU:0, one launch (start us, length us, event | category | flops | bytes accessed | tf_op | source)
XLA Modules:
  0.0 18.1 jit_solution(18145563599864568530)
XLA Ops:
  0.6 1.5 %shard_map.59 = (f32[4,8,128]{2,1,0:T(8,128)S(1)}, f32[16,128]{1,0:T(8,128)S(1)}, bf16[5,32,8,128]{3,2,1,0:T(8,128)(2,1)S(1)}) custom-call(bf16[19,32,8,128]{3,2,1,0:T(8,128)(2,1)} %adjoint.3, f32[8,2,32]{2,1,0:T(2,128)} %coefficients.1), custom_call_target="tpu_custom_call" | custom-call | tf_op jit(solution)/shard_map/pallas_call | solution.py:726
  2.2 0.1 shard_map.61
  2.3 3.0 %collective-permute-start.1 = (bf16[176,128]{1,0:T(8,128)(2,1)S(1)}, bf16[176,128]{1,0:T(8,128)(2,1)S(1)}, u32[]{:S(2)}, u32[]{:S(2)}) collective-permute-start(bf16[176,128]{1,0:T(8,128)(2,1)S(1)} %get-tuple-element.27), channel_id=1, source_target_pairs={{0,2},{2,0},{1,3},{3,1},{4,6},{6,4},{5,7},{7,5},{8,10},{10,8},{9,1... | collective-permute-start | bytes 135176 | tf_op jit(solution)/shard_map/ppermute | solution.py:746
  5.3 0.0 collective-permute-start.2
  5.3 0.2 %collective-permute-start = (f32[4,8,128]{2,1,0:T(8,128)S(1)}, f32[4,8,128]{2,1,0:T(8,128)S(1)}, u32[]{:S(2)}, u32[]{:S(2)}) collective-permute-start(f32[4,8,128]{2,1,0:T(8,128)S(1)} %get-tuple-element.21.sent), channel_id=1, source_target_pairs={{0,1},{1,0},{2,3},{3,2},{4,5},{5,4},{6,7},{7,6},{8,9},{9,8},{10,11... | collective-permute-start | bytes 49160 | tf_op jit(solution)/shard_map/ppermute | solution.py:741
  5.5 1.0 %collective-permute-done.received = f32[4,8,128]{2,1,0:T(8,128)S(1)} collective-permute-done((f32[4,8,128]{2,1,0:T(8,128)S(1)}, f32[4,8,128]{2,1,0:T(8,128)S(1)}, u32[]{:S(2)}, u32[]{:S(2)}) %collective-permute-start) | collective-permute-done | bytes 16416 | tf_op jit(solution)/shard_map/ppermute | solution.py:741
  6.5 1.7 %shard_map.60 = (f32[19,256,128]{2,1,0:T(8,128)S(1)}, f32[5,32,8,128]{3,2,1,0:T(8,128)S(1)}, f32[16,128]{1,0:T(8,128)S(1)}, s32[32,8,128]{2,1,0:T(8,128)S(1)}) custom-call(bf16[19,32,8,128]{3,2,1,0:T(8,128)(2,1)S(1)} %copy-done, bf16[19,32,8,128]{3,2,1,0:T(8,128)(2,1)} %forward_far.1, s32[32,8,128]{2,1,0:T(8,128)} %kind_far.1, ...), custom_call_target="tpu_custom_call" | custom-call | tf_op jit(solution)/shard_map/pallas_call | solution.py:751
  8.2 0.3 %collective-permute-done.2.refs_1_ = f32[40,128]{1,0:T(8,128)S(1)} collective-permute-done((f32[40,128]{1,0:T(8,128)S(1)}, f32[40,128]{1,0:T(8,128)S(1)}, u32[]{:S(2)}, u32[]{:S(2)}) %collective-permute-start.2) | collective-permute-done | bytes 20512 | tf_op jit(solution)/shard_map/ppermute | solution.py:748
  8.5 0.0 collective-permute-done.1.refs_0_
  8.5 0.2 shard_map.62
  8.7 1.7 %collective-permute-start.3 = (bf16[23,8,128]{2,1,0:T(8,128)(2,1)S(1)}, bf16[23,8,128]{2,1,0:T(8,128)(2,1)S(1)}, u32[]{:S(2)}, u32[]{:S(2)}) collective-permute-start(bf16[23,8,128]{2,1,0:T(8,128)(2,1)S(1)} %get-tuple-element.32), channel_id=1, source_target_pairs={{0,4},{1,5},{4,0},{5,1},{8,9},{9,8},{12,13},{13,12},{2,6},{3,7},{6... | collective-permute-start | bytes 141320 | tf_op jit(solution)/shard_map/ppermute | solution.py:784
  10.3 0.1 collective-permute-start.4
  10.4 0.4 %collective-permute-start.5 = (bf16[23,8,128]{2,1,0:T(8,128)(2,1)S(1)}, bf16[23,8,128]{2,1,0:T(8,128)(2,1)S(1)}, u32[]{:S(2)}, u32[]{:S(2)}) collective-permute-start(bf16[23,8,128]{2,1,0:T(8,128)(2,1)S(1)} %get-tuple-element.34), channel_id=1, source_target_pairs={{0,1},{1,0},{4,5},{5,4},{8,12},{9,13},{12,8},{13,9},{2,3},{3,2},{6... | collective-permute-start | bytes 141320 | tf_op jit(solution)/shard_map/ppermute | solution.py:784
  10.9 1.3 %shard_map.63 = (bf16[19,32,8,128]{3,2,1,0:T(8,128)(2,1)}, f32[8,8,128]{2,1,0:T(8,128)S(1)}) custom-call(f32[19,256,128]{2,1,0:T(8,128)S(1)} %get-tuple-element.29.pulled, f32[5,32,8,128]{3,2,1,0:T(8,128)S(1)} %get-tuple-element.24.flows, s32[32,8,128]{2,1,0:T(8,128)S(1)} %get-tuple-element.30.kind, f32[8,8,128]{2,1,0:T(8,128)S(1)} %get-tuple-element.31.levels), custom_call_target="tpu_custom_call" | custom-call | tf_op jit(solution)/shard_map/pallas_call | solution.py:787
  12.2 0.6 %collective-permute-done.3.refs_0_ = bf16[23,8,128]{2,1,0:T(8,128)(2,1)S(1)} collective-permute-done((bf16[23,8,128]{2,1,0:T(8,128)(2,1)S(1)}, bf16[23,8,128]{2,1,0:T(8,128)(2,1)S(1)}, u32[]{:S(2)}, u32[]{:S(2)}) %collective-permute-start.3) | collective-permute-done | bytes 47136 | tf_op jit(solution)/shard_map/ppermute | solution.py:784
  12.8 0.0 collective-permute-done.4.refs_1_
  12.8 0.0 collective-permute-done.5.refs_2_
  12.8 0.2 %shard_map.65 = (f32[32,128]{1,0:T(8,128)S(1)}, f32[6,8,128]{2,1,0:T(8,128)S(1)}) custom-call(f32[19,256,128]{2,1,0:T(8,128)S(1)} %get-tuple-element.29.pulled, f32[5,32,8,128]{3,2,1,0:T(8,128)S(1)} %get-tuple-element.24.flows, f32[2,8,8,128]{3,2,1,0:T(8,128)S(1)} %get-tuple-element.36.edges, f32[8,8,128]{2,1,0:T(8,128)S(1)} %get-tuple-element.31.levels, ...), custom_call_target="tpu_custom_call" | custom-call | tf_op jit(solution)/shard_map/pallas_call | solution.py:793
  13.0 0.0 collective-permute-start.6
  13.1 1.2 %collective-permute-done.6.taken.rims = f32[6,8,128]{2,1,0:T(8,128)S(1)} collective-permute-done((f32[6,8,128]{2,1,0:T(8,128)S(1)}, f32[6,8,128]{2,1,0:T(8,128)S(1)}, u32[]{:S(2)}, u32[]{:S(2)}) %collective-permute-start.6) | collective-permute-done | bytes 24608 | tf_op jit(solution)/shard_map/ppermute | solution.py:796
  14.3 1.3 %collective-permute-start.7 = (f32[2,8,128]{2,1,0:T(8,128)S(1)}, f32[2,8,128]{2,1,0:T(8,128)S(1)}, u32[]{:S(2)}, u32[]{:S(2)}) collective-permute-start(f32[2,8,128]{2,1,0:T(8,128)S(1)} %shard_map.66), channel_id=1, source_target_pairs={{0,3},{1,2},{2,1},{3,0},{4,7},{5,6},{6,5},{7,4},{8,11},{9,10},{10,... | collective-permute-start | bytes 24584 | tf_op jit(solution)/shard_map/ppermute | solution.py:801
  15.5 1.3 %shard_map.64 = bf16[19,32,8,128]{3,2,1,0:T(8,128)(2,1)} custom-call(f32[19,256,128]{2,1,0:T(8,128)S(1)} %get-tuple-element.29.pulled, f32[5,32,8,128]{3,2,1,0:T(8,128)S(1)} %get-tuple-element.24.flows, s32[32,8,128]{2,1,0:T(8,128)S(1)} %get-tuple-element.30.kind, f32[8,8,128]{2,1,0:T(8,128)S(1)} %get-tuple-element.31.levels, ...), custom_call_target="tpu_custom_call", output_to_operand_aliasing={{}: (7, {})} | custom-call | tf_op jit(solution)/shard_map/pallas_call | solution.py:803
  16.8 0.5 %collective-permute-done.7.refs_0_ = f32[2,8,128]{2,1,0:T(8,128)S(1)} collective-permute-done((f32[2,8,128]{2,1,0:T(8,128)S(1)}, f32[2,8,128]{2,1,0:T(8,128)S(1)}, u32[]{:S(2)}, u32[]{:S(2)}) %collective-permute-start.7) | collective-permute-done | bytes 8224 | tf_op jit(solution)/shard_map/ppermute | solution.py:801
  17.3 0.8 %shard_map.67 = f32[8,2,32]{2,1,0:T(2,128)} custom-call(f32[32,128]{1,0:T(8,128)S(1)} %get-tuple-element.38.folded, f32[6,8,128]{2,1,0:T(8,128)S(1)} %collective-permute-done.6.taken.rims, f32[2,8,128]{2,1,0:T(8,128)S(1)} %collective-permute-done.7.refs_0_), custom_call_target="tpu_custom_call" | custom-call | tf_op jit(solution)/shard_map/pallas_call | solution.py:811
  (3 shorter events, 0.0 us)
Async XLA Ops:
  0.6 5.9 %copy-start = (bf16[19,32,8,128]{3,2,1,0:T(8,128)(2,1)S(1)}, bf16[19,32,8,128]{3,2,1,0:T(8,128)(2,1)}, u32[]{:S(2)}) copy-start(bf16[19,32,8,128]{3,2,1,0:T(8,128)(2,1)} %adjoint.3) | copy-start | bytes 3735556
  2.3 6.2 %collective-permute-start.1 = (bf16[176,128]{1,0:T(8,128)(2,1)S(1)}, bf16[176,128]{1,0:T(8,128)(2,1)S(1)}, u32[]{:S(2)}, u32[]{:S(2)}) collective-permute-start(bf16[176,128]{1,0:T(8,128)(2,1)S(1)} %get-tuple-element.27), channel_id=1, source_target_pairs={{0,2},{2,0},{1,3},{3,1},{4,6},{6,4},{5,7},{7,5},{8,10},{10,8},{9,1... | collective-permute-start | bytes 135176 | tf_op jit(solution)/shard_map/ppermute | solution.py:746
  5.3 3.2 %collective-permute-start.2 = (f32[40,128]{1,0:T(8,128)S(1)}, f32[40,128]{1,0:T(8,128)S(1)}, u32[]{:S(2)}, u32[]{:S(2)}) collective-permute-start(f32[40,128]{1,0:T(8,128)S(1)} %get-tuple-element.28), channel_id=1, source_target_pairs={{0,3},{1,2},{2,1},{3,0},{4,7},{5,6},{6,5},{7,4},{8,11},{9,10},{10,... | collective-permute-start | bytes 61448 | tf_op jit(solution)/shard_map/ppermute | solution.py:748
  5.3 1.2 %collective-permute-start = (f32[4,8,128]{2,1,0:T(8,128)S(1)}, f32[4,8,128]{2,1,0:T(8,128)S(1)}, u32[]{:S(2)}, u32[]{:S(2)}) collective-permute-start(f32[4,8,128]{2,1,0:T(8,128)S(1)} %get-tuple-element.21.sent), channel_id=1, source_target_pairs={{0,1},{1,0},{2,3},{3,2},{4,5},{5,4},{6,7},{7,6},{8,9},{9,8},{10,11... | collective-permute-start | bytes 49160 | tf_op jit(solution)/shard_map/ppermute | solution.py:741
  8.7 4.1 %collective-permute-start.3 = (bf16[23,8,128]{2,1,0:T(8,128)(2,1)S(1)}, bf16[23,8,128]{2,1,0:T(8,128)(2,1)S(1)}, u32[]{:S(2)}, u32[]{:S(2)}) collective-permute-start(bf16[23,8,128]{2,1,0:T(8,128)(2,1)S(1)} %get-tuple-element.32), channel_id=1, source_target_pairs={{0,4},{1,5},{4,0},{5,1},{8,9},{9,8},{12,13},{13,12},{2,6},{3,7},{6... | collective-permute-start | bytes 141320 | tf_op jit(solution)/shard_map/ppermute | solution.py:784
  10.3 2.5 %collective-permute-start.4 = (bf16[23,8,128]{2,1,0:T(8,128)(2,1)S(1)}, bf16[23,8,128]{2,1,0:T(8,128)(2,1)S(1)}, u32[]{:S(2)}, u32[]{:S(2)}) collective-permute-start(bf16[23,8,128]{2,1,0:T(8,128)(2,1)S(1)} %get-tuple-element.33), channel_id=1, source_target_pairs={{0,1},{1,0},{4,8},{5,9},{8,4},{9,5},{12,13},{13,12},{2,3},{3,2},{6... | collective-permute-start | bytes 141320 | tf_op jit(solution)/shard_map/ppermute | solution.py:784
  10.4 2.4 %collective-permute-start.5 = (bf16[23,8,128]{2,1,0:T(8,128)(2,1)S(1)}, bf16[23,8,128]{2,1,0:T(8,128)(2,1)S(1)}, u32[]{:S(2)}, u32[]{:S(2)}) collective-permute-start(bf16[23,8,128]{2,1,0:T(8,128)(2,1)S(1)} %get-tuple-element.34), channel_id=1, source_target_pairs={{0,1},{1,0},{4,5},{5,4},{8,12},{9,13},{12,8},{13,9},{2,3},{3,2},{6... | collective-permute-start | bytes 141320 | tf_op jit(solution)/shard_map/ppermute | solution.py:784
  13.0 1.2 %collective-permute-start.6 = (f32[6,8,128]{2,1,0:T(8,128)S(1)}, f32[6,8,128]{2,1,0:T(8,128)S(1)}, u32[]{:S(2)}, u32[]{:S(2)}) collective-permute-start(f32[6,8,128]{2,1,0:T(8,128)S(1)} %get-tuple-element.39.handed), channel_id=1, source_target_pairs={{0,1},{1,0},{2,3},{3,2},{4,5},{5,4},{6,7},{7,6},{8,9},{9,8},{10,11... | collective-permute-start | bytes 73736 | tf_op jit(solution)/shard_map/ppermute | solution.py:796
  14.3 3.1 %collective-permute-start.7 = (f32[2,8,128]{2,1,0:T(8,128)S(1)}, f32[2,8,128]{2,1,0:T(8,128)S(1)}, u32[]{:S(2)}, u32[]{:S(2)}) collective-permute-start(f32[2,8,128]{2,1,0:T(8,128)S(1)} %shard_map.66), channel_id=1, source_target_pairs={{0,3},{1,2},{2,1},{3,0},{4,7},{5,6},{6,5},{7,4},{8,11},{9,10},{10,... | collective-permute-start | bytes 24584 | tf_op jit(solution)/shard_map/ppermute | solution.py:801

commit v7 on v6

--- a/solution.py
+++ b/solution.py
@@ -215,45 +215,65 @@
     return ((YM, 7), (YP, 0))
 
 
-def pack_z(directions, adjoint, coefficients, out, lines, strips, faces, coarse, semaphores):
-    core, side = lax.axis_index("gz"), lax.axis_index("gy")
-    copies = [pltpu.make_async_copy(coefficients, coarse, semaphores.at[0])]
-    for k in range(5):
-        q = ZM[k] + core * (ZP[k] - ZM[k])
-        copies.append(pltpu.make_async_copy(adjoint.at[q], faces.at[k], semaphores.at[1 + k]))
+def pack_rows(directions, adjoint, coefficients, out, lines, coarse, strips, near, plane, semaphores):
+    side = lax.axis_index("gy")
+    copies = [pltpu.make_async_copy(coefficients, near, semaphores.at[0])]
     for n in range(directions):
         for k in range(5):
             q = YM[k] + (side if directions == 1 else n) * (YP[k] - YM[k])
             slot = 5 * n + k
             copies.append(
-                pltpu.make_async_copy(adjoint.at[q], strips.at[slot], semaphores.at[6 + slot])
+                pltpu.make_async_copy(adjoint.at[q], strips.at[slot], semaphores.at[1 + slot])
             )
     for copy in copies:
         copy.start()
-    lanes = iota(1)
     count = coefficients.shape[2]
     copies[0].wait()
-    out[2] = jnp.zeros((8, 128), f32)
-    out[3] = jnp.zeros((8, 128), f32)
+    coarse[...] = jnp.zeros((2, 8, 128), f32)
     for j in range(2):
-        out[2 + j, :, 0:count] = coarse[:, j, :]
-    lines[...] = jnp.dot(
-        jnp.concatenate([out[2], out[3]], axis=0),
+        coarse[j, :, 0:count] = near[:, j, :]
+    line = jnp.dot(
+        jnp.concatenate([coarse[0], coarse[1]], axis=0),
         jnp.concatenate([basis_along_z(count), jnp.zeros((128 - count, 128), f32)], axis=0),
         precision=highest,
         preferred_element_type=f32,
     )
+    lines[...] = line
+    high = line.astype(bf16)
+    first = LINE_ROWS * directions
+    out[first : first + 16, :] = high
+    out[first + 16 : first + 32, :] = (line - high.astype(f32)).astype(bf16)
     for copy in copies[1:]:
         copy.wait()
-    for which, source in enumerate((127, 0)):
+
+    def emit(row, n):
+        for k in range(5 * n, 5 * n + 5):
+            for x in range(32):
+                plane[k - 5 * n, x * 8 : x * 8 + 8, :] = strips[k, x].astype(f32)
+        for k in range(5 * n, 5 * n + 5):
+            out[k * 32 : k * 32 + 32, :] = plane[k - 5 * n, pl.ds(row, 32, stride=8), :].astype(bf16)
+
+    for n, (_, row) in enumerate(y_sides()):
+        if directions == 1:
+            pl.when(side == n)(functools.partial(emit, row, 0))
+        else:
+            emit(row, n)
+
+
+def pack_z(adjoint, coarse, out):
+    core = lax.axis_index("gz")
+    lanes = iota(1)
+    for j in range(2):
+        out[2 + j] = coarse[j]
+    for which, (components, source) in enumerate(((ZM, 127), (ZP, 0))):
 
         @pl.when(core == which)
         def _():
             chains = {}
-            for k in range(5):
+            for k, q in enumerate(components):
                 for x in range(32):
                     group, lane = divmod(k * 32 + x, 128)
-                    column = pltpu.roll(faces[k, x].astype(f32), (lane - source) % 128, 1)
+                    column = pltpu.roll(adjoint[q, x].astype(f32), (lane - source) % 128, 1)
                     chain = group, lane // 16
                     if chain in chains:
                         column = jnp.where(lanes >= lane, column, chains[chain])
@@ -265,39 +285,34 @@
                 out[group] = tile
 
 
-def pack_y(directions, strips, sent, lines, *refs):
-    outs_y, outs_yz, plane = refs[:directions], refs[directions:-1], refs[-1]
+def pack_y(directions, count, own, taken, coarse, *outs):
     core, side = lax.axis_index("gz"), lax.axis_index("gy")
     lanes = lax.broadcasted_iota(jnp.int32, (32, 128), 1)
 
-    def emit(components, row, j, first, out, out_yz):
-        edges = {}
+    def emit(components, j, n, out):
         for k, q in enumerate(components):
-            for x in range(32):
-                plane[k, x * 8 : x * 8 + 8, :] = strips[first + k, x].astype(f32)
-        for k, q in enumerate(components):
-            rows = plane[k, pl.ds(row, 32, stride=8), :]
+            place = slice((5 * n + k) * 32, (5 * n + k) * 32 + 32)
             step = VELOCITY[q][2]
-            if step:
-                rows = pltpu.roll(rows, 127 if step > 0 else 1, 1)
-                edge = lanes == (127 if step > 0 else 0)
-                edges[step] = jnp.where(edge, rows, 0.0)
-                rows = jnp.where(edge, 0.0, rows)
-            out[k * 32 : k * 32 + 32, :] = rows.astype(bf16)
-        out_yz[0:32, :] = jnp.where(core == 1, edges[1], edges[-1])
-        out_yz[32:40, :] = sent[2 + j]
-        line = lines[8 * j : 8 * j + 8, :]
+            if not step:
+                out[k * 32 : k * 32 + 32, :] = taken[place, :]
+                continue
+            shift, edge, holder = (127, 127, 1) if step > 0 else (1, 0, 0)
+            rows = pltpu.roll(taken[place, :].astype(f32), shift, 1)
+            border = jnp.where(core == holder, pltpu.roll(own[place, :].astype(f32), shift, 1), 0.0)
+            out[k * 32 : k * 32 + 32, :] = jnp.where(lanes == edge, border, rows).astype(bf16)
+        first = LINE_ROWS * directions
+        line = taken[first : first + 16, :].astype(f32) + taken[first + 16 : first + 32, :].astype(f32)
+        line = add_rim(line[8 * j : 8 * j + 8, :], coarse[j], 1 - core, count)
         high = line.astype(bf16)
         out[LINE_ROWS:STRIP, :] = jnp.concatenate(
             [high, (line - high.astype(f32)).astype(bf16)], axis=0
         )
 
-    for n, (components, row) in enumerate(y_sides()):
+    for n, (components, _) in enumerate(y_sides()):
         if directions == 1:
-            work = functools.partial(emit, components, row, 1 - n, 0, outs_y[0], outs_yz[0])
-            pl.when(side == n)(work)
+            pl.when(side == n)(functools.partial(emit, components, 1 - n, 0, outs[0]))
         else:
-            emit(components, row, 1 - n, 5 * n, outs_y[n], outs_yz[n])
+            emit(components, 1 - n, n, outs[n])
 
 
 def add_rim(line, coarse, core, count):
@@ -353,27 +368,20 @@
         lax.fori_loop(8 * n, 8 * n + 8, flow, 0, unroll=4)
 
 
-def pack_x(directions, count, unpatched, flows, lines, *refs):
-    received = list(zip(refs[:directions], refs[directions : 2 * directions]))
-    pulled, *outs, edges, levels, extra = refs[2 * directions :]
-    core = lax.axis_index("gz")
+def pack_x(directions, unpatched, flows, lines, *refs):
+    received = refs[:directions]
+    pulled, *outs, edges, levels, extra = refs[directions:]
     del unpatched
     side = lax.axis_index("gy")
     place = lax.rem(lax.axis_index("gx"), SLOTS)
 
-    def patch(components, row, buffers):
-        strip, edge = buffers
+    def patch(components, row, strip):
         for k, q in enumerate(components):
-            rows = strip[k * 32 : k * 32 + 32, :].astype(f32)
-            step = VELOCITY[q][2]
-            if step:
-                rows = rows + jnp.where(core == (0 if step > 0 else 1), edge[0:32, :], 0.0)
-            pulled[q, pl.ds(row, 32, stride=8), :] = rows
-
-    def outer_line(buffers):
-        strip, edge = buffers
+            pulled[q, pl.ds(row, 32, stride=8), :] = strip[k * 32 : k * 32 + 32, :].astype(f32)
+
+    def outer_line(strip):
         parts = strip[LINE_ROWS:STRIP, :].astype(f32)
-        return add_rim(parts[0:8] + parts[8:16], edge[32:40, :], core, count)
+        return parts[0:8] + parts[8:16]
 
     if directions == 1:
         pl.when(side == 0)(lambda: patch(YP, 7, received[0]))
@@ -722,31 +730,31 @@
     up = [(i, i + 1) for i in range(count_y - 1)]
     down = [(i + 1, i) for i in range(count_y - 1)]
 
-    strips = shape((5 * directions,) + adjoint.shape[1:], bf16)
-    sent_z, lines, strips = kernel_call(
-        functools.partial(pack_z, directions),
-        [shape((4,) + tile, f32), shape((16, 128), f32), strips],
+    routes = [swap] if directions == 1 else [up, down]
+    crossed = [[(a * 2 + c, b * 2 + 1 - c) for a, b in route for c in range(2)] for route in routes]
+
+    own, lines, coarse = kernel_call(
+        functools.partial(pack_rows, directions),
         [
-            pltpu.VMEM((5,) + adjoint.shape[1:], bf16),
+            shape((LINE_ROWS * directions + 32, 128), bf16),
+            shape((16, 128), f32),
+            shape((2,) + tile, f32),
+        ],
+        [
+            pltpu.VMEM((5 * directions,) + adjoint.shape[1:], bf16),
             pltpu.VMEM(coefficients.shape, f32),
-            pltpu.SemaphoreType.DMA((6 + 5 * directions,)),
+            pltpu.VMEM((5, 256, 128), f32),
+            pltpu.SemaphoreType.DMA((1 + 5 * directions,)),
         ],
         in_specs=[pl.BlockSpec(memory_space=pltpu.HBM)] * 2,
     )(*(pltpu.with_memory_space_constraint(a, pltpu.HBM) for a in (adjoint, coefficients)))
-    sent = kernel_call(
-        functools.partial(pack_y, directions),
-        [shape((STRIP, 128), bf16)] * directions + [shape((40, 128), f32)] * directions,
-        [pltpu.VMEM((5, 256, 128), f32)],
-    )(strips, sent_z, lines)
+    taken_rows = lax.ppermute(own, "gz", swap)
+    sent_z = kernel_call(pack_z, shape((4,) + tile, f32))(adjoint, coarse)
     received_z = lax.ppermute(sent_z, "gz", swap)
-    routes = [swap] if directions == 1 else [up, down]
-    crossed = [
-        [(a * 2 + core, b * 2 + 1 - core) for a, b in route for core in range(2)] for route in routes
-    ]
-    received_y = [lax.ppermute(sent[n], "gy", route) for n, route in enumerate(routes)]
-    received_yz = [
-        lax.ppermute(sent[directions + n], ("gy", "gz"), route) for n, route in enumerate(crossed)
-    ]
+    sent_y = kernel_call(
+        functools.partial(pack_y, directions, count), [shape((STRIP, 128), bf16)] * directions
+    )(own, taken_rows, coarse)
+    received_y = [lax.ppermute(sent, ("gy", "gz"), route) for sent, route in zip(sent_y, crossed)]
 
     pulled, flows, lines, kind = kernel_call(
         functools.partial(pull_zy, count),
@@ -761,6 +769,7 @@
             pltpu.VMEM(forward.shape, bf16),
             pltpu.SemaphoreType.DMA((5,)),
         ],
+        cost_estimate=pl.CostEstimate(flops=10**10, bytes_accessed=10**7, transcendentals=0),
         in_specs=[
             pl.BlockSpec(memory_space=pltpu.HBM if n in (1, 2) else pltpu.VMEM) for n in range(5)
         ],
@@ -773,13 +782,13 @@
     )
 
     pulled, *sent_x, edges, levels = kernel_call(
-        functools.partial(pack_x, directions, count),
+        functools.partial(pack_x, directions),
         [pulled]
         + [shape((BUNDLE,) + tile, bf16)] * SLOTS
         + [shape((2, 8) + tile, f32), shape((8,) + tile, f32)],
         [pltpu.VMEM((32, 128), f32)],
         aliases={0: 0},
-    )(pulled, flows, lines, *received_y, *received_yz)
+    )(pulled, flows, lines, *received_y)
     received_x = [
         lax.ppermute(sent, ("gx", "gz"), pairs(count_x, slot)) for slot, sent in enumerate(sent_x)
     ]
@@ -797,7 +806,6 @@
     relayed = kernel_call(
         functools.partial(relay, directions), [shape((2,) + tile, f32)] * directions
     )(taken, handed)
-    crossed = [[(a * 2 + c, b * 2 + 1 - c) for a, b in route for c in range(2)] for route in routes]
     others = [lax.ppermute(sent, ("gy", "gz"), route) for sent, route in zip(relayed, crossed)]
     in_hbm = pl.BlockSpec(memory_space=pltpu.HBM)
     prior = kernel_call(

time: 18.3 us -> 17.9 us (0.978)
  the two profiles are of different devices: /device:TPU:0 before, /device:TPU:21 now
where the time goes in v7:
time: 17.9 us; the launch traced here: 17.7 us
  starting transfers between devices  7.87 us (44%)
  Pallas kernels  6.89 us (38%)
  waiting for transfers between devices  2.22 us (12%)
  between operations  0.71 us (4%)
    ppermute x2, starting transfers between devices, per_device(): lax.ppermute(sent, ('gy', 'gz'), route)  2.95 us
    ppermute x1, starting transfers between devices, per_device(): taken = lax.ppermute(handed, 'gz', swap)  2.05 us
    ppermute x3, starting transfers between devices, per_device(): lax.ppermute(sent, ('gx', 'gz'), pairs(count_x, slot))  1.87 us
    pallas_call x1, Pallas kernels, per_device(): kernel_call(functools.partial(pull_zy, count), [shape((19, 256, 128), f32...  1.69 us
    pallas_call x1, Pallas kernels, per_device(): kernel_call(collide_inside, [shape(adjoint.shape, bf16), shape((8,) + til...  1.31 us
    pallas_call x1, Pallas kernels, per_device(): kernel_call(collide_outside, shape(adjoint.shape, bf16), [pltpu.VMEM((19,...  1.27 us
    pallas_call x1, Pallas kernels, per_device(): kernel_call(functools.partial(pack_rows, directions), [shape((LINE_ROWS *...  1.19 us
    ppermute x1, waiting for transfers between devices, per_device(): taken = lax.ppermute(handed, 'gz', swap)  0.85 us
  transfers between devices with their start and end apart: 8, of which 5 were waited for; matrix products, arithmetic and copies ran while one was open for 0% of the time, Pallas kernels for 26%

profile of v7, /device:TPU:21, one launch (start us, length us, event | category | flops | bytes accessed | tf_op | source)
XLA Modules:
  0.0 17.7 jit_solution(15352442058507294400)
XLA Ops:
  0.6 1.2 %shard_map.59 = (bf16[192,128]{1,0:T(8,128)(2,1)S(1)}, f32[16,128]{1,0:T(8,128)S(1)}, f32[2,8,128]{2,1,0:T(8,128)S(1)}) custom-call(bf16[19,32,8,128]{3,2,1,0:T(8,128)(2,1)} %adjoint.5, f32[8,2,32]{2,1,0:T(2,128)} %coefficients.1), custom_call_target="tpu_custom_call" | custom-call | tf_op jit(solution)/shard_map/pallas_call | solution.py:736
  1.8 0.7 %collective-permute-start.1 = (bf16[192,128]{1,0:T(8,128)(2,1)S(1)}, bf16[192,128]{1,0:T(8,128)(2,1)S(1)}, u32[]{:S(2)}, u32[]{:S(2)}) collective-permute-start(bf16[192,128]{1,0:T(8,128)(2,1)S(1)} %get-tuple-element.24.own), channel_id=1, source_target_pairs={{0,1},{1,0},{2,3},{3,2},{4,5},{5,4},{6,7},{7,6},{8,9},{9,8},{10,11... | collective-permute-start | bytes 147464 | tf_op jit(solution)/shard_map/ppermute | solution.py:751
  2.6 0.2 %shard_map.60 = f32[4,8,128]{2,1,0:T(8,128)S(1)} custom-call(bf16[19,32,8,128]{3,2,1,0:T(8,128)(2,1)S(1)} %copy-done, f32[2,8,128]{2,1,0:T(8,128)S(1)} %get-tuple-element.19.coarse), custom_call_target="tpu_custom_call" | custom-call | tf_op jit(solution)/shard_map/pallas_call | solution.py:752
  2.8 0.3 %collective-permute-start = (f32[4,8,128]{2,1,0:T(8,128)S(1)}, f32[4,8,128]{2,1,0:T(8,128)S(1)}, u32[]{:S(2)}, u32[]{:S(2)}) collective-permute-start(f32[4,8,128]{2,1,0:T(8,128)S(1)} %shard_map.60), channel_id=1, source_target_pairs={{0,1},{1,0},{2,3},{3,2},{4,5},{5,4},{6,7},{7,6},{8,9},{9,8},{10,11... | collective-permute-start | bytes 49160 | tf_op jit(solution)/shard_map/ppermute | solution.py:753
  3.1 0.4 %collective-permute-done.1.taken = bf16[192,128]{1,0:T(8,128)(2,1)S(1)} collective-permute-done((bf16[192,128]{1,0:T(8,128)(2,1)S(1)}, bf16[192,128]{1,0:T(8,128)(2,1)S(1)}, u32[]{:S(2)}, u32[]{:S(2)}) %collective-permute-start.1) | collective-permute-done | bytes 49184 | tf_op jit(solution)/shard_map/ppermute | solution.py:751
  3.5 0.1 shard_map.62
  3.6 1.5 %collective-permute-start.2 = (bf16[176,128]{1,0:T(8,128)(2,1)S(1)}, bf16[176,128]{1,0:T(8,128)(2,1)S(1)}, u32[]{:S(2)}, u32[]{:S(2)}) collective-permute-start(bf16[176,128]{1,0:T(8,128)(2,1)S(1)} %shard_map.62), channel_id=1, source_target_pairs={{0,3},{1,2},{2,1},{3,0},{4,7},{5,6},{6,5},{7,4},{8,11},{9,10},{10,... | collective-permute-start | bytes 135176 | tf_op jit(solution)/shard_map/ppermute | solution.py:757
  5.1 0.0 collective-permute-done.received
  5.1 1.7 %shard_map.61 = (f32[19,256,128]{2,1,0:T(8,128)S(1)}, f32[5,32,8,128]{3,2,1,0:T(8,128)S(1)}, f32[16,128]{1,0:T(8,128)S(1)}, s32[32,8,128]{2,1,0:T(8,128)S(1)}) custom-call(bf16[19,32,8,128]{3,2,1,0:T(8,128)(2,1)S(1)} %copy-done, bf16[19,32,8,128]{3,2,1,0:T(8,128)(2,1)} %forward_far.1, s32[32,8,128]{2,1,0:T(8,128)} %kind_far.1, ...), custom_call_target="tpu_custom_call" | custom-call | flops 10000000000 | bytes 10000000 | tf_op jit(solution)/shard_map/pallas_call | solution.py:759
  6.8 0.5 %collective-permute-done.2.refs_0_ = bf16[176,128]{1,0:T(8,128)(2,1)S(1)} collective-permute-done((bf16[176,128]{1,0:T(8,128)(2,1)S(1)}, bf16[176,128]{1,0:T(8,128)(2,1)S(1)}, u32[]{:S(2)}, u32[]{:S(2)}) %collective-permute-start.2) | collective-permute-done | bytes 45088 | tf_op jit(solution)/shard_map/ppermute | solution.py:757
  7.2 0.2 shard_map.63
  7.4 0.4 %collective-permute-start.3 = (bf16[23,8,128]{2,1,0:T(8,128)(2,1)S(1)}, bf16[23,8,128]{2,1,0:T(8,128)(2,1)S(1)}, u32[]{:S(2)}, u32[]{:S(2)}) collective-permute-start(bf16[23,8,128]{2,1,0:T(8,128)(2,1)S(1)} %get-tuple-element.28), channel_id=1, source_target_pairs={{0,4},{1,5},{4,0},{5,1},{8,9},{9,8},{12,13},{13,12},{2,6},{3,7},{6... | collective-permute-start | bytes 141320 | tf_op jit(solution)/shard_map/ppermute | solution.py:793
  7.8 0.0 collective-permute-start.4
  7.8 1.5 %collective-permute-start.5 = (bf16[23,8,128]{2,1,0:T(8,128)(2,1)S(1)}, bf16[23,8,128]{2,1,0:T(8,128)(2,1)S(1)}, u32[]{:S(2)}, u32[]{:S(2)}) collective-permute-start(bf16[23,8,128]{2,1,0:T(8,128)(2,1)S(1)} %get-tuple-element.30), channel_id=1, source_target_pairs={{0,1},{1,0},{4,5},{5,4},{8,12},{9,13},{12,8},{13,9},{2,3},{3,2},{6... | collective-permute-start | bytes 141320 | tf_op jit(solution)/shard_map/ppermute | solution.py:793
  9.3 1.3 %shard_map.64 = (bf16[19,32,8,128]{3,2,1,0:T(8,128)(2,1)}, f32[8,8,128]{2,1,0:T(8,128)S(1)}) custom-call(f32[19,256,128]{2,1,0:T(8,128)S(1)} %get-tuple-element.25.pulled, f32[5,32,8,128]{3,2,1,0:T(8,128)S(1)} %get-tuple-element.22.flows, s32[32,8,128]{2,1,0:T(8,128)S(1)} %get-tuple-element.26.kind, f32[8,8,128]{2,1,0:T(8,128)S(1)} %get-tuple-element.27.levels), custom_call_target="tpu_custom_call" | custom-call | tf_op jit(solution)/shard_map/pallas_call | solution.py:796
  10.6 0.1 collective-permute-done.4.refs_1_
  10.7 0.0 collective-permute-done.5.refs_2_
  10.7 0.2 %shard_map.66 = (f32[32,128]{1,0:T(8,128)S(1)}, f32[6,8,128]{2,1,0:T(8,128)S(1)}) custom-call(f32[19,256,128]{2,1,0:T(8,128)S(1)} %get-tuple-element.25.pulled, f32[5,32,8,128]{3,2,1,0:T(8,128)S(1)} %get-tuple-element.22.flows, f32[2,8,8,128]{3,2,1,0:T(8,128)S(1)} %get-tuple-element.32.edges, f32[8,8,128]{2,1,0:T(8,128)S(1)} %get-tuple-element.27.levels, ...), custom_call_target="tpu_custom_call" | custom-call | tf_op jit(solution)/shard_map/pallas_call | solution.py:802
  11.0 2.0 %collective-permute-start.6 = (f32[6,8,128]{2,1,0:T(8,128)S(1)}, f32[6,8,128]{2,1,0:T(8,128)S(1)}, u32[]{:S(2)}, u32[]{:S(2)}) collective-permute-start(f32[6,8,128]{2,1,0:T(8,128)S(1)} %get-tuple-element.35.handed), channel_id=1, source_target_pairs={{0,1},{1,0},{2,3},{3,2},{4,5},{5,4},{6,7},{7,6},{8,9},{9,8},{10,11... | collective-permute-start | bytes 73736 | tf_op jit(solution)/shard_map/ppermute | solution.py:805
  13.0 0.8 %collective-permute-done.6.taken.rims = f32[6,8,128]{2,1,0:T(8,128)S(1)} collective-permute-done((f32[6,8,128]{2,1,0:T(8,128)S(1)}, f32[6,8,128]{2,1,0:T(8,128)S(1)}, u32[]{:S(2)}, u32[]{:S(2)}) %collective-permute-start.6) | collective-permute-done | bytes 24608 | tf_op jit(solution)/shard_map/ppermute | solution.py:805
  13.9 1.4 %collective-permute-start.7 = (f32[2,8,128]{2,1,0:T(8,128)S(1)}, f32[2,8,128]{2,1,0:T(8,128)S(1)}, u32[]{:S(2)}, u32[]{:S(2)}) collective-permute-start(f32[2,8,128]{2,1,0:T(8,128)S(1)} %shard_map.67), channel_id=1, source_target_pairs={{0,3},{1,2},{2,1},{3,0},{4,7},{5,6},{6,5},{7,4},{8,11},{9,10},{10,... | collective-permute-start | bytes 24584 | tf_op jit(solution)/shard_map/ppermute | solution.py:809
  15.3 1.3 %shard_map.65 = bf16[19,32,8,128]{3,2,1,0:T(8,128)(2,1)} custom-call(f32[19,256,128]{2,1,0:T(8,128)S(1)} %get-tuple-element.25.pulled, f32[5,32,8,128]{3,2,1,0:T(8,128)S(1)} %get-tuple-element.22.flows, s32[32,8,128]{2,1,0:T(8,128)S(1)} %get-tuple-element.26.kind, f32[8,8,128]{2,1,0:T(8,128)S(1)} %get-tuple-element.27.levels, ...), custom_call_target="tpu_custom_call", output_to_operand_aliasing={{}: (7, {})} | custom-call | tf_op jit(solution)/shard_map/pallas_call | solution.py:811
  16.6 0.4 %collective-permute-done.7.refs_0_ = f32[2,8,128]{2,1,0:T(8,128)S(1)} collective-permute-done((f32[2,8,128]{2,1,0:T(8,128)S(1)}, f32[2,8,128]{2,1,0:T(8,128)S(1)}, u32[]{:S(2)}, u32[]{:S(2)}) %collective-permute-start.7) | collective-permute-done | bytes 8224 | tf_op jit(solution)/shard_map/ppermute | solution.py:809
  16.9 0.8 %shard_map.68 = f32[8,2,32]{2,1,0:T(2,128)} custom-call(f32[32,128]{1,0:T(8,128)S(1)} %get-tuple-element.34.folded, f32[6,8,128]{2,1,0:T(8,128)S(1)} %collective-permute-done.6.taken.rims, f32[2,8,128]{2,1,0:T(8,128)S(1)} %collective-permute-done.7.refs_0_), custom_call_target="tpu_custom_call" | custom-call | tf_op jit(solution)/shard_map/pallas_call | solution.py:819
  (4 shorter events, 0.0 us)
Async XLA Ops:
  0.6 1.9 %copy-start = (bf16[19,32,8,128]{3,2,1,0:T(8,128)(2,1)S(1)}, bf16[19,32,8,128]{3,2,1,0:T(8,128)(2,1)}, u32[]{:S(2)}) copy-start(bf16[19,32,8,128]{3,2,1,0:T(8,128)(2,1)} %adjoint.5) | copy-start | bytes 3735556
  1.8 1.6 %collective-permute-start.1 = (bf16[192,128]{1,0:T(8,128)(2,1)S(1)}, bf16[192,128]{1,0:T(8,128)(2,1)S(1)}, u32[]{:S(2)}, u32[]{:S(2)}) collective-permute-start(bf16[192,128]{1,0:T(8,128)(2,1)S(1)} %get-tuple-element.24.own), channel_id=1, source_target_pairs={{0,1},{1,0},{2,3},{3,2},{4,5},{5,4},{6,7},{7,6},{8,9},{9,8},{10,11... | collective-permute-start | bytes 147464 | tf_op jit(solution)/shard_map/ppermute | solution.py:751
  2.8 2.3 %collective-permute-start = (f32[4,8,128]{2,1,0:T(8,128)S(1)}, f32[4,8,128]{2,1,0:T(8,128)S(1)}, u32[]{:S(2)}, u32[]{:S(2)}) collective-permute-start(f32[4,8,128]{2,1,0:T(8,128)S(1)} %shard_map.60), channel_id=1, source_target_pairs={{0,1},{1,0},{2,3},{3,2},{4,5},{5,4},{6,7},{7,6},{8,9},{9,8},{10,11... | collective-permute-start | bytes 49160 | tf_op jit(solution)/shard_map/ppermute | solution.py:753
  3.6 3.7 %collective-permute-start.2 = (bf16[176,128]{1,0:T(8,128)(2,1)S(1)}, bf16[176,128]{1,0:T(8,128)(2,1)S(1)}, u32[]{:S(2)}, u32[]{:S(2)}) collective-permute-start(bf16[176,128]{1,0:T(8,128)(2,1)S(1)} %shard_map.62), channel_id=1, source_target_pairs={{0,3},{1,2},{2,1},{3,0},{4,7},{5,6},{6,5},{7,4},{8,11},{9,10},{10,... | collective-permute-start | bytes 135176 | tf_op jit(solution)/shard_map/ppermute | solution.py:757
  7.4 3.2 %collective-permute-start.3 = (bf16[23,8,128]{2,1,0:T(8,128)(2,1)S(1)}, bf16[23,8,128]{2,1,0:T(8,128)(2,1)S(1)}, u32[]{:S(2)}, u32[]{:S(2)}) collective-permute-start(bf16[23,8,128]{2,1,0:T(8,128)(2,1)S(1)} %get-tuple-element.28), channel_id=1, source_target_pairs={{0,4},{1,5},{4,0},{5,1},{8,9},{9,8},{12,13},{13,12},{2,6},{3,7},{6... | collective-permute-start | bytes 141320 | tf_op jit(solution)/shard_map/ppermute | solution.py:793
  7.8 2.9 %collective-permute-start.4 = (bf16[23,8,128]{2,1,0:T(8,128)(2,1)S(1)}, bf16[23,8,128]{2,1,0:T(8,128)(2,1)S(1)}, u32[]{:S(2)}, u32[]{:S(2)}) collective-permute-start(bf16[23,8,128]{2,1,0:T(8,128)(2,1)S(1)} %get-tuple-element.29), channel_id=1, source_target_pairs={{0,1},{1,0},{4,8},{5,9},{8,4},{9,5},{12,13},{13,12},{2,3},{3,2},{6... | collective-permute-start | bytes 141320 | tf_op jit(solution)/shard_map/ppermute | solution.py:793
  7.8 2.9 %collective-permute-start.5 = (bf16[23,8,128]{2,1,0:T(8,128)(2,1)S(1)}, bf16[23,8,128]{2,1,0:T(8,128)(2,1)S(1)}, u32[]{:S(2)}, u32[]{:S(2)}) collective-permute-start(bf16[23,8,128]{2,1,0:T(8,128)(2,1)S(1)} %get-tuple-element.30), channel_id=1, source_target_pairs={{0,1},{1,0},{4,5},{5,4},{8,12},{9,13},{12,8},{13,9},{2,3},{3,2},{6... | collective-permute-start | bytes 141320 | tf_op jit(solution)/shard_map/ppermute | solution.py:793
  11.0 2.9 %collective-permute-start.6 = (f32[6,8,128]{2,1,0:T(8,128)S(1)}, f32[6,8,128]{2,1,0:T(8,128)S(1)}, u32[]{:S(2)}, u32[]{:S(2)}) collective-permute-start(f32[6,8,128]{2,1,0:T(8,128)S(1)} %get-tuple-element.35.handed), channel_id=1, source_target_pairs={{0,1},{1,0},{2,3},{3,2},{4,5},{5,4},{6,7},{7,6},{8,9},{9,8},{10,11... | collective-permute-start | bytes 73736 | tf_op jit(solution)/shard_map/ppermute | solution.py:805
  13.9 3.1 %collective-permute-start.7 = (f32[2,8,128]{2,1,0:T(8,128)S(1)}, f32[2,8,128]{2,1,0:T(8,128)S(1)}, u32[]{:S(2)}, u32[]{:S(2)}) collective-permute-start(f32[2,8,128]{2,1,0:T(8,128)S(1)} %shard_map.67), channel_id=1, source_target_pairs={{0,3},{1,2},{2,1},{3,0},{4,7},{5,6},{6,5},{7,4},{8,11},{9,10},{10,... | collective-permute-start | bytes 24584 | tf_op jit(solution)/shard_map/ppermute | solution.py:809

commit v8 on v7

--- a/solution.py
+++ b/solution.py
@@ -565,8 +565,8 @@
     return tiles[0]
 
 
-def project(count, pulled, flows, edges, levels, *refs):
-    inner, folded, handed = refs[SLOTS:]
+def project(count, directions, pulled, flows, edges, levels, *refs):
+    inner, folded, handed, kept = refs[SLOTS:]
     core = lax.axis_index("gz")
     low, high = along_x(refs[:SLOTS])
     totals = [inner[i] for i in range(8)]
@@ -614,13 +614,22 @@
             add(block, position, alpha, beta)
     lanes = iota(1)
     rim_z = rim_along_z(core, count)
+    sums, rims = [], []
     for j in range(4):
-        sums = fold_rows(totals, basis_along_y(j - 1))
-        folded[8 * j : 8 * j + 8, :] = sums
-        across = jnp.sum(sums * rim_z, axis=1, keepdims=True)
-        handed[j] = jnp.where(lanes == core * (count - 1), across, 0.0)
-        if j in (0, 3):
-            handed[4 + j // 3] = sums
+        sums.append(fold_rows(totals, basis_along_y(j - 1)))
+        across = jnp.sum(sums[j] * rim_z, axis=1, keepdims=True)
+        rims.append(jnp.where(lanes == core * (count - 1), across, 0.0))
+    for j in (1, 2):
+        folded[8 * j - 8 : 8 * j, :] = sums[j]
+        handed[j - 1] = rims[j]
+    if directions == 1:
+        upper = lax.axis_index("gy") == 0
+        handed[2] = jnp.where(upper, sums[3], sums[0])
+        kept[0] = jnp.where(upper, rims[3], rims[0])
+    else:
+        for n, j in enumerate((3, 0)):
+            handed[2 + n] = sums[j]
+            kept[n] = rims[j]
 
 
 def collide_outside(pulled, flows, kind, levels, *refs):
@@ -674,15 +683,10 @@
         copy.wait()
 
 
-def relay(directions, taken, handed, *outs):
-    if directions == 1:
-        side = lax.axis_index("gy")
-        outs[0][0] = taken[5 - side]
-        outs[0][1] = handed[3 - 3 * side]
-    else:
-        for n in range(2):
-            outs[n][0] = taken[5 - n]
-            outs[n][1] = handed[3 - 3 * n]
+def relay(taken, kept, *outs):
+    for n, out in enumerate(outs):
+        out[0] = taken[2 + n]
+        out[1] = kept[n]
 
 
 def finish(folded, rims, *refs):
@@ -694,7 +698,7 @@
         from_high = [jnp.where(side == 0, others[0][n], 0.0) for n in range(2)]
     else:
         from_low, from_high = [[other[n] for n in range(2)] for other in others]
-    sums = jnp.concatenate([folded[8:16, :] + from_low[0], folded[16:24, :] + from_high[0]], axis=0)
+    sums = jnp.concatenate([folded[0:8, :] + from_low[0], folded[8:16, :] + from_high[0]], axis=0)
     result = lax.dot_general(
         sums,
         basis_along_z(count),
@@ -702,8 +706,8 @@
         precision=highest,
         preferred_element_type=f32,
     )
-    out[:, 0, :] = result[0:8] + (rims[1] + from_low[1])[:, 0:count]
-    out[:, 1, :] = result[8:16] + (rims[2] + from_high[1])[:, 0:count]
+    out[:, 0, :] = result[0:8] + (rims[0] + from_low[1])[:, 0:count]
+    out[:, 1, :] = result[8:16] + (rims[1] + from_high[1])[:, 0:count]
 
 
 def pairs(count, slot):
@@ -799,13 +803,16 @@
         [pltpu.VMEM((19, INNER) + tile, bf16), pltpu.SemaphoreType.DMA((INNER // 8,))],
         out_specs=[pl.BlockSpec(memory_space=pltpu.HBM), pl.BlockSpec(memory_space=pltpu.VMEM)],
     )(pulled, flows, kind, levels)
-    folded, handed = kernel_call(
-        functools.partial(project, count), [shape((32, 128), f32), shape((6,) + tile, f32)]
+    folded, handed, kept = kernel_call(
+        functools.partial(project, count, directions),
+        [
+            shape((16, 128), f32),
+            shape((2 + directions,) + tile, f32),
+            shape((directions,) + tile, f32),
+        ],
     )(pulled, flows, edges, levels, *received_x, totals)
     taken = lax.ppermute(handed, "gz", swap)
-    relayed = kernel_call(
-        functools.partial(relay, directions), [shape((2,) + tile, f32)] * directions
-    )(taken, handed)
+    relayed = kernel_call(relay, [shape((2,) + tile, f32)] * directions)(taken, kept)
     others = [lax.ppermute(sent, ("gy", "gz"), route) for sent, route in zip(relayed, crossed)]
     in_hbm = pl.BlockSpec(memory_space=pltpu.HBM)
     prior = kernel_call(

time: 17.9 us -> 17.8 us (level)
  no operation moved by 1% of the time
where the time goes in v8:
time: 17.8 us; the launch traced here: 17.7 us
  starting transfers between devices  7.87 us (44%)
  Pallas kernels  6.89 us (39%)
  waiting for transfers between devices  2.21 us (12%)
  between operations  0.71 us (4%)
    ppermute x2, starting transfers between devices, per_device(): lax.ppermute(sent, ('gy', 'gz'), route)  2.94 us
    ppermute x1, starting transfers between devices, per_device(): taken = lax.ppermute(handed, 'gz', swap)  2.05 us
    ppermute x3, starting transfers between devices, per_device(): lax.ppermute(sent, ('gx', 'gz'), pairs(count_x, slot))  1.87 us
    pallas_call x1, Pallas kernels, per_device(): kernel_call(functools.partial(pull_zy, count), [shape((19, 256, 128), f32...  1.69 us
    pallas_call x1, Pallas kernels, per_device(): kernel_call(collide_inside, [shape(adjoint.shape, bf16), shape((8,) + til...  1.31 us
    pallas_call x1, Pallas kernels, per_device(): kernel_call(collide_outside, shape(adjoint.shape, bf16), [pltpu.VMEM((19,...  1.26 us
    pallas_call x1, Pallas kernels, per_device(): kernel_call(functools.partial(pack_rows, directions), [shape((LINE_ROWS *...  1.19 us
    ppermute x2, waiting for transfers between devices, per_device(): lax.ppermute(sent, ('gy', 'gz'), route)  0.84 us
  transfers between devices with their start and end apart: 8, of which 5 were waited for; matrix products, arithmetic and copies ran while one was open for 0% of the time, Pallas kernels for 26%

profile of v8, /device:TPU:21, one launch (start us, length us, event | category | flops | bytes accessed | tf_op | source)
XLA Modules:
  0.0 17.7 jit_solution(18404972522261397312)
XLA Ops:
  0.6 1.2 %shard_map.59 = (bf16[192,128]{1,0:T(8,128)(2,1)S(1)}, f32[16,128]{1,0:T(8,128)S(1)}, f32[2,8,128]{2,1,0:T(8,128)S(1)}) custom-call(bf16[19,32,8,128]{3,2,1,0:T(8,128)(2,1)} %adjoint.5, f32[8,2,32]{2,1,0:T(2,128)} %coefficients.1), custom_call_target="tpu_custom_call" | custom-call | tf_op jit(solution)/shard_map/pallas_call | solution.py:740
  1.8 0.7 %collective-permute-start.1 = (bf16[192,128]{1,0:T(8,128)(2,1)S(1)}, bf16[192,128]{1,0:T(8,128)(2,1)S(1)}, u32[]{:S(2)}, u32[]{:S(2)}) collective-permute-start(bf16[192,128]{1,0:T(8,128)(2,1)S(1)} %get-tuple-element.25.own), channel_id=1, source_target_pairs={{0,1},{1,0},{2,3},{3,2},{4,5},{5,4},{6,7},{7,6},{8,9},{9,8},{10,11... | collective-permute-start | bytes 147464 | tf_op jit(solution)/shard_map/ppermute | solution.py:755
  2.6 0.2 %shard_map.60 = f32[4,8,128]{2,1,0:T(8,128)S(1)} custom-call(bf16[19,32,8,128]{3,2,1,0:T(8,128)(2,1)S(1)} %copy-done, f32[2,8,128]{2,1,0:T(8,128)S(1)} %get-tuple-element.20.coarse), custom_call_target="tpu_custom_call" | custom-call | tf_op jit(solution)/shard_map/pallas_call | solution.py:756
  2.8 0.3 %collective-permute-start = (f32[4,8,128]{2,1,0:T(8,128)S(1)}, f32[4,8,128]{2,1,0:T(8,128)S(1)}, u32[]{:S(2)}, u32[]{:S(2)}) collective-permute-start(f32[4,8,128]{2,1,0:T(8,128)S(1)} %shard_map.60), channel_id=1, source_target_pairs={{0,1},{1,0},{2,3},{3,2},{4,5},{5,4},{6,7},{7,6},{8,9},{9,8},{10,11... | collective-permute-start | bytes 49160 | tf_op jit(solution)/shard_map/ppermute | solution.py:757
  3.1 0.4 %collective-permute-done.1.taken = bf16[192,128]{1,0:T(8,128)(2,1)S(1)} collective-permute-done((bf16[192,128]{1,0:T(8,128)(2,1)S(1)}, bf16[192,128]{1,0:T(8,128)(2,1)S(1)}, u32[]{:S(2)}, u32[]{:S(2)}) %collective-permute-start.1) | collective-permute-done | bytes 49184 | tf_op jit(solution)/shard_map/ppermute | solution.py:755
  3.5 0.1 shard_map.62
  3.6 1.5 %collective-permute-start.2 = (bf16[176,128]{1,0:T(8,128)(2,1)S(1)}, bf16[176,128]{1,0:T(8,128)(2,1)S(1)}, u32[]{:S(2)}, u32[]{:S(2)}) collective-permute-start(bf16[176,128]{1,0:T(8,128)(2,1)S(1)} %shard_map.62), channel_id=1, source_target_pairs={{0,3},{1,2},{2,1},{3,0},{4,7},{5,6},{6,5},{7,4},{8,11},{9,10},{10,... | collective-permute-start | bytes 135176 | tf_op jit(solution)/shard_map/ppermute | solution.py:761
  5.1 0.0 collective-permute-done.received
  5.1 1.7 %shard_map.61 = (f32[19,256,128]{2,1,0:T(8,128)S(1)}, f32[5,32,8,128]{3,2,1,0:T(8,128)S(1)}, f32[16,128]{1,0:T(8,128)S(1)}, s32[32,8,128]{2,1,0:T(8,128)S(1)}) custom-call(bf16[19,32,8,128]{3,2,1,0:T(8,128)(2,1)S(1)} %copy-done, bf16[19,32,8,128]{3,2,1,0:T(8,128)(2,1)} %forward_far.1, s32[32,8,128]{2,1,0:T(8,128)} %kind_far.1, ...), custom_call_target="tpu_custom_call" | custom-call | flops 10000000000 | bytes 10000000 | tf_op jit(solution)/shard_map/pallas_call | solution.py:763
  6.8 0.5 %collective-permute-done.2.refs_0_ = bf16[176,128]{1,0:T(8,128)(2,1)S(1)} collective-permute-done((bf16[176,128]{1,0:T(8,128)(2,1)S(1)}, bf16[176,128]{1,0:T(8,128)(2,1)S(1)}, u32[]{:S(2)}, u32[]{:S(2)}) %collective-permute-start.2) | collective-permute-done | bytes 45088 | tf_op jit(solution)/shard_map/ppermute | solution.py:761
  7.2 0.2 shard_map.63
  7.4 0.4 %collective-permute-start.3 = (bf16[23,8,128]{2,1,0:T(8,128)(2,1)S(1)}, bf16[23,8,128]{2,1,0:T(8,128)(2,1)S(1)}, u32[]{:S(2)}, u32[]{:S(2)}) collective-permute-start(bf16[23,8,128]{2,1,0:T(8,128)(2,1)S(1)} %get-tuple-element.29), channel_id=1, source_target_pairs={{0,4},{1,5},{4,0},{5,1},{8,9},{9,8},{12,13},{13,12},{2,6},{3,7},{6... | collective-permute-start | bytes 141320 | tf_op jit(solution)/shard_map/ppermute | solution.py:797
  7.8 0.0 collective-permute-start.4
  7.8 1.5 %collective-permute-start.5 = (bf16[23,8,128]{2,1,0:T(8,128)(2,1)S(1)}, bf16[23,8,128]{2,1,0:T(8,128)(2,1)S(1)}, u32[]{:S(2)}, u32[]{:S(2)}) collective-permute-start(bf16[23,8,128]{2,1,0:T(8,128)(2,1)S(1)} %get-tuple-element.31), channel_id=1, source_target_pairs={{0,1},{1,0},{4,5},{5,4},{8,12},{9,13},{12,8},{13,9},{2,3},{3,2},{6... | collective-permute-start | bytes 141320 | tf_op jit(solution)/shard_map/ppermute | solution.py:797
  9.3 1.3 %shard_map.64 = (bf16[19,32,8,128]{3,2,1,0:T(8,128)(2,1)}, f32[8,8,128]{2,1,0:T(8,128)S(1)}) custom-call(f32[19,256,128]{2,1,0:T(8,128)S(1)} %get-tuple-element.26.pulled, f32[5,32,8,128]{3,2,1,0:T(8,128)S(1)} %get-tuple-element.23.flows, s32[32,8,128]{2,1,0:T(8,128)S(1)} %get-tuple-element.27.kind, f32[8,8,128]{2,1,0:T(8,128)S(1)} %get-tuple-element.28.levels), custom_call_target="tpu_custom_call" | custom-call | tf_op jit(solution)/shard_map/pallas_call | solution.py:800
  10.6 0.0 collective-permute-done.3.refs_0_
  10.6 0.1 collective-permute-done.4.refs_1_
  10.7 0.2 %shard_map.66 = (f32[16,128]{1,0:T(8,128)S(1)}, f32[3,8,128]{2,1,0:T(8,128)S(1)}, f32[1,8,128]{2,1,0:T(8,128)S(1)}) custom-call(f32[19,256,128]{2,1,0:T(8,128)S(1)} %get-tuple-element.26.pulled, f32[5,32,8,128]{3,2,1,0:T(8,128)S(1)} %get-tuple-element.23.flows, f32[2,8,8,128]{3,2,1,0:T(8,128)S(1)} %get-tuple-element.33.edges, ...), custom_call_target="tpu_custom_call" | custom-call | tf_op jit(solution)/shard_map/pallas_call | solution.py:806
  11.0 2.0 %collective-permute-start.6 = (f32[3,8,128]{2,1,0:T(8,128)S(1)}, f32[3,8,128]{2,1,0:T(8,128)S(1)}, u32[]{:S(2)}, u32[]{:S(2)}) collective-permute-start(f32[3,8,128]{2,1,0:T(8,128)S(1)} %get-tuple-element.36), channel_id=1, source_target_pairs={{0,1},{1,0},{2,3},{3,2},{4,5},{5,4},{6,7},{7,6},{8,9},{9,8},{10,11... | collective-permute-start | bytes 36872 | tf_op jit(solution)/shard_map/ppermute | solution.py:814
  13.0 0.8 %collective-permute-done.6.taken.rims = f32[3,8,128]{2,1,0:T(8,128)S(1)} collective-permute-done((f32[3,8,128]{2,1,0:T(8,128)S(1)}, f32[3,8,128]{2,1,0:T(8,128)S(1)}, u32[]{:S(2)}, u32[]{:S(2)}) %collective-permute-start.6) | collective-permute-done | bytes 12320 | tf_op jit(solution)/shard_map/ppermute | solution.py:814
  13.8 1.4 %collective-permute-start.7 = (f32[2,8,128]{2,1,0:T(8,128)S(1)}, f32[2,8,128]{2,1,0:T(8,128)S(1)}, u32[]{:S(2)}, u32[]{:S(2)}) collective-permute-start(f32[2,8,128]{2,1,0:T(8,128)S(1)} %shard_map.67), channel_id=1, source_target_pairs={{0,3},{1,2},{2,1},{3,0},{4,7},{5,6},{6,5},{7,4},{8,11},{9,10},{10,... | collective-permute-start | bytes 24584 | tf_op jit(solution)/shard_map/ppermute | solution.py:816
  15.3 1.3 %shard_map.65 = bf16[19,32,8,128]{3,2,1,0:T(8,128)(2,1)} custom-call(f32[19,256,128]{2,1,0:T(8,128)S(1)} %get-tuple-element.26.pulled, f32[5,32,8,128]{3,2,1,0:T(8,128)S(1)} %get-tuple-element.23.flows, s32[32,8,128]{2,1,0:T(8,128)S(1)} %get-tuple-element.27.kind, f32[8,8,128]{2,1,0:T(8,128)S(1)} %get-tuple-element.28.levels, ...), custom_call_target="tpu_custom_call", output_to_operand_aliasing={{}: (7, {})} | custom-call | tf_op jit(solution)/shard_map/pallas_call | solution.py:818
  16.6 0.4 %collective-permute-done.7.refs_0_ = f32[2,8,128]{2,1,0:T(8,128)S(1)} collective-permute-done((f32[2,8,128]{2,1,0:T(8,128)S(1)}, f32[2,8,128]{2,1,0:T(8,128)S(1)}, u32[]{:S(2)}, u32[]{:S(2)}) %collective-permute-start.7) | collective-permute-done | bytes 8224 | tf_op jit(solution)/shard_map/ppermute | solution.py:816
  16.9 0.8 %shard_map.68 = f32[8,2,32]{2,1,0:T(2,128)} custom-call(f32[16,128]{1,0:T(8,128)S(1)} %get-tuple-element.35.folded, f32[3,8,128]{2,1,0:T(8,128)S(1)} %collective-permute-done.6.taken.rims, f32[2,8,128]{2,1,0:T(8,128)S(1)} %collective-permute-done.7.refs_0_), custom_call_target="tpu_custom_call" | custom-call | tf_op jit(solution)/shard_map/pallas_call | solution.py:826
  (4 shorter events, 0.0 us)
Async XLA Ops:
  0.6 1.9 %copy-start = (bf16[19,32,8,128]{3,2,1,0:T(8,128)(2,1)S(1)}, bf16[19,32,8,128]{3,2,1,0:T(8,128)(2,1)}, u32[]{:S(2)}) copy-start(bf16[19,32,8,128]{3,2,1,0:T(8,128)(2,1)} %adjoint.5) | copy-start | bytes 3735556
  1.8 1.6 %collective-permute-start.1 = (bf16[192,128]{1,0:T(8,128)(2,1)S(1)}, bf16[192,128]{1,0:T(8,128)(2,1)S(1)}, u32[]{:S(2)}, u32[]{:S(2)}) collective-permute-start(bf16[192,128]{1,0:T(8,128)(2,1)S(1)} %get-tuple-element.25.own), channel_id=1, source_target_pairs={{0,1},{1,0},{2,3},{3,2},{4,5},{5,4},{6,7},{7,6},{8,9},{9,8},{10,11... | collective-permute-start | bytes 147464 | tf_op jit(solution)/shard_map/ppermute | solution.py:755
  2.8 2.3 %collective-permute-start = (f32[4,8,128]{2,1,0:T(8,128)S(1)}, f32[4,8,128]{2,1,0:T(8,128)S(1)}, u32[]{:S(2)}, u32[]{:S(2)}) collective-permute-start(f32[4,8,128]{2,1,0:T(8,128)S(1)} %shard_map.60), channel_id=1, source_target_pairs={{0,1},{1,0},{2,3},{3,2},{4,5},{5,4},{6,7},{7,6},{8,9},{9,8},{10,11... | collective-permute-start | bytes 49160 | tf_op jit(solution)/shard_map/ppermute | solution.py:757
  3.6 3.7 %collective-permute-start.2 = (bf16[176,128]{1,0:T(8,128)(2,1)S(1)}, bf16[176,128]{1,0:T(8,128)(2,1)S(1)}, u32[]{:S(2)}, u32[]{:S(2)}) collective-permute-start(bf16[176,128]{1,0:T(8,128)(2,1)S(1)} %shard_map.62), channel_id=1, source_target_pairs={{0,3},{1,2},{2,1},{3,0},{4,7},{5,6},{6,5},{7,4},{8,11},{9,10},{10,... | collective-permute-start | bytes 135176 | tf_op jit(solution)/shard_map/ppermute | solution.py:761
  7.4 3.2 %collective-permute-start.3 = (bf16[23,8,128]{2,1,0:T(8,128)(2,1)S(1)}, bf16[23,8,128]{2,1,0:T(8,128)(2,1)S(1)}, u32[]{:S(2)}, u32[]{:S(2)}) collective-permute-start(bf16[23,8,128]{2,1,0:T(8,128)(2,1)S(1)} %get-tuple-element.29), channel_id=1, source_target_pairs={{0,4},{1,5},{4,0},{5,1},{8,9},{9,8},{12,13},{13,12},{2,6},{3,7},{6... | collective-permute-start | bytes 141320 | tf_op jit(solution)/shard_map/ppermute | solution.py:797
  7.8 2.9 %collective-permute-start.4 = (bf16[23,8,128]{2,1,0:T(8,128)(2,1)S(1)}, bf16[23,8,128]{2,1,0:T(8,128)(2,1)S(1)}, u32[]{:S(2)}, u32[]{:S(2)}) collective-permute-start(bf16[23,8,128]{2,1,0:T(8,128)(2,1)S(1)} %get-tuple-element.30), channel_id=1, source_target_pairs={{0,1},{1,0},{4,8},{5,9},{8,4},{9,5},{12,13},{13,12},{2,3},{3,2},{6... | collective-permute-start | bytes 141320 | tf_op jit(solution)/shard_map/ppermute | solution.py:797
  7.8 2.9 %collective-permute-start.5 = (bf16[23,8,128]{2,1,0:T(8,128)(2,1)S(1)}, bf16[23,8,128]{2,1,0:T(8,128)(2,1)S(1)}, u32[]{:S(2)}, u32[]{:S(2)}) collective-permute-start(bf16[23,8,128]{2,1,0:T(8,128)(2,1)S(1)} %get-tuple-element.31), channel_id=1, source_target_pairs={{0,1},{1,0},{4,5},{5,4},{8,12},{9,13},{12,8},{13,9},{2,3},{3,2},{6... | collective-permute-start | bytes 141320 | tf_op jit(solution)/shard_map/ppermute | solution.py:797
  11.0 2.9 %collective-permute-start.6 = (f32[3,8,128]{2,1,0:T(8,128)S(1)}, f32[3,8,128]{2,1,0:T(8,128)S(1)}, u32[]{:S(2)}, u32[]{:S(2)}) collective-permute-start(f32[3,8,128]{2,1,0:T(8,128)S(1)} %get-tuple-element.36), channel_id=1, source_target_pairs={{0,1},{1,0},{2,3},{3,2},{4,5},{5,4},{6,7},{7,6},{8,9},{9,8},{10,11... | collective-permute-start | bytes 36872 | tf_op jit(solution)/shard_map/ppermute | solution.py:814
  13.8 3.1 %collective-permute-start.7 = (f32[2,8,128]{2,1,0:T(8,128)S(1)}, f32[2,8,128]{2,1,0:T(8,128)S(1)}, u32[]{:S(2)}, u32[]{:S(2)}) collective-permute-start(f32[2,8,128]{2,1,0:T(8,128)S(1)} %shard_map.67), channel_id=1, source_target_pairs={{0,3},{1,2},{2,1},{3,0},{4,7},{5,6},{6,5},{7,4},{8,11},{9,10},{10,... | collective-permute-start | bytes 24584 | tf_op jit(solution)/shard_map/ppermute | solution.py:816

commit v9 on v8

--- a/solution.py
+++ b/solution.py
@@ -46,6 +46,7 @@
 FACE, NEAR, FAR, FIELD, LEVEL, BUNDLE = 0, 5, 9, 15, 19, 23
 SLOTS = 3
 LINE_ROWS, STRIP = 160, 176
+AHEAD, LATE = 80, 112
 MASS, INVERSE = 3, 4
 EDGE_PLANES = (0, 1, 2, 3, 28, 29, 30, 31)
 INNER = 16
@@ -207,8 +208,12 @@
     return alpha, beta
 
 
-def rows_of(x):
-    return pl.ds(pl.multiple_of(x * 8, 8), 8) if not isinstance(x, int) else slice(x * 8, x * 8 + 8)
+def rows_of(x, shift=0):
+    return pl.ds(x * 8 + 8 - shift, 8)
+
+
+def rows_at(row, first=0, count=32):
+    return pl.ds(8 * first + 8 + row, count, stride=8)
 
 
 def y_sides():
@@ -285,34 +290,38 @@
                 out[group] = tile
 
 
-def pack_y(directions, count, own, taken, coarse, *outs):
+def pack_y(directions, count, own, taken, coarse, *refs):
+    outs, lates, plane = refs[:directions], refs[directions:-1], refs[-1]
     core, side = lax.axis_index("gz"), lax.axis_index("gy")
     lanes = lax.broadcasted_iota(jnp.int32, (32, 128), 1)
 
-    def emit(components, j, n, out):
+    def emit(components, j, n, out, late):
+        plane[...] = jnp.zeros((AHEAD + LATE, 128), f32)
         for k, q in enumerate(components):
             place = slice((5 * n + k) * 32, (5 * n + k) * 32 + 32)
+            rows = taken[place, :].astype(f32)
             step = VELOCITY[q][2]
-            if not step:
-                out[k * 32 : k * 32 + 32, :] = taken[place, :]
-                continue
-            shift, edge, holder = (127, 127, 1) if step > 0 else (1, 0, 0)
-            rows = pltpu.roll(taken[place, :].astype(f32), shift, 1)
-            border = jnp.where(core == holder, pltpu.roll(own[place, :].astype(f32), shift, 1), 0.0)
-            out[k * 32 : k * 32 + 32, :] = jnp.where(lanes == edge, border, rows).astype(bf16)
+            if step:
+                shift, edge, holder = (127, 127, 1) if step > 0 else (1, 0, 0)
+                border = jnp.where(core == holder, pltpu.roll(own[place, :].astype(f32), shift, 1), 0.0)
+                rows = jnp.where(lanes == edge, border, pltpu.roll(rows, shift, 1))
+            plane[10 * k : 10 * k + 5, :] = rows[0:5]
+            plane[10 * k + 5 : 10 * k + 10, :] = rows[27:32]
+            plane[AHEAD + 22 * k : AHEAD + 22 * k + 22, :] = rows[5:27]
         first = LINE_ROWS * directions
         line = taken[first : first + 16, :].astype(f32) + taken[first + 16 : first + 32, :].astype(f32)
         line = add_rim(line[8 * j : 8 * j + 8, :], coarse[j], 1 - core, count)
         high = line.astype(bf16)
-        out[LINE_ROWS:STRIP, :] = jnp.concatenate(
-            [high, (line - high.astype(f32)).astype(bf16)], axis=0
-        )
+        plane[64:72, :] = high.astype(f32)
+        plane[72:80, :] = line - high.astype(f32)
+        out[...] = plane[0:AHEAD, :].astype(bf16)
+        late[...] = plane[AHEAD : AHEAD + LATE, :].astype(bf16)
 
     for n, (components, _) in enumerate(y_sides()):
         if directions == 1:
-            pl.when(side == n)(functools.partial(emit, components, 1 - n, 0, outs[0]))
+            pl.when(side == n)(functools.partial(emit, components, 1 - n, 0, outs[0], lates[0]))
         else:
-            emit(components, 1 - n, n, outs[n])
+            emit(components, 1 - n, n, outs[n], lates[n])
 
 
 def add_rim(line, coarse, core, count):
@@ -321,35 +330,22 @@
 
 
 def pull_zy(
-    count, adjoint, forward_far, kind_far, received, own_lines,
-    pulled, flows, lines, kind, columns, forward, semaphores,
+    count, adjoint, forward, kind_far, received, own_lines,
+    pulled, flows, lines, kind, columns, semaphores,
 ):
-    copies = [
-        pltpu.make_async_copy(
-            forward_far.at[:, pl.ds(8 * n, 8)], forward.at[:, pl.ds(8 * n, 8)], semaphores.at[n]
-        )
-        for n in range(4)
-    ]
-    copies.append(pltpu.make_async_copy(kind_far, kind, semaphores.at[4]))
-    for copy in copies:
-        copy.start()
+    copy = pltpu.make_async_copy(kind_far, kind, semaphores.at[0])
+    copy.start()
     core = lax.axis_index("gz")
     load_columns(core, received, columns)
     for j in range(2):
         lines[8 * j : 8 * j + 8, :] = add_rim(
             own_lines[8 * j : 8 * j + 8, :], received[2 + j], core, count
         )
-    sublanes = iota(0)
 
     def step(x, carry):
         for q in range(19):
             tile = pulled_z(q, adjoint[q, x].astype(f32), x, columns)
-            step_y = VELOCITY[q][1]
-            if step_y > 0:
-                tile = jnp.where(sublanes == 7, 0.0, pltpu.roll(tile, 7, 0))
-            elif step_y < 0:
-                tile = jnp.where(sublanes == 0, 0.0, pltpu.roll(tile, 1, 0))
-            pulled[q, rows_of(x), :] = tile
+            pulled[q, rows_of(x, VELOCITY[q][1]), :] = tile
         return carry
 
     def flow(x, carry):
@@ -362,10 +358,11 @@
         return carry
 
     lax.fori_loop(0, 32, step, 0, unroll=4)
-    copies[4].wait()
-    for n in range(4):
-        copies[n].wait()
-        lax.fori_loop(8 * n, 8 * n + 8, flow, 0, unroll=4)
+    for k in range(5):
+        pulled[YP[k], rows_at(7), :] = jnp.zeros((32, 128), f32)
+        pulled[YM[k], rows_at(0), :] = jnp.zeros((32, 128), f32)
+    copy.wait()
+    lax.fori_loop(0, 32, flow, 0, unroll=4)
 
 
 def pack_x(directions, unpatched, flows, lines, *refs):
@@ -376,11 +373,13 @@
     place = lax.rem(lax.axis_index("gx"), SLOTS)
 
     def patch(components, row, strip):
+        rows = strip[0:64, :].astype(f32)
         for k, q in enumerate(components):
-            pulled[q, pl.ds(row, 32, stride=8), :] = strip[k * 32 : k * 32 + 32, :].astype(f32)
+            pulled[q, rows_at(row, 0, 5), :] = rows[10 * k : 10 * k + 5]
+            pulled[q, rows_at(row, 27, 5), :] = rows[10 * k + 5 : 10 * k + 10]
 
     def outer_line(strip):
-        parts = strip[LINE_ROWS:STRIP, :].astype(f32)
+        parts = strip[64:80, :].astype(f32)
         return parts[0:8] + parts[8:16]
 
     if directions == 1:
@@ -487,7 +486,22 @@
         stage[q, slot] = (kept + shift).astype(bf16)
 
 
-def collide_inside(pulled, flows, kind, levels, out, totals, stage, semaphores):
+def collide_inside(directions, unpatched, flows, kind, levels, *refs):
+    late, (pulled, out, totals, stage, semaphores) = refs[:directions], refs[directions:]
+    del unpatched
+    side = lax.axis_index("gy")
+
+    def patch(components, row, strip):
+        rows = strip[...].astype(f32)
+        for k, q in enumerate(components):
+            pulled[q, rows_at(row, 5, 22), :] = rows[22 * k : 22 * k + 22]
+
+    if directions == 1:
+        pl.when(side == 0)(lambda: patch(YP, 7, late[0]))
+        pl.when(side == 1)(lambda: patch(YM, 0, late[0]))
+    else:
+        patch(YM, 0, late[0])
+        patch(YP, 7, late[1])
     totals[...] = jnp.zeros((8, 8, 128), f32)
 
     def middle(with_prior, block, carry):
@@ -756,30 +770,32 @@
     sent_z = kernel_call(pack_z, shape((4,) + tile, f32))(adjoint, coarse)
     received_z = lax.ppermute(sent_z, "gz", swap)
     sent_y = kernel_call(
-        functools.partial(pack_y, directions, count), [shape((STRIP, 128), bf16)] * directions
+        functools.partial(pack_y, directions, count),
+        [shape((AHEAD, 128), bf16)] * directions + [shape((LATE, 128), bf16)] * directions,
+        [pltpu.VMEM((AHEAD + LATE, 128), f32)],
     )(own, taken_rows, coarse)
-    received_y = [lax.ppermute(sent, ("gy", "gz"), route) for sent, route in zip(sent_y, crossed)]
+    received = [lax.ppermute(sent, ("gy", "gz"), route) for sent, route in zip(sent_y, crossed * 2)]
+    received_y, received_late = received[:directions], received[directions:]
 
     pulled, flows, lines, kind = kernel_call(
         functools.partial(pull_zy, count),
         [
-            shape((19, 256, 128), f32),
+            shape((19, 272, 128), f32),
             shape((5,) + kind.shape, f32),
             shape((16, 128), f32),
             shape(kind.shape, jnp.int32),
         ],
         [
             pltpu.VMEM((2, 2) + tile, f32),
-            pltpu.VMEM(forward.shape, bf16),
-            pltpu.SemaphoreType.DMA((5,)),
+            pltpu.SemaphoreType.DMA((1,)),
         ],
         cost_estimate=pl.CostEstimate(flops=10**10, bytes_accessed=10**7, transcendentals=0),
         in_specs=[
-            pl.BlockSpec(memory_space=pltpu.HBM if n in (1, 2) else pltpu.VMEM) for n in range(5)
+            pl.BlockSpec(memory_space=pltpu.HBM if n == 2 else pltpu.VMEM) for n in range(5)
         ],
     )(
         adjoint,
-        pltpu.with_memory_space_constraint(forward, pltpu.HBM),
+        forward,
         pltpu.with_memory_space_constraint(kind, pltpu.HBM),
         received_z,
         lines,
@@ -797,12 +813,16 @@
         lax.ppermute(sent, ("gx", "gz"), pairs(count_x, slot)) for slot, sent in enumerate(sent_x)
     ]
 
-    prior, totals = kernel_call(
-        collide_inside,
-        [shape(adjoint.shape, bf16), shape((8,) + tile, f32)],
+    pulled, prior, totals = kernel_call(
+        functools.partial(collide_inside, directions),
+        [pulled, shape(adjoint.shape, bf16), shape((8,) + tile, f32)],
         [pltpu.VMEM((19, INNER) + tile, bf16), pltpu.SemaphoreType.DMA((INNER // 8,))],
-        out_specs=[pl.BlockSpec(memory_space=pltpu.HBM), pl.BlockSpec(memory_space=pltpu.VMEM)],
-    )(pulled, flows, kind, levels)
+        aliases={0: 0},
+        out_specs=[
+            pl.BlockSpec(memory_space=space) for space in (pltpu.VMEM, pltpu.HBM, pltpu.VMEM)
+        ],
+        cost_estimate=pl.CostEstimate(flops=10**10, bytes_accessed=1, transcendentals=0),
+    )(pulled, flows, kind, levels, *received_late)
     folded, handed, kept = kernel_call(
         functools.partial(project, count, directions),
         [

time: 17.8 us -> 17.6 us (0.989)
  the two profiles are of different devices: /device:TPU:21 before, /device:TPU:0 now
where the time goes in v9:
time: 17.6 us; the launch traced here: 17.3 us
  starting transfers between devices  7.72 us (44%)
  Pallas kernels  6.84 us (39%)
  waiting for transfers between devices  1.97 us (11%)
  between operations  0.72 us (4%)
    ppermute x3, starting transfers between devices, per_device(): lax.ppermute(sent, ('gy', 'gz'), route)  4.43 us
    ppermute x3, starting transfers between devices, per_device(): lax.ppermute(sent, ('gx', 'gz'), pairs(count_x, slot))  2.57 us
    pallas_call x1, Pallas kernels, per_device(): kernel_call(functools.partial(pull_zy, count), [shape((19, 272, 128), f32...  1.54 us
    pallas_call x1, Pallas kernels, per_device(): kernel_call(functools.partial(collide_inside, directions), [pulled, shape...  1.33 us
    pallas_call x1, Pallas kernels, per_device(): kernel_call(collide_outside, shape(adjoint.shape, bf16), [pltpu.VMEM((19,...  1.27 us
    pallas_call x1, Pallas kernels, per_device(): kernel_call(functools.partial(pack_rows, directions), [shape((LINE_ROWS *...  1.24 us
    ppermute x1, waiting for transfers between devices, per_device(): taken = lax.ppermute(handed, 'gz', swap)  1.17 us
    pallas_call x1, Pallas kernels, per_device(): kernel_call(finish, shape(coefficients.shape, f32))(folded, taken, *others)  0.76 us
  transfers between devices with their start and end apart: 9, of which 4 were waited for; matrix products, arithmetic and copies ran while one was open for 0% of the time, Pallas kernels for 27%

profile of v9, /device:TPU:0, one launch (start us, length us, event | category | flops | bytes accessed | tf_op | source)
XLA Modules:
  0.0 17.3 jit_solution(14973747347112375685)
XLA Ops:
  0.6 1.2 %shard_map.59 = (bf16[192,128]{1,0:T(8,128)(2,1)S(1)}, f32[16,128]{1,0:T(8,128)S(1)}, f32[2,8,128]{2,1,0:T(8,128)S(1)}) custom-call(bf16[19,32,8,128]{3,2,1,0:T(8,128)(2,1)} %adjoint.5, f32[8,2,32]{2,1,0:T(2,128)} %coefficients.1), custom_call_target="tpu_custom_call" | custom-call | tf_op jit(solution)/shard_map/pallas_call | solution.py:754
  1.9 0.5 %collective-permute-start.1 = (bf16[192,128]{1,0:T(8,128)(2,1)S(1)}, bf16[192,128]{1,0:T(8,128)(2,1)S(1)}, u32[]{:S(2)}, u32[]{:S(2)}) collective-permute-start(bf16[192,128]{1,0:T(8,128)(2,1)S(1)} %get-tuple-element.28.own), channel_id=1, source_target_pairs={{0,1},{1,0},{2,3},{3,2},{4,5},{5,4},{6,7},{7,6},{8,9},{9,8},{10,11... | collective-permute-start | bytes 147464 | tf_op jit(solution)/shard_map/ppermute | solution.py:769
  2.4 0.2 %shard_map.60 = f32[4,8,128]{2,1,0:T(8,128)S(1)} custom-call(bf16[19,32,8,128]{3,2,1,0:T(8,128)(2,1)S(1)} %copy-done, f32[2,8,128]{2,1,0:T(8,128)S(1)} %get-tuple-element.23.coarse), custom_call_target="tpu_custom_call" | custom-call | tf_op jit(solution)/shard_map/pallas_call | solution.py:770
  2.6 0.2 %collective-permute-start = (f32[4,8,128]{2,1,0:T(8,128)S(1)}, f32[4,8,128]{2,1,0:T(8,128)S(1)}, u32[]{:S(2)}, u32[]{:S(2)}) collective-permute-start(f32[4,8,128]{2,1,0:T(8,128)S(1)} %shard_map.60), channel_id=1, source_target_pairs={{0,1},{1,0},{2,3},{3,2},{4,5},{5,4},{6,7},{7,6},{8,9},{9,8},{10,11... | collective-permute-start | bytes 49160 | tf_op jit(solution)/shard_map/ppermute | solution.py:771
  2.8 0.5 %collective-permute-done.1.taken = bf16[192,128]{1,0:T(8,128)(2,1)S(1)} collective-permute-done((bf16[192,128]{1,0:T(8,128)(2,1)S(1)}, bf16[192,128]{1,0:T(8,128)(2,1)S(1)}, u32[]{:S(2)}, u32[]{:S(2)}) %collective-permute-start.1) | collective-permute-done | bytes 49184 | tf_op jit(solution)/shard_map/ppermute | solution.py:769
  3.3 0.1 shard_map.62
  3.4 2.7 %collective-permute-start.2 = (bf16[80,128]{1,0:T(8,128)(2,1)S(1)}, bf16[80,128]{1,0:T(8,128)(2,1)S(1)}, u32[]{:S(2)}, u32[]{:S(2)}) collective-permute-start(bf16[80,128]{1,0:T(8,128)(2,1)S(1)} %get-tuple-element.29), channel_id=1, source_target_pairs={{0,3},{1,2},{2,1},{3,0},{4,7},{5,6},{6,5},{7,4},{8,11},{9,10},{10,... | collective-permute-start | bytes 61448 | tf_op jit(solution)/shard_map/ppermute | solution.py:777
  6.1 0.1 collective-permute-start.3
  6.1 0.0 collective-permute-done.received
  6.1 1.5 %shard_map.61 = (f32[19,272,128]{2,1,0:T(8,128)S(1)}, f32[5,32,8,128]{3,2,1,0:T(8,128)S(1)}, f32[16,128]{1,0:T(8,128)S(1)}, s32[32,8,128]{2,1,0:T(8,128)S(1)}) custom-call(bf16[19,32,8,128]{3,2,1,0:T(8,128)(2,1)S(1)} %copy-done, bf16[19,32,8,128]{3,2,1,0:T(8,128)(2,1)S(1)} %copy-done.1, s32[32,8,128]{2,1,0:T(8,128)} %kind_far.1, ...), custom_call_target="tpu_custom_call" | custom-call | flops 10000000000 | bytes 10000000 | tf_op jit(solution)/shard_map/pallas_call | solution.py:780
  7.7 0.2 shard_map.63
  7.9 2.1 %collective-permute-start.4 = (bf16[23,8,128]{2,1,0:T(8,128)(2,1)S(1)}, bf16[23,8,128]{2,1,0:T(8,128)(2,1)S(1)}, u32[]{:S(2)}, u32[]{:S(2)}) collective-permute-start(bf16[23,8,128]{2,1,0:T(8,128)(2,1)S(1)} %get-tuple-element.35), channel_id=1, source_target_pairs={{0,4},{1,5},{4,0},{5,1},{8,9},{9,8},{12,13},{13,12},{2,6},{3,7},{6... | collective-permute-start | bytes 141320 | tf_op jit(solution)/shard_map/ppermute | solution.py:813
  9.9 0.5 %collective-permute-start.6 = (bf16[23,8,128]{2,1,0:T(8,128)(2,1)S(1)}, bf16[23,8,128]{2,1,0:T(8,128)(2,1)S(1)}, u32[]{:S(2)}, u32[]{:S(2)}) collective-permute-start(bf16[23,8,128]{2,1,0:T(8,128)(2,1)S(1)} %get-tuple-element.37), channel_id=1, source_target_pairs={{0,1},{1,0},{4,5},{5,4},{8,12},{9,13},{12,8},{13,9},{2,3},{3,2},{6... | collective-permute-start | bytes 141320 | tf_op jit(solution)/shard_map/ppermute | solution.py:813
  10.4 0.0 collective-permute-done.3.refs_0_
  10.4 1.3 %shard_map.64 = (f32[19,272,128]{2,1,0:T(8,128)S(1)}, bf16[19,32,8,128]{3,2,1,0:T(8,128)(2,1)}, f32[8,8,128]{2,1,0:T(8,128)S(1)}) custom-call(f32[19,272,128]{2,1,0:T(8,128)S(1)} %get-tuple-element.30.unpatched, f32[5,32,8,128]{3,2,1,0:T(8,128)S(1)} %get-tuple-element.26.flows, ...), custom_call_target="tpu_custom_call", output_to_operand_aliasing={{0}: (0, {})} | custom-call | flops 10000000000 | bytes 1 | tf_op jit(solution)/shard_map/pallas_call | solution.py:816
  11.8 0.2 %collective-permute-done.4.refs_0_ = bf16[23,8,128]{2,1,0:T(8,128)(2,1)S(1)} collective-permute-done((bf16[23,8,128]{2,1,0:T(8,128)(2,1)S(1)}, bf16[23,8,128]{2,1,0:T(8,128)(2,1)S(1)}, u32[]{:S(2)}, u32[]{:S(2)}) %collective-permute-start.4) | collective-permute-done | bytes 47136 | tf_op jit(solution)/shard_map/ppermute | solution.py:813
  12.0 0.0 collective-permute-done.5.refs_1_
  12.0 0.2 %shard_map.66 = (f32[16,128]{1,0:T(8,128)S(1)}, f32[3,8,128]{2,1,0:T(8,128)S(1)}, f32[1,8,128]{2,1,0:T(8,128)S(1)}) custom-call(f32[19,272,128]{2,1,0:T(8,128)S(1)} %get-tuple-element.34.pulled, f32[5,32,8,128]{3,2,1,0:T(8,128)S(1)} %get-tuple-element.26.flows, f32[2,8,8,128]{3,2,1,0:T(8,128)S(1)} %get-tuple-element.39.edges, ...), custom_call_target="tpu_custom_call" | custom-call | tf_op jit(solution)/shard_map/pallas_call | solution.py:826
  12.2 0.0 collective-permute-start.7
  12.3 1.2 %collective-permute-done.7.taken.rims = f32[3,8,128]{2,1,0:T(8,128)S(1)} collective-permute-done((f32[3,8,128]{2,1,0:T(8,128)S(1)}, f32[3,8,128]{2,1,0:T(8,128)S(1)}, u32[]{:S(2)}, u32[]{:S(2)}) %collective-permute-start.7) | collective-permute-done | bytes 12320 | tf_op jit(solution)/shard_map/ppermute | solution.py:834
  13.4 1.7 %collective-permute-start.8 = (f32[2,8,128]{2,1,0:T(8,128)S(1)}, f32[2,8,128]{2,1,0:T(8,128)S(1)}, u32[]{:S(2)}, u32[]{:S(2)}) collective-permute-start(f32[2,8,128]{2,1,0:T(8,128)S(1)} %shard_map.67), channel_id=1, source_target_pairs={{0,3},{1,2},{2,1},{3,0},{4,7},{5,6},{6,5},{7,4},{8,11},{9,10},{10,... | collective-permute-start | bytes 24584 | tf_op jit(solution)/shard_map/ppermute | solution.py:836
  15.1 1.3 %shard_map.65 = bf16[19,32,8,128]{3,2,1,0:T(8,128)(2,1)} custom-call(f32[19,272,128]{2,1,0:T(8,128)S(1)} %get-tuple-element.34.pulled, f32[5,32,8,128]{3,2,1,0:T(8,128)S(1)} %get-tuple-element.26.flows, s32[32,8,128]{2,1,0:T(8,128)S(1)} %get-tuple-element.31.kind, f32[8,8,128]{2,1,0:T(8,128)S(1)} %get-tuple-element.32.levels, ...), custom_call_target="tpu_custom_call", output_to_operand_aliasing={{}: (7, {})} | custom-call | tf_op jit(solution)/shard_map/pallas_call | solution.py:838
  16.4 0.1 collective-permute-done.8.refs_0_
  16.5 0.8 %shard_map.68 = f32[8,2,32]{2,1,0:T(2,128)} custom-call(f32[16,128]{1,0:T(8,128)S(1)} %get-tuple-element.41.folded, f32[3,8,128]{2,1,0:T(8,128)S(1)} %collective-permute-done.7.taken.rims, f32[2,8,128]{2,1,0:T(8,128)S(1)} %collective-permute-done.8.refs_0_), custom_call_target="tpu_custom_call" | custom-call | tf_op jit(solution)/shard_map/pallas_call | solution.py:846
  (8 shorter events, 0.0 us)
Async XLA Ops:
  0.6 1.8 %copy-start = (bf16[19,32,8,128]{3,2,1,0:T(8,128)(2,1)S(1)}, bf16[19,32,8,128]{3,2,1,0:T(8,128)(2,1)}, u32[]{:S(2)}) copy-start(bf16[19,32,8,128]{3,2,1,0:T(8,128)(2,1)} %adjoint.5) | copy-start | bytes 3735556
  0.6 5.5 %copy-start.1 = (bf16[19,32,8,128]{3,2,1,0:T(8,128)(2,1)S(1)}, bf16[19,32,8,128]{3,2,1,0:T(8,128)(2,1)}, u32[]{:S(2)}) copy-start(bf16[19,32,8,128]{3,2,1,0:T(8,128)(2,1)} %forward.1) | copy-start | bytes 3735556
  1.9 1.4 %collective-permute-start.1 = (bf16[192,128]{1,0:T(8,128)(2,1)S(1)}, bf16[192,128]{1,0:T(8,128)(2,1)S(1)}, u32[]{:S(2)}, u32[]{:S(2)}) collective-permute-start(bf16[192,128]{1,0:T(8,128)(2,1)S(1)} %get-tuple-element.28.own), channel_id=1, source_target_pairs={{0,1},{1,0},{2,3},{3,2},{4,5},{5,4},{6,7},{7,6},{8,9},{9,8},{10,11... | collective-permute-start | bytes 147464 | tf_op jit(solution)/shard_map/ppermute | solution.py:769
  2.6 3.5 %collective-permute-start = (f32[4,8,128]{2,1,0:T(8,128)S(1)}, f32[4,8,128]{2,1,0:T(8,128)S(1)}, u32[]{:S(2)}, u32[]{:S(2)}) collective-permute-start(f32[4,8,128]{2,1,0:T(8,128)S(1)} %shard_map.60), channel_id=1, source_target_pairs={{0,1},{1,0},{2,3},{3,2},{4,5},{5,4},{6,7},{7,6},{8,9},{9,8},{10,11... | collective-permute-start | bytes 49160 | tf_op jit(solution)/shard_map/ppermute | solution.py:771
  3.4 4.3 %collective-permute-start.2 = (bf16[80,128]{1,0:T(8,128)(2,1)S(1)}, bf16[80,128]{1,0:T(8,128)(2,1)S(1)}, u32[]{:S(2)}, u32[]{:S(2)}) collective-permute-start(bf16[80,128]{1,0:T(8,128)(2,1)S(1)} %get-tuple-element.29), channel_id=1, source_target_pairs={{0,3},{1,2},{2,1},{3,0},{4,7},{5,6},{6,5},{7,4},{8,11},{9,10},{10,... | collective-permute-start | bytes 61448 | tf_op jit(solution)/shard_map/ppermute | solution.py:777
  6.1 4.4 %collective-permute-start.3 = (bf16[112,128]{1,0:T(8,128)(2,1)S(1)}, bf16[112,128]{1,0:T(8,128)(2,1)S(1)}, u32[]{:S(2)}, u32[]{:S(2)}) collective-permute-start(bf16[112,128]{1,0:T(8,128)(2,1)S(1)} %get-tuple-element.33), channel_id=1, source_target_pairs={{0,3},{1,2},{2,1},{3,0},{4,7},{5,6},{6,5},{7,4},{8,11},{9,10},{10,... | collective-permute-start | bytes 86024 | tf_op jit(solution)/shard_map/ppermute | solution.py:777
  7.9 4.1 %collective-permute-start.4 = (bf16[23,8,128]{2,1,0:T(8,128)(2,1)S(1)}, bf16[23,8,128]{2,1,0:T(8,128)(2,1)S(1)}, u32[]{:S(2)}, u32[]{:S(2)}) collective-permute-start(bf16[23,8,128]{2,1,0:T(8,128)(2,1)S(1)} %get-tuple-element.35), channel_id=1, source_target_pairs={{0,4},{1,5},{4,0},{5,1},{8,9},{9,8},{12,13},{13,12},{2,6},{3,7},{6... | collective-permute-start | bytes 141320 | tf_op jit(solution)/shard_map/ppermute | solution.py:813
  9.9 2.1 %collective-permute-start.5 = (bf16[23,8,128]{2,1,0:T(8,128)(2,1)S(1)}, bf16[23,8,128]{2,1,0:T(8,128)(2,1)S(1)}, u32[]{:S(2)}, u32[]{:S(2)}) collective-permute-start(bf16[23,8,128]{2,1,0:T(8,128)(2,1)S(1)} %get-tuple-element.36), channel_id=1, source_target_pairs={{0,1},{1,0},{4,8},{5,9},{8,4},{9,5},{12,13},{13,12},{2,3},{3,2},{6... | collective-permute-start | bytes 141320 | tf_op jit(solution)/shard_map/ppermute | solution.py:813
  9.9 2.1 %collective-permute-start.6 = (bf16[23,8,128]{2,1,0:T(8,128)(2,1)S(1)}, bf16[23,8,128]{2,1,0:T(8,128)(2,1)S(1)}, u32[]{:S(2)}, u32[]{:S(2)}) collective-permute-start(bf16[23,8,128]{2,1,0:T(8,128)(2,1)S(1)} %get-tuple-element.37), channel_id=1, source_target_pairs={{0,1},{1,0},{4,5},{5,4},{8,12},{9,13},{12,8},{13,9},{2,3},{3,2},{6... | collective-permute-start | bytes 141320 | tf_op jit(solution)/shard_map/ppermute | solution.py:813
  12.2 1.2 %collective-permute-start.7 = (f32[3,8,128]{2,1,0:T(8,128)S(1)}, f32[3,8,128]{2,1,0:T(8,128)S(1)}, u32[]{:S(2)}, u32[]{:S(2)}) collective-permute-start(f32[3,8,128]{2,1,0:T(8,128)S(1)} %get-tuple-element.42), channel_id=1, source_target_pairs={{0,1},{1,0},{2,3},{3,2},{4,5},{5,4},{6,7},{7,6},{8,9},{9,8},{10,11... | collective-permute-start | bytes 36872 | tf_op jit(solution)/shard_map/ppermute | solution.py:834
  13.4 3.1 %collective-permute-start.8 = (f32[2,8,128]{2,1,0:T(8,128)S(1)}, f32[2,8,128]{2,1,0:T(8,128)S(1)}, u32[]{:S(2)}, u32[]{:S(2)}) collective-permute-start(f32[2,8,128]{2,1,0:T(8,128)S(1)} %shard_map.67), channel_id=1, source_target_pairs={{0,3},{1,2},{2,1},{3,0},{4,7},{5,6},{6,5},{7,4},{8,11},{9,10},{10,... | collective-permute-start | bytes 24584 | tf_op jit(solution)/shard_map/ppermute | solution.py:836

commit v10 on v9

--- a/solution.py
+++ b/solution.py
@@ -92,26 +92,13 @@
     return lax.broadcasted_iota(jnp.int32, (8, 128), dimension)
 
 
-def pulled_z(q, tile, x, columns):
+def pulled_z(q, tile, edges):
     step = VELOCITY[q][2]
     if step == 0:
         return tile
-    slot = (ZP if step > 0 else ZM).index(q) * 32
-    group, lane = slot // 128, slot % 128
-    lanes = iota(1)
-    edge = columns[0 if step > 0 else 1, group]
     if step > 0:
-        edge = pltpu.roll(edge, 127 - lane - x, 1)
-        return jnp.where(lanes == 127, edge, pltpu.roll(tile, 127, 1))
-    edge = pltpu.roll(edge, (128 - lane - x) & 127, 1)
-    return jnp.where(lanes == 0, edge, pltpu.roll(tile, 1, 1))
-
-
-def load_columns(core, received, columns):
-    for group in range(2):
-        tile = received[group]
-        columns[0, group] = jnp.where(core == 0, tile, 0.0)
-        columns[1, group] = jnp.where(core == 1, tile, 0.0)
+        return jnp.where(iota(1) == 127, edges[0][ZP.index(q)], pltpu.roll(tile, 127, 1))
+    return jnp.where(iota(1) == 0, edges[1][ZM.index(q)], pltpu.roll(tile, 1, 1))
 
 
 def pair_moments(populations):
@@ -331,20 +318,25 @@
 
 def pull_zy(
     count, adjoint, forward, kind_far, received, own_lines,
-    pulled, flows, lines, kind, columns, semaphores,
+    pulled, flows, lines, kind, semaphores,
 ):
     copy = pltpu.make_async_copy(kind_far, kind, semaphores.at[0])
     copy.start()
     core = lax.axis_index("gz")
-    load_columns(core, received, columns)
     for j in range(2):
         lines[8 * j : 8 * j + 8, :] = add_rim(
             own_lines[8 * j : 8 * j + 8, :], received[2 + j], core, count
         )
 
     def step(x, carry):
+        edges = [], []
+        for k in range(5):
+            group, lane = divmod(k * 32, 128)
+            edge = pltpu.roll(received[group], (127 * (1 - core) - lane - x) & 127, 1)
+            edges[0].append(jnp.where(core == 0, edge, 0.0))
+            edges[1].append(jnp.where(core == 1, edge, 0.0))
         for q in range(19):
-            tile = pulled_z(q, adjoint[q, x].astype(f32), x, columns)
+            tile = pulled_z(q, adjoint[q, x].astype(f32), edges)
             pulled[q, rows_of(x, VELOCITY[q][1]), :] = tile
         return carry
 
@@ -357,12 +349,12 @@
         flows[INVERSE, x] = inverse
         return carry
 
-    lax.fori_loop(0, 32, step, 0, unroll=4)
+    lax.fori_loop(0, 32, step, 0, unroll=8)
     for k in range(5):
         pulled[YP[k], rows_at(7), :] = jnp.zeros((32, 128), f32)
         pulled[YM[k], rows_at(0), :] = jnp.zeros((32, 128), f32)
     copy.wait()
-    lax.fori_loop(0, 32, flow, 0, unroll=4)
+    lax.fori_loop(0, 32, flow, 0, unroll=8)
 
 
 def pack_x(directions, unpatched, flows, lines, *refs):
@@ -786,7 +778,6 @@
             shape(kind.shape, jnp.int32),
         ],
         [
-            pltpu.VMEM((2, 2) + tile, f32),
             pltpu.SemaphoreType.DMA((1,)),
         ],
         cost_estimate=pl.CostEstimate(flops=10**10, bytes_accessed=10**7, transcendentals=0),

time: 17.6 us -> 17.5 us (level)
  Pallas kernels: 6.84 us -> 6.51 us
    pallas_call x1, Pallas kernels: 1.54 us -> 1.23 us  [per_device(): kernel_call(functools.partial(pull_zy, count), [shape((19, 272, 128), f32...]
    ppermute x3, waiting for transfers between devices: 0.11 us -> 0.29 us  [per_device(): lax.ppermute(sent, ('gy', 'gz'), route)]
  transfers between devices with their start and end apart: 9 -> 9, of which waited for: 4 -> 5; matrix products, arithmetic and copies ran while one was open for 0% -> 0% of each run, Pallas kernels for 27% -> 25%
where the time goes in v10:
time: 17.5 us; the launch traced here: 17.2 us
  starting transfers between devices  7.89 us (45%)
  Pallas kernels  6.51 us (37%)
  waiting for transfers between devices  2.13 us (12%)
  between operations  0.72 us (4%)
    ppermute x3, starting transfers between devices, per_device(): lax.ppermute(sent, ('gy', 'gz'), route)  4.58 us
    ppermute x3, starting transfers between devices, per_device(): lax.ppermute(sent, ('gx', 'gz'), pairs(count_x, slot))  2.59 us
    pallas_call x1, Pallas kernels, per_device(): kernel_call(functools.partial(collide_inside, directions), [pulled, shape...  1.33 us
    pallas_call x1, Pallas kernels, per_device(): kernel_call(collide_outside, shape(adjoint.shape, bf16), [pltpu.VMEM((19,...  1.27 us
    pallas_call x1, Pallas kernels, per_device(): kernel_call(functools.partial(pack_rows, directions), [shape((LINE_ROWS *...  1.24 us
    pallas_call x1, Pallas kernels, per_device(): kernel_call(functools.partial(pull_zy, count), [shape((19, 272, 128), f32...  1.23 us
    ppermute x1, waiting for transfers between devices, per_device(): taken = lax.ppermute(handed, 'gz', swap)  1.17 us
    pallas_call x1, Pallas kernels, per_device(): kernel_call(finish, shape(coefficients.shape, f32))(folded, taken, *others)  0.76 us
  transfers between devices with their start and end apart: 9, of which 5 were waited for; matrix products, arithmetic and copies ran while one was open for 0% of the time, Pallas kernels for 25%

profile of v10, /device:TPU:0, one launch (start us, length us, event | category | flops | bytes accessed | tf_op | source)
XLA Modules:
  0.0 17.2 jit_solution(7633177054109712128)
XLA Ops:
  0.6 1.2 %shard_map.59 = (bf16[192,128]{1,0:T(8,128)(2,1)S(1)}, f32[16,128]{1,0:T(8,128)S(1)}, f32[2,8,128]{2,1,0:T(8,128)S(1)}) custom-call(bf16[19,32,8,128]{3,2,1,0:T(8,128)(2,1)} %adjoint.5, f32[8,2,32]{2,1,0:T(2,128)} %coefficients.1), custom_call_target="tpu_custom_call" | custom-call | tf_op jit(solution)/shard_map/pallas_call | solution.py:746
  1.9 0.5 %collective-permute-start.1 = (bf16[192,128]{1,0:T(8,128)(2,1)S(1)}, bf16[192,128]{1,0:T(8,128)(2,1)S(1)}, u32[]{:S(2)}, u32[]{:S(2)}) collective-permute-start(bf16[192,128]{1,0:T(8,128)(2,1)S(1)} %get-tuple-element.28.own), channel_id=1, source_target_pairs={{0,1},{1,0},{2,3},{3,2},{4,5},{5,4},{6,7},{7,6},{8,9},{9,8},{10,11... | collective-permute-start | bytes 147464 | tf_op jit(solution)/shard_map/ppermute | solution.py:761
  2.4 0.2 %shard_map.60 = f32[4,8,128]{2,1,0:T(8,128)S(1)} custom-call(bf16[19,32,8,128]{3,2,1,0:T(8,128)(2,1)S(1)} %copy-done, f32[2,8,128]{2,1,0:T(8,128)S(1)} %get-tuple-element.23.coarse), custom_call_target="tpu_custom_call" | custom-call | tf_op jit(solution)/shard_map/pallas_call | solution.py:762
  2.6 0.2 %collective-permute-start = (f32[4,8,128]{2,1,0:T(8,128)S(1)}, f32[4,8,128]{2,1,0:T(8,128)S(1)}, u32[]{:S(2)}, u32[]{:S(2)}) collective-permute-start(f32[4,8,128]{2,1,0:T(8,128)S(1)} %shard_map.60), channel_id=1, source_target_pairs={{0,1},{1,0},{2,3},{3,2},{4,5},{5,4},{6,7},{7,6},{8,9},{9,8},{10,11... | collective-permute-start | bytes 49160 | tf_op jit(solution)/shard_map/ppermute | solution.py:763
  2.8 0.5 %collective-permute-done.1.taken = bf16[192,128]{1,0:T(8,128)(2,1)S(1)} collective-permute-done((bf16[192,128]{1,0:T(8,128)(2,1)S(1)}, bf16[192,128]{1,0:T(8,128)(2,1)S(1)}, u32[]{:S(2)}, u32[]{:S(2)}) %collective-permute-start.1) | collective-permute-done | bytes 49184 | tf_op jit(solution)/shard_map/ppermute | solution.py:761
  3.3 0.1 shard_map.62
  3.4 2.7 %collective-permute-start.2 = (bf16[80,128]{1,0:T(8,128)(2,1)S(1)}, bf16[80,128]{1,0:T(8,128)(2,1)S(1)}, u32[]{:S(2)}, u32[]{:S(2)}) collective-permute-start(bf16[80,128]{1,0:T(8,128)(2,1)S(1)} %get-tuple-element.29), channel_id=1, source_target_pairs={{0,3},{1,2},{2,1},{3,0},{4,7},{5,6},{6,5},{7,4},{8,11},{9,10},{10,... | collective-permute-start | bytes 61448 | tf_op jit(solution)/shard_map/ppermute | solution.py:769
  6.1 0.1 collective-permute-start.3
  6.1 1.2 %shard_map.61 = (f32[19,272,128]{2,1,0:T(8,128)S(1)}, f32[5,32,8,128]{3,2,1,0:T(8,128)S(1)}, f32[16,128]{1,0:T(8,128)S(1)}, s32[32,8,128]{2,1,0:T(8,128)S(1)}) custom-call(bf16[19,32,8,128]{3,2,1,0:T(8,128)(2,1)S(1)} %copy-done, bf16[19,32,8,128]{3,2,1,0:T(8,128)(2,1)S(1)} %copy-done.1, s32[32,8,128]{2,1,0:T(8,128)} %kind_far.1, ...), custom_call_target="tpu_custom_call" | custom-call | flops 10000000000 | bytes 10000000 | tf_op jit(solution)/shard_map/pallas_call | solution.py:772
  7.4 0.2 %collective-permute-done.2.refs_0_ = bf16[80,128]{1,0:T(8,128)(2,1)S(1)} collective-permute-done((bf16[80,128]{1,0:T(8,128)(2,1)S(1)}, bf16[80,128]{1,0:T(8,128)(2,1)S(1)}, u32[]{:S(2)}, u32[]{:S(2)}) %collective-permute-start.2) | collective-permute-done | bytes 20512 | tf_op jit(solution)/shard_map/ppermute | solution.py:769
  7.6 0.1 shard_map.63
  7.7 2.1 %collective-permute-start.4 = (bf16[23,8,128]{2,1,0:T(8,128)(2,1)S(1)}, bf16[23,8,128]{2,1,0:T(8,128)(2,1)S(1)}, u32[]{:S(2)}, u32[]{:S(2)}) collective-permute-start(bf16[23,8,128]{2,1,0:T(8,128)(2,1)S(1)} %get-tuple-element.35), channel_id=1, source_target_pairs={{0,4},{1,5},{4,0},{5,1},{8,9},{9,8},{12,13},{13,12},{2,6},{3,7},{6... | collective-permute-start | bytes 141320 | tf_op jit(solution)/shard_map/ppermute | solution.py:804
  9.8 0.0 collective-permute-start.5
  9.8 0.5 %collective-permute-start.6 = (bf16[23,8,128]{2,1,0:T(8,128)(2,1)S(1)}, bf16[23,8,128]{2,1,0:T(8,128)(2,1)S(1)}, u32[]{:S(2)}, u32[]{:S(2)}) collective-permute-start(bf16[23,8,128]{2,1,0:T(8,128)(2,1)S(1)} %get-tuple-element.37), channel_id=1, source_target_pairs={{0,1},{1,0},{4,5},{5,4},{8,12},{9,13},{12,8},{13,9},{2,3},{3,2},{6... | collective-permute-start | bytes 141320 | tf_op jit(solution)/shard_map/ppermute | solution.py:804
  10.3 0.0 collective-permute-done.3.refs_0_
  10.3 1.3 %shard_map.64 = (f32[19,272,128]{2,1,0:T(8,128)S(1)}, bf16[19,32,8,128]{3,2,1,0:T(8,128)(2,1)}, f32[8,8,128]{2,1,0:T(8,128)S(1)}) custom-call(f32[19,272,128]{2,1,0:T(8,128)S(1)} %get-tuple-element.30.unpatched, f32[5,32,8,128]{3,2,1,0:T(8,128)S(1)} %get-tuple-element.26.flows, ...), custom_call_target="tpu_custom_call", output_to_operand_aliasing={{0}: (0, {})} | custom-call | flops 10000000000 | bytes 1 | tf_op jit(solution)/shard_map/pallas_call | solution.py:807
  11.7 0.2 %collective-permute-done.4.refs_0_ = bf16[23,8,128]{2,1,0:T(8,128)(2,1)S(1)} collective-permute-done((bf16[23,8,128]{2,1,0:T(8,128)(2,1)S(1)}, bf16[23,8,128]{2,1,0:T(8,128)(2,1)S(1)}, u32[]{:S(2)}, u32[]{:S(2)}) %collective-permute-start.4) | collective-permute-done | bytes 47136 | tf_op jit(solution)/shard_map/ppermute | solution.py:804
  11.9 0.2 %shard_map.66 = (f32[16,128]{1,0:T(8,128)S(1)}, f32[3,8,128]{2,1,0:T(8,128)S(1)}, f32[1,8,128]{2,1,0:T(8,128)S(1)}) custom-call(f32[19,272,128]{2,1,0:T(8,128)S(1)} %get-tuple-element.34.pulled, f32[5,32,8,128]{3,2,1,0:T(8,128)S(1)} %get-tuple-element.26.flows, f32[2,8,8,128]{3,2,1,0:T(8,128)S(1)} %get-tuple-element.39.edges, ...), custom_call_target="tpu_custom_call" | custom-call | tf_op jit(solution)/shard_map/pallas_call | solution.py:817
  12.1 0.0 collective-permute-start.7
  12.1 1.2 %collective-permute-done.7.taken.rims = f32[3,8,128]{2,1,0:T(8,128)S(1)} collective-permute-done((f32[3,8,128]{2,1,0:T(8,128)S(1)}, f32[3,8,128]{2,1,0:T(8,128)S(1)}, u32[]{:S(2)}, u32[]{:S(2)}) %collective-permute-start.7) | collective-permute-done | bytes 12320 | tf_op jit(solution)/shard_map/ppermute | solution.py:825
  13.3 1.8 %collective-permute-start.8 = (f32[2,8,128]{2,1,0:T(8,128)S(1)}, f32[2,8,128]{2,1,0:T(8,128)S(1)}, u32[]{:S(2)}, u32[]{:S(2)}) collective-permute-start(f32[2,8,128]{2,1,0:T(8,128)S(1)} %shard_map.67), channel_id=1, source_target_pairs={{0,3},{1,2},{2,1},{3,0},{4,7},{5,6},{6,5},{7,4},{8,11},{9,10},{10,... | collective-permute-start | bytes 24584 | tf_op jit(solution)/shard_map/ppermute | solution.py:827
  15.1 1.3 %shard_map.65 = bf16[19,32,8,128]{3,2,1,0:T(8,128)(2,1)} custom-call(f32[19,272,128]{2,1,0:T(8,128)S(1)} %get-tuple-element.34.pulled, f32[5,32,8,128]{3,2,1,0:T(8,128)S(1)} %get-tuple-element.26.flows, s32[32,8,128]{2,1,0:T(8,128)S(1)} %get-tuple-element.31.kind, f32[8,8,128]{2,1,0:T(8,128)S(1)} %get-tuple-element.32.levels, ...), custom_call_target="tpu_custom_call", output_to_operand_aliasing={{}: (7, {})} | custom-call | tf_op jit(solution)/shard_map/pallas_call | solution.py:829
  16.4 0.1 collective-permute-done.8.refs_0_
  16.5 0.8 %shard_map.68 = f32[8,2,32]{2,1,0:T(2,128)} custom-call(f32[16,128]{1,0:T(8,128)S(1)} %get-tuple-element.41.folded, f32[3,8,128]{2,1,0:T(8,128)S(1)} %collective-permute-done.7.taken.rims, f32[2,8,128]{2,1,0:T(8,128)S(1)} %collective-permute-done.8.refs_0_), custom_call_target="tpu_custom_call" | custom-call | tf_op jit(solution)/shard_map/pallas_call | solution.py:837
  (8 shorter events, 0.0 us)
Async XLA Ops:
  0.6 1.8 %copy-start = (bf16[19,32,8,128]{3,2,1,0:T(8,128)(2,1)S(1)}, bf16[19,32,8,128]{3,2,1,0:T(8,128)(2,1)}, u32[]{:S(2)}) copy-start(bf16[19,32,8,128]{3,2,1,0:T(8,128)(2,1)} %adjoint.5) | copy-start | bytes 3735556
  0.6 5.5 %copy-start.1 = (bf16[19,32,8,128]{3,2,1,0:T(8,128)(2,1)S(1)}, bf16[19,32,8,128]{3,2,1,0:T(8,128)(2,1)}, u32[]{:S(2)}) copy-start(bf16[19,32,8,128]{3,2,1,0:T(8,128)(2,1)} %forward.1) | copy-start | bytes 3735556
  1.9 1.4 %collective-permute-start.1 = (bf16[192,128]{1,0:T(8,128)(2,1)S(1)}, bf16[192,128]{1,0:T(8,128)(2,1)S(1)}, u32[]{:S(2)}, u32[]{:S(2)}) collective-permute-start(bf16[192,128]{1,0:T(8,128)(2,1)S(1)} %get-tuple-element.28.own), channel_id=1, source_target_pairs={{0,1},{1,0},{2,3},{3,2},{4,5},{5,4},{6,7},{7,6},{8,9},{9,8},{10,11... | collective-permute-start | bytes 147464 | tf_op jit(solution)/shard_map/ppermute | solution.py:761
  2.6 3.5 %collective-permute-start = (f32[4,8,128]{2,1,0:T(8,128)S(1)}, f32[4,8,128]{2,1,0:T(8,128)S(1)}, u32[]{:S(2)}, u32[]{:S(2)}) collective-permute-start(f32[4,8,128]{2,1,0:T(8,128)S(1)} %shard_map.60), channel_id=1, source_target_pairs={{0,1},{1,0},{2,3},{3,2},{4,5},{5,4},{6,7},{7,6},{8,9},{9,8},{10,11... | collective-permute-start | bytes 49160 | tf_op jit(solution)/shard_map/ppermute | solution.py:763
  3.4 4.2 %collective-permute-start.2 = (bf16[80,128]{1,0:T(8,128)(2,1)S(1)}, bf16[80,128]{1,0:T(8,128)(2,1)S(1)}, u32[]{:S(2)}, u32[]{:S(2)}) collective-permute-start(bf16[80,128]{1,0:T(8,128)(2,1)S(1)} %get-tuple-element.29), channel_id=1, source_target_pairs={{0,3},{1,2},{2,1},{3,0},{4,7},{5,6},{6,5},{7,4},{8,11},{9,10},{10,... | collective-permute-start | bytes 61448 | tf_op jit(solution)/shard_map/ppermute | solution.py:769
  6.1 4.3 %collective-permute-start.3 = (bf16[112,128]{1,0:T(8,128)(2,1)S(1)}, bf16[112,128]{1,0:T(8,128)(2,1)S(1)}, u32[]{:S(2)}, u32[]{:S(2)}) collective-permute-start(bf16[112,128]{1,0:T(8,128)(2,1)S(1)} %get-tuple-element.33), channel_id=1, source_target_pairs={{0,3},{1,2},{2,1},{3,0},{4,7},{5,6},{6,5},{7,4},{8,11},{9,10},{10,... | collective-permute-start | bytes 86024 | tf_op jit(solution)/shard_map/ppermute | solution.py:769
  7.7 4.1 %collective-permute-start.4 = (bf16[23,8,128]{2,1,0:T(8,128)(2,1)S(1)}, bf16[23,8,128]{2,1,0:T(8,128)(2,1)S(1)}, u32[]{:S(2)}, u32[]{:S(2)}) collective-permute-start(bf16[23,8,128]{2,1,0:T(8,128)(2,1)S(1)} %get-tuple-element.35), channel_id=1, source_target_pairs={{0,4},{1,5},{4,0},{5,1},{8,9},{9,8},{12,13},{13,12},{2,6},{3,7},{6... | collective-permute-start | bytes 141320 | tf_op jit(solution)/shard_map/ppermute | solution.py:804
  9.8 2.1 %collective-permute-start.5 = (bf16[23,8,128]{2,1,0:T(8,128)(2,1)S(1)}, bf16[23,8,128]{2,1,0:T(8,128)(2,1)S(1)}, u32[]{:S(2)}, u32[]{:S(2)}) collective-permute-start(bf16[23,8,128]{2,1,0:T(8,128)(2,1)S(1)} %get-tuple-element.36), channel_id=1, source_target_pairs={{0,1},{1,0},{4,8},{5,9},{8,4},{9,5},{12,13},{13,12},{2,3},{3,2},{6... | collective-permute-start | bytes 141320 | tf_op jit(solution)/shard_map/ppermute | solution.py:804
  9.8 2.1 %collective-permute-start.6 = (bf16[23,8,128]{2,1,0:T(8,128)(2,1)S(1)}, bf16[23,8,128]{2,1,0:T(8,128)(2,1)S(1)}, u32[]{:S(2)}, u32[]{:S(2)}) collective-permute-start(bf16[23,8,128]{2,1,0:T(8,128)(2,1)S(1)} %get-tuple-element.37), channel_id=1, source_target_pairs={{0,1},{1,0},{4,5},{5,4},{8,12},{9,13},{12,8},{13,9},{2,3},{3,2},{6... | collective-permute-start | bytes 141320 | tf_op jit(solution)/shard_map/ppermute | solution.py:804
  12.1 1.2 %collective-permute-start.7 = (f32[3,8,128]{2,1,0:T(8,128)S(1)}, f32[3,8,128]{2,1,0:T(8,128)S(1)}, u32[]{:S(2)}, u32[]{:S(2)}) collective-permute-start(f32[3,8,128]{2,1,0:T(8,128)S(1)} %get-tuple-element.42), channel_id=1, source_target_pairs={{0,1},{1,0},{2,3},{3,2},{4,5},{5,4},{6,7},{7,6},{8,9},{9,8},{10,11... | collective-permute-start | bytes 36872 | tf_op jit(solution)/shard_map/ppermute | solution.py:825
  13.3 3.2 %collective-permute-start.8 = (f32[2,8,128]{2,1,0:T(8,128)S(1)}, f32[2,8,128]{2,1,0:T(8,128)S(1)}, u32[]{:S(2)}, u32[]{:S(2)}) collective-permute-start(f32[2,8,128]{2,1,0:T(8,128)S(1)} %shard_map.67), channel_id=1, source_target_pairs={{0,3},{1,2},{2,1},{3,0},{4,7},{5,6},{6,5},{7,4},{8,11},{9,10},{10,... | collective-permute-start | bytes 24584 | tf_op jit(solution)/shard_map/ppermute | solution.py:827
